TPU v7x, 32 devices: a whole 2x2x4 slice. The times are simulated.
32 devices in a mesh: frame: 8 (over y, x, core), tile: 4 (over z).
Axes of the slice: x: 2, y: 2, z: 4, core: 2. Of those that a mesh axis runs over, the one named last changes fastest.
Arguments:
- grid: bfloat16 [64, 16, 32, 1024], P(None, 'frame', None, 'tile'), may hold values from -6 to 6
- conv_weight: bfloat16 [9, 64, 8], replicated, may hold values from -0.75 to 0.75
- conv_bias: float32 [64], replicated, may hold values from -3 to 3
- depth_kernel: float32 [4, 3, 64], replicated, may hold values from -3 to 3
- point_weight: bfloat16 [4, 64, 64], replicated, may hold values from -0.75 to 0.75
- occupied: int32 [4, 32], P('tile'), may hold values from 0 to 63, as said below
- counts: int32 [4], P('tile'), may hold values from 10 to 32, as said below
Outputs:
- features: bfloat16 [64, 16, 32, 1024], P(None, 'frame', None, 'tile')
Inputs may be any that keep to these rules, and one draw needn't show every extreme that they name: Each row holds 32 distinct block numbers of its tile; its first counts[t] entries are the occupied blocks, the rest are unoccupied blocks used as padding. `counts`: some tile's list is fully occupied, and some tile has exactly the fewest occupied entries.
All inputs are finite; a program needn't handle non-finite values.
Results may differ from a plain program's by a relative error of at most 0.0051.
Values may be sent and summed in bfloat16 or wider, within the bound.
No kernel may reach another device: no remote copies, remote signals or barrier semaphores. Data moves between devices by JAX's collectives and lax.ppermute only.
A program may use at most 128 MiB of HBM per device.

v0:
```python
import jax
import jax.numpy as jnp
from jax import lax
from jax.sharding import PartitionSpec as P

GROUP = 8


def with_halo(cells, sides, width):
    for axis, dim in sides:
        count = lax.axis_size(axis)
        ends = count - 1
        head = lax.slice_in_dim(cells, 0, width, axis=dim)
        tail = lax.slice_in_dim(cells, cells.shape[dim] - width, cells.shape[dim], axis=dim)
        cells = jnp.concatenate(
            [
                lax.ppermute(tail, axis, [(i, (i + 1) % count) for i in range(ends)]),
                cells,
                lax.ppermute(head, axis, [((i + 1) % count, i) for i in range(ends)]),
            ],
            axis=dim,
        )
    return cells


def shifted(series, amount):
    if amount == 0:
        return series
    frames = series.shape[1]
    if amount >= frames:
        return jnp.zeros_like(series)
    leading = jnp.zeros_like(series[:, :amount])
    return jnp.concatenate([leading, series[:, : frames - amount]], axis=1)


def temporal(blocks, depth_kernel, point_weight):
    current = blocks.astype(jnp.float32)
    for layer_idx in range(depth_kernel.shape[0]):
        spacing = 2**layer_idx
        blended = jnp.zeros_like(current)
        for offset in range(depth_kernel.shape[1]):
            blended = blended + depth_kernel[layer_idx, offset][:, None, None, None] * shifted(
                current, offset * spacing
            )
        squashed = jax.nn.silu(blended).astype(jnp.bfloat16)
        current = current + jnp.einsum(
            "oc,cfsn->ofsn", point_weight[layer_idx], squashed, preferred_element_type=jnp.float32
        )
    return current.astype(jnp.bfloat16)


def spatial(padded, center, conv_weight, conv_bias):
    channels, frames, height, columns = center.shape
    group_count = channels // GROUP
    grouped = padded.reshape(group_count, GROUP, frames, height + 2, columns + 2)
    summed = jnp.zeros((group_count, GROUP, frames, height, columns), jnp.float32)
    for tap_row in range(3):
        for tap_col in range(3):
            window = grouped[:, :, :, tap_row : tap_row + height, tap_col : tap_col + columns]
            kernel = conv_weight[tap_row * 3 + tap_col].reshape(group_count, GROUP, GROUP)
            summed = summed + jnp.einsum(
                "goi,gifrw->gofrw", kernel, window, preferred_element_type=jnp.float32
            )
    activation = summed.reshape(channels, frames, height, columns) + conv_bias[:, None, None, None]
    return (center.astype(jnp.float32) + jax.nn.silu(activation)).astype(jnp.bfloat16)


def on_device(grid, conv_weight, conv_bias, depth_kernel, point_weight, occupied, counts):
    widened = with_halo(grid, (("tile", 3),), 1)
    padded = jnp.pad(widened, ((0, 0), (0, 0), (1, 1), (0, 0)))
    hidden = spatial(padded, grid, conv_weight, conv_bias)
    channels, frames, height, columns = grid.shape
    blocks = hidden.reshape(channels, frames, height * (columns // 128), 128)
    block_ids = occupied[0]
    slot_count = block_ids.shape[0]
    live_slots = jnp.arange(slot_count, dtype=jnp.int32) < counts[0]
    picked = jnp.take(blocks, block_ids, axis=2)
    updated = lax.all_to_all(
        temporal(
            lax.all_to_all(picked, "frame", split_axis=2, concat_axis=1, tiled=True),
            depth_kernel,
            point_weight,
        ),
        "frame",
        split_axis=1,
        concat_axis=2,
        tiled=True,
    )
    chosen = jnp.where(live_slots[None, None, :, None], updated, picked)
    blocks = blocks.at[:, :, block_ids].set(chosen)
    return blocks.reshape(channels, frames, height, columns)


def solution(mesh):
    placed = (P(None, "frame", None, "tile"), P(), P(), P(), P(), P("tile", None), P("tile"))
    return jax.shard_map(
        on_device,
        mesh=mesh,
        in_specs=placed,
        out_specs=P(None, "frame", None, "tile"),
        check_vma=False,
    )
```

profile of v0, /device:TPU:0, one launch (start us, length us, event | category | flops | bytes accessed | tf_op | source)
XLA Modules:
  0.0 142.0 jit_solution(2651350653088067173)
XLA Ops:
  0.0 3.0 %fusion.64 = (bf16[64,2,32,1]{3,2,1,0:T(8,128)(2,1)}, bf16[64,2,32,1]{3,2,1,0:T(8,128)(2,1)S(1)}) fusion(bf16[64,2,32,256]{3,2,1,0:T(8,128)(2,1)} %param.7), kind=kLoop, calls=%fused_computation.98 | loop fusion | bytes 32768 | tf_op jit(solution)/shard_map/slice | solution.py:14
  3.0 2.5 %copy.115 = bf16[64,2,32,1]{0,2,3,1:T(8,128)(2,1)S(1)} copy(bf16[64,2,32,1]{3,2,1,0:T(8,128)(2,1)} %get-tuple-element.14) | data formatting | bytes 16384
  5.6 4.9 %collective-permute-start = (bf16[64,2,32,1]{0,2,3,1:T(8,128)(2,1)S(1)}, bf16[64,2,32,1]{0,2,3,1:T(8,128)(2,1)S(1)}, u32[]{:S(2)}, u32[]{:S(2)}) collective-permute-start(bf16[64,2,32,1]{0,2,3,1:T(8,128)(2,1)S(1)} %copy.115), channel_id=1, source_target_pairs={{0,1},{1,2},{2,3},{4,5},{5,6},{6,7},{8,9},{9,10},{10,11},{12,13},{... | collective-permute-start | bytes 24584 | tf_op jit(solution)/shard_map/ppermute | solution.py:17
  18.8 3.6 %fusion.6 = bf16[8,8,2,34,258]{4,1,0,3,2:T(8,128)(2,1)S(1)} fusion(bf16[64,2,32,1]{3,0,2,1:T(8,128)(2,1)} %copy.77, bf16[64,2,32,256]{3,0,2,1:T(8,128)(2,1)} %copy.76, bf16[64,2,32,1]{3,0,2,1:T(8,128)(2,1)S(1)} %copy.75), kind=kLoop, calls=%fused_computation.13 | loop fusion | flops 13473792 | bytes 4359168 | tf_op jit(solution)/shard_map/reshape | solution.py:55
  22.5 7.9 %fusion.63 = (bf16[8,8,2,32,256]{4,1,0,3,2:T(8,128)(2,1)S(1)}, bf16[8,8,2,32,256]{4,1,0,3,2:T(8,128)(2,1)}, bf16[8,8,2,32,256]{4,1,0,3,2:T(8,128)(2,1)}, bf16[8,...) fusion(bf16[8,8,2,34,258]{4,1,0,3,2:T(8,128)(2,1)S(1)} %fusion.6), kind=kLoop, calls=%fused_computation.97 | loop fusion | bytes 37748736 | tf_op jit(solution)/shard_map/slice | solution.py:59
  32.8 2.6 %fusion.12 = f32[8,2,32,256,8]{3,4,2,1,0:T(8,128)} fusion(bf16[8,8,2,32,256]{4,1,0,3,2:T(8,128)(2,1)S(1)} %copy-done.7, bf16[1,64,8]{2,1,0:T(8,128)(2,1)S(1)} %copy.89), kind=kOutput, calls=%fused_computation.19 | convolution fusion | flops 16777216 | bytes 6292480 | tf_op jit(solution)/shard_map/goi,gifrw->gofrw/dot_general | solution.py:61
  35.5 2.7 %fusion.14 = f32[8,2,32,256,8]{3,4,2,1,0:T(8,128)} fusion(bf16[8,8,2,32,256]{4,1,0,3,2:T(8,128)(2,1)S(1)} %copy-done.6, bf16[1,64,8]{2,1,0:T(8,128)(2,1)S(1)} %copy.87), kind=kOutput, calls=%fused_computation.21 | convolution fusion | flops 16777216 | bytes 6292480 | tf_op jit(solution)/shard_map/goi,gifrw->gofrw/dot_general | solution.py:61
  38.2 2.7 %fusion.16 = f32[8,2,32,256,8]{3,4,2,1,0:T(8,128)} fusion(bf16[8,8,2,32,256]{4,1,0,3,2:T(8,128)(2,1)S(1)} %copy-done.5, bf16[1,64,8]{2,1,0:T(8,128)(2,1)S(1)} %copy.85), kind=kOutput, calls=%fused_computation.23 | convolution fusion | flops 16777216 | bytes 6292480 | tf_op jit(solution)/shard_map/goi,gifrw->gofrw/dot_general | solution.py:61
  40.8 2.6 %fusion.18 = f32[8,2,32,256,8]{3,4,2,1,0:T(8,128)} fusion(bf16[8,8,2,32,256]{4,1,0,3,2:T(8,128)(2,1)S(1)} %copy-done.4, bf16[1,64,8]{2,1,0:T(8,128)(2,1)S(1)} %copy.83), kind=kOutput, calls=%fused_computation.25 | convolution fusion | flops 16777216 | bytes 6292480 | tf_op jit(solution)/shard_map/goi,gifrw->gofrw/dot_general | solution.py:61
  43.5 2.6 %fusion.20 = f32[8,2,32,256,8]{3,4,2,1,0:T(8,128)} fusion(bf16[8,8,2,32,256]{4,1,0,3,2:T(8,128)(2,1)S(1)} %copy-done.3, bf16[1,64,8]{2,1,0:T(8,128)(2,1)S(1)} %copy.81), kind=kOutput, calls=%fused_computation.27 | convolution fusion | flops 16777216 | bytes 6292480 | tf_op jit(solution)/shard_map/goi,gifrw->gofrw/dot_general | solution.py:61
  46.1 2.7 %fusion.22 = f32[8,2,32,256,8]{3,4,2,1,0:T(8,128)} fusion(bf16[8,8,2,32,256]{4,1,0,3,2:T(8,128)(2,1)S(1)} %copy-done.2, bf16[1,64,8]{2,1,0:T(8,128)(2,1)S(1)} %copy.79), kind=kOutput, calls=%fused_computation.29 | convolution fusion | flops 16777216 | bytes 6292480 | tf_op jit(solution)/shard_map/goi,gifrw->gofrw/dot_general | solution.py:61
  48.8 2.7 %fusion.8 = f32[8,2,32,256,8]{3,4,2,1,0:T(8,128)} fusion(bf16[8,8,2,32,256]{4,1,0,3,2:T(8,128)(2,1)S(1)} %copy-done.1, bf16[1,64,8]{2,1,0:T(8,128)(2,1)S(1)} %copy.93), kind=kOutput, calls=%fused_computation.15 | convolution fusion | flops 16777216 | bytes 6292480 | tf_op jit(solution)/shard_map/goi,gifrw->gofrw/dot_general | solution.py:61
  51.5 12.9 %add_bitcast_fusion = f32[8,8,2,32,256]{4,1,3,2,0:T(8,128)} fusion(f32[8,2,32,256,8]{3,4,2,1,0:T(8,128)} %fusion.8, f32[8,2,32,256,8]{3,4,2,1,0:T(8,128)S(1)} %fusion.10, f32[8,2,32,256,8]{3,4,2,1,0:T(8,128)} %fusion.12, f32[8,2,32,256,8]{3,4,2,1,0:T(8,128)} %fusion.14, f32[8,2,32,256,8]{3,4,2,1,0:T(8,128)} %fusion.16, f32[8,2,32,256,8]{3,4,2,1,0:T(8,128)} %fusion.18, ...), kind=kOutput, calls=%fused_computation.6 | convolution fusion | flops 25165824 | bytes 39846912 | tf_op jit(solution)/shard_map/goi,gifrw->gofrw/dot_general | solution.py:61
  64.3 3.5 %copy.96 = f32[8,8,2,32,256]{4,3,2,1,0:T(8,128)S(1)} copy(f32[8,8,2,32,256]{4,1,3,2,0:T(8,128)} %add_bitcast_fusion) | data formatting | bytes 8388608 | tf_op jit(solution)/shard_map/add | solution.py:61
  67.8 3.3 %add_convert_fusion = bf16[64,2,32,256]{3,2,1,0:T(8,128)(2,1)} fusion(f32[8,8,2,32,256]{4,3,2,1,0:T(8,128)S(1)} %copy.96, bf16[64,2,32,256]{3,2,1,0:T(8,128)(2,1)S(1)} %copy-done, f32[64]{0:T(128)S(1)} %copy-done.10), kind=kLoop, calls=%fused_computation.7 | loop fusion | flops 8388608 | bytes 8388864 | tf_op jit(solution)/shard_map/convert_element_type | solution.py:65
  71.1 4.1 %reshape.71 = bf16[64,2,64,128]{3,2,1,0:T(8,128)(2,1)} reshape(bf16[64,2,32,256]{3,2,1,0:T(8,128)(2,1)} %add_convert_fusion) | data formatting | bytes 4194304 | tf_op jit(solution)/shard_map/reshape | solution.py:73
  75.2 2.9 %copy.100 = bf16[64,2,64,128]{3,0,2,1:T(8,128)(2,1)S(1)} copy(bf16[64,2,64,128]{3,2,1,0:T(8,128)(2,1)} %reshape.71) | data formatting | bytes 4194304 | tf_op jit(solution)/shard_map/reshape | solution.py:73
  80.1 4.2 %all-to-all-start = ((bf16[64,2,32,128]{3,0,1,2:T(8,128)(2,1)}), bf16[64,2,32,128]{3,0,1,2:T(8,128)(2,1)}, u32[]{:S(2)}, u32[]{:S(2)}) async-start(bf16[64,2,32,128]{3,0,1,2:T(8,128)(2,1)} %select_bitcast_fusion), calls=%async_computation | async-start | bytes 2097152 | tf_op jit(solution)/shard_map/all_to_all | solution.py:80
  84.4 15.4 %all-to-all-done = bf16[64,2,32,128]{3,0,1,2:T(8,128)(2,1)} async-done(((bf16[64,2,32,128]{3,0,1,2:T(8,128)(2,1)}), bf16[64,2,32,128]{3,0,1,2:T(8,128)(2,1)}, u32[]{:S(2)}, u32[]{:S(2)}) %all-to-all-start) | async-done | bytes 1048608 | tf_op jit(solution)/shard_map/all_to_all | solution.py:80
  109.0 4.2 %all-to-all-start.1 = ((bf16[64,16,4,128]{3,0,2,1:T(8,128)(2,1)}), bf16[64,16,4,128]{3,0,2,1:T(8,128)(2,1)}, u32[]{:S(2)}, u32[]{:S(2)}) async-start(bf16[64,16,4,128]{3,0,2,1:T(8,128)(2,1)} %fusion.24), calls=%async_computation.1 | async-start | bytes 2097152 | tf_op jit(solution)/shard_map/all_to_all | solution.py:78
  113.9 14.8 %all-to-all-done.1 = bf16[64,16,4,128]{3,0,2,1:T(8,128)(2,1)} async-done(((bf16[64,16,4,128]{3,0,2,1:T(8,128)(2,1)}), bf16[64,16,4,128]{3,0,2,1:T(8,128)(2,1)}, u32[]{:S(2)}, u32[]{:S(2)}) %all-to-all-start.1) | async-done | bytes 1048608 | tf_op jit(solution)/shard_map/all_to_all | solution.py:78
  131.2 4.0 %scatter_fusion = bf16[64,2,64,128]{3,0,2,1:T(8,128)(2,1)S(1)} fusion(bf16[64,2,64,128]{3,0,2,1:T(8,128)(2,1)S(1)} %copy.100, s32[32]{0:T(128)S(1)} %fusion.54, bf16[32,64,2,128]{3,1,2,0:T(8,128)(2,1)} %bitcast.163), kind=kCustom, calls=%fused_computation.1 | custom fusion | bytes 3145856 | tf_op jit(solution)/shard_map/scatter | solution.py:90
  135.2 2.7 %copy.101 = bf16[64,2,64,128]{3,2,1,0:T(8,128)(2,1)} copy(bf16[64,2,64,128]{3,0,2,1:T(8,128)(2,1)S(1)} %scatter_fusion) | data formatting | bytes 4194304 | tf_op jit(solution)/shard_map/scatter | solution.py:90
  137.9 4.1 %reshape.72 = bf16[64,2,32,256]{3,2,1,0:T(8,128)(2,1)} reshape(bf16[64,2,64,128]{3,2,1,0:T(8,128)(2,1)} %copy.101) | data formatting | bytes 4194304 | tf_op jit(solution)/shard_map/reshape | solution.py:91
  (65 shorter events, 24.3 us)
Async XLA Ops:
  3.0 10.0 %copy-start.12 = (s32[1,32]{1,0:T(1,128)S(1)}, s32[1,32]{1,0:T(1,128)}, u32[]{:S(2)}) copy-start(s32[1,32]{1,0:T(1,128)} %param.12) | copy-start | bytes 388
  3.0 10.0 %copy-start.8 = (bf16[9,64,8]{1,2,0:T(8,128)(2,1)S(1)}, bf16[9,64,8]{1,2,0:T(8,128)(2,1)}, u32[]{:S(2)}) copy-start(bf16[9,64,8]{1,2,0:T(8,128)(2,1)} %param.8) | copy-start | bytes 27652
  3.0 10.1 %copy-start = (bf16[64,2,32,256]{3,2,1,0:T(8,128)(2,1)S(1)}, bf16[64,2,32,256]{3,2,1,0:T(8,128)(2,1)}, u32[]{:S(2)}) copy-start(bf16[64,2,32,256]{3,2,1,0:T(8,128)(2,1)} %param.7) | copy-start | bytes 6291460
  5.6 11.0 %collective-permute-start = (bf16[64,2,32,1]{0,2,3,1:T(8,128)(2,1)S(1)}, bf16[64,2,32,1]{0,2,3,1:T(8,128)(2,1)S(1)}, u32[]{:S(2)}, u32[]{:S(2)}) collective-permute-start(bf16[64,2,32,1]{0,2,3,1:T(8,128)(2,1)S(1)} %copy.115), channel_id=1, source_target_pairs={{0,1},{1,2},{2,3},{4,5},{5,6},{6,7},{8,9},{9,10},{10,11},{12,13},{... | collective-permute-start | bytes 24584 | tf_op jit(solution)/shard_map/ppermute | solution.py:17
  11.7 5.6 %collective-permute-start.1 = (bf16[64,2,32,1]{0,2,3,1:T(8,128)(2,1)S(1)}, bf16[64,2,32,1]{0,2,3,1:T(8,128)(2,1)S(1)}, u32[]{:S(2)}, u32[]{:S(2)}) collective-permute-start(bf16[64,2,32,1]{0,2,3,1:T(8,128)(2,1)S(1)} %copy.116), channel_id=1, source_target_pairs={{1,0},{2,1},{3,2},{5,4},{6,5},{7,6},{9,8},{10,9},{11,10},{13,12},{... | collective-permute-start | bytes 24584 | tf_op jit(solution)/shard_map/ppermute | solution.py:19
  30.4 2.4 %copy-start.7 = (bf16[8,8,2,32,256]{4,1,0,3,2:T(8,128)(2,1)S(1)}, bf16[8,8,2,32,256]{4,1,0,3,2:T(8,128)(2,1)}, u32[]{:S(2)}) copy-start(bf16[8,8,2,32,256]{4,1,0,3,2:T(8,128)(2,1)} %get-tuple-element.8) | copy-start | bytes 6291460
  32.8 2.7 %copy-start.6 = (bf16[8,8,2,32,256]{4,1,0,3,2:T(8,128)(2,1)S(1)}, bf16[8,8,2,32,256]{4,1,0,3,2:T(8,128)(2,1)}, u32[]{:S(2)}) copy-start(bf16[8,8,2,32,256]{4,1,0,3,2:T(8,128)(2,1)} %get-tuple-element.9) | copy-start | bytes 6291460
  35.5 2.7 %copy-start.5 = (bf16[8,8,2,32,256]{4,1,0,3,2:T(8,128)(2,1)S(1)}, bf16[8,8,2,32,256]{4,1,0,3,2:T(8,128)(2,1)}, u32[]{:S(2)}) copy-start(bf16[8,8,2,32,256]{4,1,0,3,2:T(8,128)(2,1)} %get-tuple-element.10) | copy-start | bytes 6291460
  38.2 2.7 %copy-start.4 = (bf16[8,8,2,32,256]{4,1,0,3,2:T(8,128)(2,1)S(1)}, bf16[8,8,2,32,256]{4,1,0,3,2:T(8,128)(2,1)}, u32[]{:S(2)}) copy-start(bf16[8,8,2,32,256]{4,1,0,3,2:T(8,128)(2,1)} %get-tuple-element.11) | copy-start | bytes 6291460
  40.8 2.6 %copy-start.3 = (bf16[8,8,2,32,256]{4,1,0,3,2:T(8,128)(2,1)S(1)}, bf16[8,8,2,32,256]{4,1,0,3,2:T(8,128)(2,1)}, u32[]{:S(2)}) copy-start(bf16[8,8,2,32,256]{4,1,0,3,2:T(8,128)(2,1)} %get-tuple-element.12) | copy-start | bytes 6291460
  43.5 2.6 %copy-start.2 = (bf16[8,8,2,32,256]{4,1,0,3,2:T(8,128)(2,1)S(1)}, bf16[8,8,2,32,256]{4,1,0,3,2:T(8,128)(2,1)}, u32[]{:S(2)}) copy-start(bf16[8,8,2,32,256]{4,1,0,3,2:T(8,128)(2,1)} %get-tuple-element.13) | copy-start | bytes 6291460
  46.1 2.7 %copy-start.1 = (bf16[8,8,2,32,256]{4,1,0,3,2:T(8,128)(2,1)S(1)}, bf16[8,8,2,32,256]{4,1,0,3,2:T(8,128)(2,1)}, u32[]{:S(2)}) copy-start(bf16[8,8,2,32,256]{4,1,0,3,2:T(8,128)(2,1)} %get-tuple-element.6) | copy-start | bytes 6291460
  64.3 3.5 %copy-start.10 = (f32[64]{0:T(128)S(1)}, f32[64]{0:T(128)}, u32[]{:S(2)}) copy-start(f32[64]{0:T(128)} %param.9) | copy-start | bytes 772
  78.9 5.4 %copy-start.9 = (f32[4,3,64]{2,0,1:T(4,128)S(1)}, f32[4,3,64]{2,0,1:T(4,128)}, u32[]{:S(2)}) copy-start(f32[4,3,64]{2,0,1:T(4,128)} %param.10) | copy-start | bytes 9220
  80.1 19.7 %all-to-all-start = ((bf16[64,2,32,128]{3,0,1,2:T(8,128)(2,1)}), bf16[64,2,32,128]{3,0,1,2:T(8,128)(2,1)}, u32[]{:S(2)}, u32[]{:S(2)}) async-start(bf16[64,2,32,128]{3,0,1,2:T(8,128)(2,1)} %select_bitcast_fusion), calls=%async_computation | async-start | bytes 2097152 | tf_op jit(solution)/shard_map/all_to_all | solution.py:80
  101.4 0.8 copy-start.11
  109.0 19.7 %all-to-all-start.1 = ((bf16[64,16,4,128]{3,0,2,1:T(8,128)(2,1)}), bf16[64,16,4,128]{3,0,2,1:T(8,128)(2,1)}, u32[]{:S(2)}, u32[]{:S(2)}) async-start(bf16[64,16,4,128]{3,0,2,1:T(8,128)(2,1)} %fusion.24), calls=%async_computation.1 | async-start | bytes 2097152 | tf_op jit(solution)/shard_map/all_to_all | solution.py:78
where the time goes:
time: 143 us; the launch traced here: 142 us
  local copies, waits for them, and re-layouts  46.7 us (33%)
  matrix products  39.8 us (28%)
  waiting for transfers between devices  30.4 us (21%)
  starting transfers between devices  14.7 us (10%)
  other arithmetic  9.4 us (7%)
    dot_general x9, matrix products, spatial(): jnp.einsum('goi,gifrw->gofrw', kernel, window, preferred_element_type=jnp...  33.9 us
    all_to_all x1, waiting for transfers between devices, on_device(): lax.all_to_all(picked, 'frame', split_axis=2, concat_axis=1, tiled=True)  15.4 us
    all_to_all x1, waiting for transfers between devices, on_device(): lax.all_to_all(temporal(lax.all_to_all(picked, 'frame', split_axis=2, con...  14.8 us
    slice x1, local copies, waits for them, and re-layouts, spatial(): grouped[:, :, :, tap_row:tap_row + height, tap_col:tap_col + columns]  7.92 us
    reshape x2, local copies, waits for them, and re-layouts, on_device(): blocks = hidden.reshape(channels, frames, height * (columns // 128), 128)  7.03 us
    unnamed x29, local copies, waits for them, and re-layouts  6.95 us
    scatter x2, local copies, waits for them, and re-layouts, on_device(): blocks = blocks.at[:, :, block_ids].set(chosen)  6.73 us
    dot_general x4, matrix products, temporal(): jnp.einsum('oc,cfsn->ofsn', point_weight[layer_idx], squashed, preferred_...  5.91 us
  transfers between devices with their start and end apart: 4, of which 3 were waited for; matrix products, arithmetic and copies ran while one was open for 4% of the time, Pallas kernels for 0%

commit v1 on v0

v1 whole, which is shorter than its diff:
```python
import functools

import jax
import jax.numpy as jnp
from jax import lax
from jax.experimental import pallas as pl
from jax.experimental.pallas import tpu as pltpu
from jax.sharding import PartitionSpec as P

GROUP = 8
LANES = 128
MIB = 2**20


def params(mib):
    return pltpu.CompilerParams(vmem_limit_bytes=mib * MIB)


def whole(shape):
    return pl.BlockSpec(shape, lambda *_: (0,) * len(shape))


def dot(a, b, dims=((1,), (0,))):
    return lax.dot_general(a, b, (dims, ((), ())), preferred_element_type=jnp.float32)


def iota(shape, dim):
    return lax.broadcasted_iota(jnp.int32, shape, dim)


def edges_kernel(grid_ref, _, second_ref, first_ref):
    channels, frames, height, columns = grid_ref.shape
    groups, wide = channels // GROUP, GROUP * height
    count = groups * frames
    rows = iota((2 * count, columns), 0)
    lanes = iota((2 * count, columns), 1)
    even = lax.axis_index("tile") % 2 == 0
    ahead, behind = jnp.where(even, columns - 1, 0), jnp.where(even, 0, columns - 1)
    total = jnp.zeros((2 * count, wide), jnp.float32)
    for g in range(groups):
        for f in range(frames):
            at = g * frames + f
            pick = ((rows == at) & (lanes == ahead)) | ((rows == count + at) & (lanes == behind))
            cells = grid_ref[g * GROUP : (g + 1) * GROUP, f].reshape(wide, columns)
            total += dot(pick.astype(jnp.bfloat16), cells, ((1,), (1,)))
    first_ref[...] = total[:count].astype(jnp.bfloat16)
    second_ref[...] = total[count:].astype(jnp.bfloat16)


def swaps(count, start):
    partner = {i: i for i in range(count)}
    for i in range(start, count - 1, 2):
        partner[i], partner[i + 1] = i + 1, i
    return sorted(partner.items())


def edge_columns(grid, after):
    channels, frames, height, _ = grid.shape
    shape = jax.ShapeDtypeStruct((channels // GROUP * frames, GROUP * height), jnp.bfloat16)
    return pl.pallas_call(
        edges_kernel,
        in_specs=[pl.BlockSpec(memory_space=pltpu.VMEM), pl.BlockSpec(memory_space=pl.ANY)],
        out_shape=(shape, shape),
        compiler_params=params(8),
        cost_estimate=pl.CostEstimate(flops=2**28, bytes_accessed=2**21, transcendentals=0),
        name="edge_columns",
    )(grid, after)


def bands_kernel(height, taps_ref, band_ref, spread):
    _, inner, channels = taps_ref.shape
    groups, wide = channels // GROUP, GROUP * height
    repeat = (iota((inner, wide), 0) == iota((inner, wide), 1) // height).astype(jnp.bfloat16)
    offset = iota((height, wide), 1) % height - iota((height, wide), 0)
    masks = [offset == row - 1 for row in range(3)]
    for tap in range(9):
        half = (taps_ref[tap].astype(jnp.float32) * 0.5).astype(jnp.bfloat16)
        spread[tap] = dot(half, repeat, ((0,), (0,)))

    def band(g, carry):
        for col in range(3):
            rows = [spread[3 * row + col, pl.ds(pl.multiple_of(g * GROUP, GROUP), GROUP), :] for row in range(3)]
            for out in range(GROUP):
                value = jnp.zeros((height, wide), jnp.float32)
                for row in range(3):
                    value = jnp.where(masks[row], rows[row][out : out + 1], value)
                band_ref[g, out * height : (out + 1) * height, col * wide : (col + 1) * wide] = value.astype(
                    jnp.bfloat16
                )
        return carry

    lax.fori_loop(0, groups, band, 0, unroll=True)


def bands(conv_weight, height):
    taps = jnp.transpose(conv_weight, (0, 2, 1))
    channels = taps.shape[2]
    groups, wide = channels // GROUP, GROUP * height
    return pl.pallas_call(
        functools.partial(bands_kernel, height),
        out_shape=jax.ShapeDtypeStruct((groups, wide, 3 * wide), jnp.bfloat16),
        scratch_shapes=[pltpu.VMEM((9, channels, wide), jnp.float32)],
        compiler_params=params(8),
        cost_estimate=pl.CostEstimate(flops=2**28, bytes_accessed=2**23, transcendentals=0),
        name="bands",
    )(taps)


def inner_kernel(grid_ref, band_ref, summed_ref):
    channels, frames, height, columns = grid_ref.shape
    wide = GROUP * height
    lanes = iota((wide, columns), 1)

    def convolve(g, carry):
        base = pl.multiple_of(g * GROUP, GROUP)
        for f in range(frames):
            cells = grid_ref[pl.ds(base, GROUP), f].reshape(wide, columns)
            full = cells.astype(jnp.float32)
            before = jnp.where(lanes == 0, 0.0, pltpu.roll(full, 1, 1)).astype(jnp.bfloat16)
            after = jnp.where(lanes == columns - 1, 0.0, pltpu.roll(full, columns - 1, 1)).astype(jnp.bfloat16)
            summed_ref[g, f] = dot(band_ref[g], jnp.concatenate([before, cells, after], axis=0))
        return carry

    lax.fori_loop(0, channels // GROUP, convolve, 0, unroll=True)


def inner(grid, band):
    channels, frames, height, columns = grid.shape
    return pl.pallas_call(
        inner_kernel,
        out_shape=jax.ShapeDtypeStruct((channels // GROUP, frames, GROUP * height, columns), jnp.float32),
        compiler_params=params(8),
        cost_estimate=pl.CostEstimate(flops=2**31, bytes_accessed=2**23, transcendentals=0),
        name="inner",
    )(grid, band)


def steps_of(count, core_first=False):
    mixed = [(4, 2), (2, 4), (5, 3), (3, 5)] if count >= 8 else []
    seen = {0, 1} | {a for a, _ in mixed}
    across = mixed + [(d, d) for d in range(count) if d not in seen]
    return [(0, 0), (1, 1)] + across if core_first else [(0, 0)] + across + [(1, 1)]


def sent_to(me, step):
    return me ^ jnp.where(me % 2 == 0, step[0], step[1])


def got_from(me, step):
    return sent_to(me, step) if step[0] % 2 == 0 else sent_to(me, step[::-1])


def finish_kernel(occupied_ref, bias_ref, grid_ref, band_ref, summed_ref, second_ref, first_ref, hidden_ref, *rest):
    message_refs, (pick_ref, side_ref) = rest[:-2], rest[-2:]
    me = lax.axis_index("frame")
    channels, frames, height, columns = grid_ref.shape
    halves = columns // LANES
    wide = GROUP * height
    slots = occupied_ref.shape[1] // len(message_refs)
    part = GROUP * slots
    rows, lanes = iota((part, wide), 0), iota((part, wide), 1)
    at_slot, at_side = rows % slots, iota((part, LANES), 0) % slots
    same_channel, at_row = lanes // height == rows // slots, lanes % height
    for d, step in enumerate(steps_of(len(message_refs))):
        row, side = jnp.zeros((part, wide), jnp.int32), jnp.zeros((part, LANES), jnp.int32)
        for j in range(slots):
            block = occupied_ref[0, sent_to(me, step) * slots + j]
            row = jnp.where(at_slot == j, block // halves, row)
            side = jnp.where(at_side == j, block % halves, side)
        pick_ref[d * part : (d + 1) * part, :] = (same_channel & (at_row == row)).astype(jnp.bfloat16)
        side_ref[d * part : (d + 1) * part, :] = side

    tile, tiles = lax.axis_index("tile"), lax.axis_size("tile")
    even = tile % 2 == 0
    first, second = first_ref[...].astype(jnp.float32), second_ref[...].astype(jnp.float32)
    left = jnp.where(tile > 0, jnp.where(even, second, first), 0.0)
    right = jnp.where(tile < tiles - 1, jnp.where(even, first, second), 0.0)
    rim = 16
    rim_rows = iota((rim, wide), 0)
    blank = jnp.zeros((LANES - rim, wide), jnp.bfloat16)

    def edge_terms(g):
        before, after = [], []
        for f in range(frames):
            at = slice(g * frames + f, g * frames + f + 1)
            before += [jnp.where(rim_rows == 0, left[at], 0.0).astype(jnp.bfloat16), blank]
            after += [blank, jnp.where(rim_rows == rim - 1, right[at], 0.0).astype(jnp.bfloat16)]
        return (
            dot(band_ref[g, :, :wide], jnp.concatenate(before, axis=0), ((1,), (1,))),
            dot(band_ref[g, :, 2 * wide :], jnp.concatenate(after, axis=0), ((1,), (1,))),
        )

    def activate(g):
        at_left, at_right = edge_terms(g)
        for f in range(frames):
            across = slice(f * LANES, (f + 1) * LANES)
            for out in range(GROUP):
                c = g * GROUP + out
                part = slice(out * height, (out + 1) * height)
                half = summed_ref[g, f, part, :] + 0.5 * bias_ref[c]
                tiles = [half[:, side * LANES : (side + 1) * LANES] for side in range(halves)]
                tiles[0] += at_left[part, across]
                tiles[-1] += at_right[part, across]
                half = jnp.concatenate(tiles, axis=1)
                hidden = grid_ref[c, f].astype(jnp.float32) + (half + half * jnp.tanh(half))
                hidden_ref[c, f] = hidden.astype(jnp.bfloat16)

    def pick(g):
        for f in range(frames):
            picked = dot(pick_ref[...], hidden_ref[g * GROUP : (g + 1) * GROUP, f].reshape(wide, columns))
            chosen = picked[:, :LANES]
            for side in range(1, halves):
                chosen = jnp.where(side_ref[...] == side, picked[:, side * LANES : (side + 1) * LANES], chosen)
            chosen = chosen.astype(jnp.bfloat16)
            for d, message_ref in enumerate(message_refs):
                message_ref[f, g * part : (g + 1) * part, :] = chosen[d * part : (d + 1) * part]

    groups = channels // GROUP
    for g in range(groups + 1):
        if g < groups:
            activate(g)
        if g > 0:
            pick(g - 1)


def finish(grid, band, summed, conv_bias, second, first, occupied, parts):
    channels, frames, height, columns = grid.shape
    slots = occupied.shape[1] // parts
    smem, vmem = pl.BlockSpec(memory_space=pltpu.SMEM), pl.BlockSpec(memory_space=pltpu.VMEM)
    return pl.pallas_call(
        finish_kernel,
        in_specs=[smem, smem, vmem, vmem, vmem, vmem, vmem],
        out_shape=[jax.ShapeDtypeStruct(grid.shape, jnp.bfloat16)]
        + [jax.ShapeDtypeStruct((frames, channels * slots, LANES), jnp.bfloat16)] * parts,
        scratch_shapes=[
            pltpu.VMEM((parts * GROUP * slots, GROUP * height), jnp.bfloat16),
            pltpu.VMEM((parts * GROUP * slots, LANES), jnp.int32),
        ],
        compiler_params=params(8),
        cost_estimate=pl.CostEstimate(flops=2**30, bytes_accessed=2**23, transcendentals=2**20),
        name="finish",
    )(occupied, conv_bias, grid, band, summed, second, first)


def tables_kernel(depth_ref, point_ref, _, table_ref, mix_ref):
    layers, channels, _ = point_ref.shape
    taps = depth_ref.shape[0]
    tall = mix_ref.shape[1]
    slots = tall // channels
    same_channel = iota((tall, channels), 0) // slots == iota((tall, channels), 1)
    up = same_channel.astype(jnp.bfloat16)
    across = (iota((channels, tall), 1) // slots == iota((channels, tall), 0)).astype(jnp.bfloat16)
    same_slot = iota((tall, tall), 0) % slots == iota((tall, tall), 1) % slots
    for layer in range(layers):
        for tap in range(taps):
            row = 0.5 * depth_ref[tap, layer : layer + 1, :]
            column = jnp.sum(jnp.where(same_channel, row, 0.0), axis=1, keepdims=True)
            table_ref[layer * taps + tap] = jnp.broadcast_to(column, table_ref.shape[1:])
        spread = dot(dot(up, point_ref[layer]).astype(jnp.bfloat16), across)
        mix_ref[layer] = jnp.where(same_slot, spread, 0.0).astype(jnp.bfloat16)


def tables(depth_kernel, point_weight, slots, after):
    layers, taps, channels = depth_kernel.shape
    vmem = pl.BlockSpec(memory_space=pltpu.VMEM)
    return pl.pallas_call(
        tables_kernel,
        in_specs=[vmem, vmem, pl.BlockSpec(memory_space=pl.ANY)],
        out_shape=(
            jax.ShapeDtypeStruct((layers * taps, channels * slots, LANES), jnp.float32),
            jax.ShapeDtypeStruct((layers, channels * slots, channels * slots), jnp.bfloat16),
        ),
        compiler_params=params(8),
        cost_estimate=pl.CostEstimate(flops=2**27, bytes_accessed=2**22, transcendentals=0),
        name="tables",
    )(jnp.transpose(depth_kernel, (1, 0, 2)), point_weight, after)


def temporal_kernel(sources, depth_ref, mix_ref, *refs):
    message_refs, out_refs = refs[:sources], refs[sources : 2 * sources]
    state, squashed, final = refs[2 * sources :]
    me = lax.axis_index("frame")
    local, tall, lanes = message_refs[0].shape
    frames = sources * local
    layers = mix_ref.shape[0]
    taps = depth_ref.shape[0] // layers
    quads, _, width = squashed.shape
    quad = width // lanes
    for step, message_ref in zip(steps_of(sources), message_refs):
        for f in range(local):
            state[got_from(me, step) * local + f] = message_ref[f].astype(jnp.float32)
    height = 32
    for layer in range(layers):
        spacing = 2**layer
        for q in reversed(range(quads)):
            inside = range(q * quad, (q + 1) * quad)
            for top in range(0, tall, height):
                part = slice(top, top + height)
                scale = [depth_ref[layer * taps + tap, part] for tap in range(taps)]
                needed = {f - tap * spacing for f in inside for tap in range(taps)}
                series = {f: state[f, part] for f in needed if f >= 0}
                for f in inside:
                    half = scale[0] * series[f]
                    for tap in range(1, taps):
                        if f >= tap * spacing:
                            half += scale[tap] * series[f - tap * spacing]
                    across = slice((f - q * quad) * lanes, (f - q * quad + 1) * lanes)
                    squashed[q, part, across] = (half + half * jnp.tanh(half)).astype(jnp.bfloat16)
            mixed = dot(mix_ref[layer], squashed[q])
            for f in inside:
                after = state[f] + mixed[:, (f - q * quad) * lanes : (f - q * quad + 1) * lanes]
                if layer + 1 < layers:
                    state[f] = after
                else:
                    final[f] = after.astype(jnp.bfloat16)
    for step, out_ref in zip(steps_of(sources, True), out_refs):
        for f in range(local):
            out_ref[f] = final[sent_to(me, step) * local + f]


def temporal(messages, depth, mix):
    sources = len(messages)
    local, tall, lanes = messages[0].shape
    vmem = pl.BlockSpec(memory_space=pltpu.VMEM)
    return pl.pallas_call(
        functools.partial(temporal_kernel, sources),
        in_specs=[vmem, vmem] + [vmem] * sources,
        out_shape=[jax.ShapeDtypeStruct(messages[0].shape, jnp.bfloat16)] * sources,
        scratch_shapes=[
            pltpu.VMEM((sources * local, tall, lanes), jnp.float32),
            pltpu.VMEM((sources * local // 4, tall, 4 * lanes), jnp.bfloat16),
            pltpu.VMEM((sources * local, tall, lanes), jnp.bfloat16),
        ],
        compiler_params=params(12),
        cost_estimate=pl.CostEstimate(flops=2**30, bytes_accessed=2**21, transcendentals=2**21),
        name="temporal",
    )(depth, mix, *messages)


def plan_kernel(sources, occupied_ref, counts_ref, _, put_ref, cover_ref):
    me = lax.axis_index("frame")
    halves, wide, tall = put_ref.shape
    part = tall // sources
    slots = part // GROUP
    height = wide // GROUP
    rows, lanes = iota((part, wide), 0), iota((part, wide), 1)
    same_channel, at_slot, at_row = lanes // height == rows // slots, rows % slots, lanes % height
    for side in range(halves):
        hits = []
        for step in steps_of(sources, True):
            row = jnp.full((part, wide), -1, jnp.int32)
            for j in range(slots):
                slot = got_from(me, step) * slots + j
                block = occupied_ref[0, slot]
                used = (slot < counts_ref[0]) & (block % halves == side)
                row = jnp.where(at_slot == j, jnp.where(used, block // halves, -1), row)
            hits.append((same_channel & (at_row == row)).astype(jnp.float32))
        put = jnp.transpose(jnp.concatenate(hits, axis=0)).astype(jnp.bfloat16)
        put_ref[side] = put
        cover_ref[side] = dot(put, jnp.ones((tall, LANES), jnp.bfloat16))


def plan(occupied, counts, wide, halves, sources, after):
    smem = pl.BlockSpec(memory_space=pltpu.SMEM)
    return pl.pallas_call(
        functools.partial(plan_kernel, sources),
        in_specs=[smem, smem, pl.BlockSpec(memory_space=pl.ANY)],
        out_shape=(
            jax.ShapeDtypeStruct((halves, wide, GROUP * occupied.shape[1]), jnp.bfloat16),
            jax.ShapeDtypeStruct((halves, wide, LANES), jnp.float32),
        ),
        compiler_params=params(8),
        cost_estimate=pl.CostEstimate(flops=2**27, bytes_accessed=2**22, transcendentals=0),
        name="plan",
    )(occupied, counts, after)


def place_kernel(sources, put_ref, cover_ref, hidden_ref, *refs):
    message_refs, (out_hbm, out_ref, sems) = refs[:sources], refs[sources:]
    channels, frames, height, columns = hidden_ref.shape
    halves = columns // LANES
    wide = GROUP * height
    part = put_ref.shape[2] // sources

    def group_copy(g):
        cells = pl.ds(pl.multiple_of(g * GROUP, GROUP), GROUP)
        return pltpu.make_async_copy(out_ref.at[cells], out_hbm.at[cells], sems.at[g])

    def merge(g, carry):
        base = pl.multiple_of(g * GROUP, GROUP)
        rows_of = pl.ds(pl.multiple_of(g * part, part), part)
        updated = jnp.concatenate(
            [
                jnp.concatenate([ref[f, rows_of, :] for f in range(frames)], axis=1)
                for ref in message_refs
            ],
            axis=0,
        )
        for side in range(halves):
            spread = dot(put_ref[side], updated)
            across = slice(side * LANES, (side + 1) * LANES)
            for f in range(frames):
                cells = hidden_ref[pl.ds(base, GROUP), f, :, across].reshape(wide, LANES).astype(jnp.float32)
                merged = jnp.where(cover_ref[side] > 0.5, spread[:, f * LANES : (f + 1) * LANES], cells)
                out_ref[pl.ds(base, GROUP), f, :, across] = merged.astype(jnp.bfloat16).reshape(GROUP, height, LANES)
        group_copy(g).start()
        return carry

    groups = channels // GROUP
    lax.fori_loop(0, groups, merge, 0, unroll=True)
    for g in range(groups):
        group_copy(g).wait()


def place(hidden, messages, put, cover):
    channels = hidden.shape[0]
    sources = len(messages)
    vmem, anywhere = pl.BlockSpec(memory_space=pltpu.VMEM), pl.BlockSpec(memory_space=pl.ANY)
    return pl.pallas_call(
        functools.partial(place_kernel, sources),
        in_specs=[vmem, vmem, vmem] + [vmem] * sources,
        out_specs=anywhere,
        out_shape=jax.ShapeDtypeStruct(hidden.shape, jnp.bfloat16),
        scratch_shapes=[
            pltpu.VMEM(hidden.shape, jnp.bfloat16),
            pltpu.SemaphoreType.DMA((channels // GROUP,)),
        ],
        compiler_params=params(8),
        cost_estimate=pl.CostEstimate(flops=2**28, bytes_accessed=2**22, transcendentals=0),
        name="place",
    )(put, cover, hidden, *messages)


def exchange(arrays, core_first):
    count = len(arrays)
    return [
        array if step == (0, 0) else lax.ppermute(array, "frame", [(i, i ^ step[i % 2]) for i in range(count)])
        for array, step in zip(arrays, steps_of(count, core_first))
    ]


def on_device(grid, conv_weight, conv_bias, depth_kernel, point_weight, occupied, counts):
    channels, frames, height, columns = grid.shape
    tiles, parts = lax.axis_size("tile"), lax.axis_size("frame")
    slots = occupied.shape[1] // parts
    band = bands(conv_weight, height)
    second, first = edge_columns(grid, band)
    second = lax.ppermute(second, "tile", swaps(tiles, 1))
    first = lax.ppermute(first, "tile", swaps(tiles, 0))
    summed = inner(grid, band)
    hidden, *messages = finish(grid, band, summed, conv_bias, second, first, occupied, parts)
    depth, mix = tables(depth_kernel, point_weight, slots, messages[0])
    updated = temporal(exchange(messages, False), depth, mix)
    put, cover = plan(occupied, counts, GROUP * height, columns // LANES, parts, updated[0])
    return place(hidden, exchange(updated, True), put, cover)


def solution(mesh):
    placed = (P(None, "frame", None, "tile"), P(), P(), P(), P(), P("tile", None), P("tile"))
    return jax.shard_map(
        on_device,
        mesh=mesh,
        in_specs=placed,
        out_specs=P(None, "frame", None, "tile"),
        check_vma=False,
    )
```

time: 143 us -> 49.1 us (0.34)
  the two profiles are of different devices: /device:TPU:0 before, /device:TPU:1 now
where the time goes in v1:
time: 49.1 us; the launch traced here: 49 us
  starting transfers between devices  22.1 us (45%)
  Pallas kernels  14.2 us (29%)
  waiting for transfers between devices  10.9 us (22%)
  local copies, waits for them, and re-layouts  0.9 us (2%)
  between operations  0.81 us (2%)
    ppermute x14, starting transfers between devices, exchange(): lax.ppermute(array, 'frame', [(i, i ^ step[i % 2]) for i in range(count)])  16.7 us
    ppermute x14, waiting for transfers between devices, exchange(): lax.ppermute(array, 'frame', [(i, i ^ step[i % 2]) for i in range(count)])  10.9 us
    ppermute x1, starting transfers between devices, on_device(): first = lax.ppermute(first, 'tile', swaps(tiles, 0))  4.73 us
    pallas_call x1, Pallas kernels, temporal(): pl.pallas_call(functools.partial(temporal_kernel, sources), in_specs=[vme...  3.82 us
    pallas_call x1, Pallas kernels, finish(): pl.pallas_call(finish_kernel, in_specs=[smem, smem, vmem, vmem, vmem, vme...  2.68 us
    pallas_call x1, Pallas kernels, inner(): pl.pallas_call(inner_kernel, out_shape=jax.ShapeDtypeStruct((channels //...  2.18 us
    pallas_call x1, Pallas kernels, place(): pl.pallas_call(functools.partial(place_kernel, sources), in_specs=[vmem,...  1.63 us
    pallas_call x1, Pallas kernels, bands(): pl.pallas_call(functools.partial(bands_kernel, height), out_shape=jax.Sha...  1.39 us
  transfers between devices with their start and end apart: 16, of which 7 were waited for; matrix products, arithmetic and copies ran while one was open for 0% of the time, Pallas kernels for 8%

profile of v1, /device:TPU:1, one launch (start us, length us, event | category | flops | bytes accessed | tf_op | source)
XLA Modules:
  0.0 49.0 jit_solution(4906160530800861488)
XLA Ops:
  0.0 0.9 %copy-done.1 = bf16[9,64,8]{1,2,0:T(8,128)(2,1)S(1)} copy-done((bf16[9,64,8]{1,2,0:T(8,128)(2,1)S(1)}, bf16[9,64,8]{1,2,0:T(8,128)(2,1)}, u32[]{:S(2)}) %copy-start.1) | copy-done | bytes 9240
  0.9 1.4 %bands.1.band_ref._ = bf16[8,256,768]{2,1,0:T(8,128)(2,1)S(1)} custom-call(bf16[9,8,64]{2,1,0:T(8,128)(2,1)S(1)} %bitcast.2), custom_call_target="tpu_custom_call" | custom-call | flops 268435456 | bytes 8388608 | tf_op jit(solution)/shard_map/bands/pallas_call | solution.py:99
  2.3 0.7 %edge_columns.1 = (bf16[16,256]{1,0:T(8,128)(2,1)S(1)}, bf16[16,256]{1,0:T(8,128)(2,1)S(1)}) custom-call(bf16[64,2,32,256]{3,2,1,0:T(8,128)(2,1)S(1)} %copy-done, bf16[8,256,768]{2,1,0:T(8,128)(2,1)S(1)} %bands.1.band_ref._), custom_call_target="tpu_custom_call" | custom-call | flops 268435456 | bytes 2097152 | tf_op jit(solution)/shard_map/edge_columns/pallas_call | solution.py:60
  3.7 4.7 %collective-permute-start.1 = (bf16[16,256]{1,0:T(8,128)(2,1)S(1)}, bf16[16,256]{1,0:T(8,128)(2,1)S(1)}, u32[]{:S(2)}, u32[]{:S(2)}) collective-permute-start(bf16[16,256]{1,0:T(8,128)(2,1)S(1)} %get-tuple-element.29), channel_id=1, source_target_pairs={{0,1},{1,0},{2,3},{3,2},{4,5},{5,4},{6,7},{7,6},{8,9},{9,8},{10,11... | collective-permute-start | bytes 24584 | tf_op jit(solution)/shard_map/ppermute | solution.py:449
  8.4 2.2 %inner.1.summed_ref = f32[8,2,256,256]{3,2,1,0:T(8,128)S(1)} custom-call(bf16[64,2,32,256]{3,2,1,0:T(8,128)(2,1)S(1)} %copy-done, bf16[8,256,768]{2,1,0:T(8,128)(2,1)S(1)} %bands.1.band_ref._), custom_call_target="tpu_custom_call" | custom-call | flops 2147483648 | bytes 8388608 | tf_op jit(solution)/shard_map/inner/pallas_call | solution.py:129
  10.7 2.7 %finish.1 = (bf16[64,2,32,256]{3,2,1,0:T(8,128)(2,1)S(1)}, bf16[2,256,128]{2,1,0:T(8,128)(2,1)S(1)}, bf16[2,256,128]{2,1,0:T(8,128)(2,1)S(1)}, bf16[2,256,128]{2...) custom-call(s32[1,32]{1,0:T(1,128)S(1)} %copy-done.3, ...), custom_call_target="tpu_custom_call" | custom-call | flops 1073741824 | bytes 8388608 | tf_op jit(solution)/shard_map/finish/pallas_call | solution.py:230
  13.4 1.3 %collective-permute-start.2 = (bf16[2,256,128]{2,1,0:T(8,128)(2,1)S(1)}, bf16[2,256,128]{2,1,0:T(8,128)(2,1)S(1)}, u32[]{:S(2)}, u32[]{:S(2)}) collective-permute-start(bf16[2,256,128]{2,1,0:T(8,128)(2,1)S(1)} %get-tuple-element.33), channel_id=1, source_target_pairs={{0,16},{4,12},{8,24},{12,4},{16,0},{20,28},{24,8},{28,20},{1,17},{... | collective-permute-start | bytes 393224 | tf_op jit(solution)/shard_map/ppermute | solution.py:437
  14.6 1.2 %collective-permute-start.3 = (bf16[2,256,128]{2,1,0:T(8,128)(2,1)S(1)}, bf16[2,256,128]{2,1,0:T(8,128)(2,1)S(1)}, u32[]{:S(2)}, u32[]{:S(2)}) collective-permute-start(bf16[2,256,128]{2,1,0:T(8,128)(2,1)S(1)} %get-tuple-element.34), channel_id=1, source_target_pairs={{0,8},{4,20},{8,0},{12,28},{16,24},{20,4},{24,16},{28,12},{1,9},{5... | collective-permute-start | bytes 393224 | tf_op jit(solution)/shard_map/ppermute | solution.py:437
  15.9 1.9 %collective-permute-start.4 = (bf16[2,256,128]{2,1,0:T(8,128)(2,1)S(1)}, bf16[2,256,128]{2,1,0:T(8,128)(2,1)S(1)}, u32[]{:S(2)}, u32[]{:S(2)}) collective-permute-start(bf16[2,256,128]{2,1,0:T(8,128)(2,1)S(1)} %get-tuple-element.35), channel_id=1, source_target_pairs={{0,20},{4,8},{8,28},{12,0},{16,4},{20,24},{24,12},{28,16},{1,21},{... | collective-permute-start | bytes 393224 | tf_op jit(solution)/shard_map/ppermute | solution.py:437
  17.8 1.2 %collective-permute-start.6 = (bf16[2,256,128]{2,1,0:T(8,128)(2,1)S(1)}, bf16[2,256,128]{2,1,0:T(8,128)(2,1)S(1)}, u32[]{:S(2)}, u32[]{:S(2)}) collective-permute-start(bf16[2,256,128]{2,1,0:T(8,128)(2,1)S(1)} %get-tuple-element.37), channel_id=1, source_target_pairs={{0,24},{4,28},{8,16},{12,20},{16,8},{20,12},{24,0},{28,4},{1,25},{... | collective-permute-start | bytes 393224 | tf_op jit(solution)/shard_map/ppermute | solution.py:437
  19.0 3.0 %collective-permute-start.7 = (bf16[2,256,128]{2,1,0:T(8,128)(2,1)S(1)}, bf16[2,256,128]{2,1,0:T(8,128)(2,1)S(1)}, u32[]{:S(2)}, u32[]{:S(2)}) collective-permute-start(bf16[2,256,128]{2,1,0:T(8,128)(2,1)S(1)} %get-tuple-element.38), channel_id=1, source_target_pairs={{0,28},{4,24},{8,20},{12,16},{16,12},{20,8},{24,4},{28,0},{1,29},{... | collective-permute-start | bytes 393224 | tf_op jit(solution)/shard_map/ppermute | solution.py:437
  22.8 1.3 %collective-permute-done.5.refs_4_ = bf16[2,256,128]{2,1,0:T(8,128)(2,1)S(1)} collective-permute-done((bf16[2,256,128]{2,1,0:T(8,128)(2,1)S(1)}, bf16[2,256,128]{2,1,0:T(8,128)(2,1)S(1)}, u32[]{:S(2)}, u32[]{:S(2)}) %collective-permute-start.5) | collective-permute-done | bytes 131104 | tf_op jit(solution)/shard_map/ppermute | solution.py:437
  24.0 1.8 %collective-permute-done.6.refs_5_ = bf16[2,256,128]{2,1,0:T(8,128)(2,1)S(1)} collective-permute-done((bf16[2,256,128]{2,1,0:T(8,128)(2,1)S(1)}, bf16[2,256,128]{2,1,0:T(8,128)(2,1)S(1)}, u32[]{:S(2)}, u32[]{:S(2)}) %collective-permute-start.6) | collective-permute-done | bytes 131104 | tf_op jit(solution)/shard_map/ppermute | solution.py:437
  25.8 3.0 %collective-permute-done.7.refs_6_ = bf16[2,256,128]{2,1,0:T(8,128)(2,1)S(1)} collective-permute-done((bf16[2,256,128]{2,1,0:T(8,128)(2,1)S(1)}, bf16[2,256,128]{2,1,0:T(8,128)(2,1)S(1)}, u32[]{:S(2)}, u32[]{:S(2)}) %collective-permute-start.7) | collective-permute-done | bytes 131104 | tf_op jit(solution)/shard_map/ppermute | solution.py:437
  28.8 3.8 %temporal.1 = (bf16[2,256,128]{2,1,0:T(8,128)(2,1)S(1)}, bf16[2,256,128]{2,1,0:T(8,128)(2,1)S(1)}, bf16[2,256,128]{2,1,0:T(8,128)(2,1)S(1)}, bf16[2,256,128]{2,1...) custom-call(f32[12,256,128]{2,1,0:T(8,128)S(1)} %get-tuple-element.3, ...), custom_call_target="tpu_custom_call" | custom-call | flops 1073741824 | bytes 2097152 | tf_op jit(solution)/shard_map/temporal/pallas_call | solution.py:325
  32.6 1.2 %collective-permute-start.10 = (bf16[2,256,128]{2,1,0:T(8,128)(2,1)S(1)}, bf16[2,256,128]{2,1,0:T(8,128)(2,1)S(1)}, u32[]{:S(2)}, u32[]{:S(2)}) collective-permute-start(bf16[2,256,128]{2,1,0:T(8,128)(2,1)S(1)} %get-tuple-element.45), channel_id=1, source_target_pairs={{0,16},{4,12},{8,24},{12,4},{16,0},{20,28},{24,8},{28,20},{1,17},{... | collective-permute-start | bytes 393224 | tf_op jit(solution)/shard_map/ppermute | solution.py:437
  33.9 1.2 %collective-permute-start.11 = (bf16[2,256,128]{2,1,0:T(8,128)(2,1)S(1)}, bf16[2,256,128]{2,1,0:T(8,128)(2,1)S(1)}, u32[]{:S(2)}, u32[]{:S(2)}) collective-permute-start(bf16[2,256,128]{2,1,0:T(8,128)(2,1)S(1)} %get-tuple-element.46), channel_id=1, source_target_pairs={{0,8},{4,20},{8,0},{12,28},{16,24},{20,4},{24,16},{28,12},{1,9},{5... | collective-permute-start | bytes 393224 | tf_op jit(solution)/shard_map/ppermute | solution.py:437
  35.1 0.9 %collective-permute-start.12 = (bf16[2,256,128]{2,1,0:T(8,128)(2,1)S(1)}, bf16[2,256,128]{2,1,0:T(8,128)(2,1)S(1)}, u32[]{:S(2)}, u32[]{:S(2)}) collective-permute-start(bf16[2,256,128]{2,1,0:T(8,128)(2,1)S(1)} %get-tuple-element.47), channel_id=1, source_target_pairs={{0,20},{4,8},{8,28},{12,0},{16,4},{20,24},{24,12},{28,16},{1,21},{... | collective-permute-start | bytes 393224 | tf_op jit(solution)/shard_map/ppermute | solution.py:437
  36.1 0.8 %collective-permute-start.13 = (bf16[2,256,128]{2,1,0:T(8,128)(2,1)S(1)}, bf16[2,256,128]{2,1,0:T(8,128)(2,1)S(1)}, u32[]{:S(2)}, u32[]{:S(2)}) collective-permute-start(bf16[2,256,128]{2,1,0:T(8,128)(2,1)S(1)} %get-tuple-element.48), channel_id=1, source_target_pairs={{0,12},{4,16},{8,4},{12,24},{16,28},{20,0},{24,20},{28,8},{1,13},{... | collective-permute-start | bytes 393224 | tf_op jit(solution)/shard_map/ppermute | solution.py:437
  37.2 2.7 %collective-permute-start.15 = (bf16[2,256,128]{2,1,0:T(8,128)(2,1)S(1)}, bf16[2,256,128]{2,1,0:T(8,128)(2,1)S(1)}, u32[]{:S(2)}, u32[]{:S(2)}) collective-permute-start(bf16[2,256,128]{2,1,0:T(8,128)(2,1)S(1)} %get-tuple-element.50), channel_id=1, source_target_pairs={{0,28},{4,24},{8,20},{12,16},{16,12},{20,8},{24,4},{28,0},{1,29},{... | collective-permute-start | bytes 393224 | tf_op jit(solution)/shard_map/ppermute | solution.py:437
  39.9 0.9 %collective-permute-start.9 = (bf16[2,256,128]{2,1,0:T(8,128)(2,1)S(1)}, bf16[2,256,128]{2,1,0:T(8,128)(2,1)S(1)}, u32[]{:S(2)}, u32[]{:S(2)}) collective-permute-start(bf16[2,256,128]{2,1,0:T(8,128)(2,1)S(1)} %get-tuple-element.44), channel_id=1, source_target_pairs={{0,4},{4,0},{8,12},{12,8},{16,20},{20,16},{24,28},{28,24},{1,5},{5... | collective-permute-start | bytes 393224 | tf_op jit(solution)/shard_map/ppermute | solution.py:437
  41.4 1.3 %plan.1 = (bf16[2,256,256]{2,1,0:T(8,128)(2,1)S(1)}, f32[2,256,128]{2,1,0:T(8,128)S(1)}) custom-call(s32[1,32]{1,0:T(1,128)S(1)} %copy-done.3, s32[1]{0:T(128)S(6)} %copy.8.counts_ref, bf16[2,256,128]{2,1,0:T(8,128)(2,1)S(1)} %get-tuple-element.40._.refs_0_), custom_call_target="tpu_custom_call" | custom-call | flops 134217728 | bytes 4194304 | tf_op jit(solution)/shard_map/plan/pallas_call | solution.py:365
  43.6 3.7 %collective-permute-done.15.refs_7_ = bf16[2,256,128]{2,1,0:T(8,128)(2,1)S(1)} collective-permute-done((bf16[2,256,128]{2,1,0:T(8,128)(2,1)S(1)}, bf16[2,256,128]{2,1,0:T(8,128)(2,1)S(1)}, u32[]{:S(2)}, u32[]{:S(2)}) %collective-permute-start.15) | collective-permute-done | bytes 131104 | tf_op jit(solution)/shard_map/ppermute | solution.py:437
  47.3 1.6 %place.1 = bf16[64,2,32,256]{3,2,1,0:T(8,128)(2,1)} custom-call(bf16[2,256,256]{2,1,0:T(8,128)(2,1)S(1)} %get-tuple-element.41.put_ref, f32[2,256,128]{2,1,0:T(8,128)S(1)} %get-tuple-element.42.cover_ref, bf16[64,2,32,256]{3,2,1,0:T(8,128)(2,1)S(1)} %get-tuple-element.43.hidden_ref, bf16[2,256,128]{2,1,0:T(8,128)(2,1)S(1)} %get-tuple-element.40._.refs_0_, ...), custom_call_target="tpu_custom_call" | custom-call | flops 268435456 | bytes 4194304 | tf_op jit(solution)/shard_map/place/pallas_call | solution.py:419
  (28 shorter events, 2.8 us)
Async XLA Ops:
  0.0 2.3 %copy-start = (bf16[64,2,32,256]{3,2,1,0:T(8,128)(2,1)S(1)}, bf16[64,2,32,256]{3,2,1,0:T(8,128)(2,1)}, u32[]{:S(2)}) copy-start(bf16[64,2,32,256]{3,2,1,0:T(8,128)(2,1)} %grid_ref.5) | copy-start | bytes 6291460
  0.0 0.9 %copy-start.1 = (bf16[9,64,8]{1,2,0:T(8,128)(2,1)S(1)}, bf16[9,64,8]{1,2,0:T(8,128)(2,1)}, u32[]{:S(2)}) copy-start(bf16[9,64,8]{1,2,0:T(8,128)(2,1)} %param.8) | copy-start | bytes 27652
  3.0 7.6 %collective-permute-start = (bf16[16,256]{1,0:T(8,128)(2,1)S(1)}, bf16[16,256]{1,0:T(8,128)(2,1)S(1)}, u32[]{:S(2)}, u32[]{:S(2)}) collective-permute-start(bf16[16,256]{1,0:T(8,128)(2,1)S(1)} %get-tuple-element.28), channel_id=1, source_target_pairs={{0,0},{1,2},{2,1},{3,3},{4,4},{5,6},{6,5},{7,7},{8,8},{9,10},{10,9... | collective-permute-start | bytes 24584 | tf_op jit(solution)/shard_map/ppermute | solution.py:448
  3.7 7.0 %copy-start.2 = (f32[64]{0:T(128)S(1)}, f32[64]{0:T(128)}, u32[]{:S(2)}) copy-start(f32[64]{0:T(128)} %bias_ref.1) | copy-start | bytes 772
  3.7 7.0 %copy-start.3 = (s32[1,32]{1,0:T(1,128)S(1)}, s32[1,32]{1,0:T(1,128)}, u32[]{:S(2)}) copy-start(s32[1,32]{1,0:T(1,128)} %occupied_ref.3) | copy-start | bytes 388
  3.7 7.0 %collective-permute-start.1 = (bf16[16,256]{1,0:T(8,128)(2,1)S(1)}, bf16[16,256]{1,0:T(8,128)(2,1)S(1)}, u32[]{:S(2)}, u32[]{:S(2)}) collective-permute-start(bf16[16,256]{1,0:T(8,128)(2,1)S(1)} %get-tuple-element.29), channel_id=1, source_target_pairs={{0,1},{1,0},{2,3},{3,2},{4,5},{5,4},{6,7},{7,6},{8,9},{9,8},{10,11... | collective-permute-start | bytes 24584 | tf_op jit(solution)/shard_map/ppermute | solution.py:449
  10.6 11.4 %copy-start.4 = (bf16[4,64,64]{2,1,0:T(8,128)(2,1)S(1)}, bf16[4,64,64]{2,1,0:T(8,128)(2,1)}, u32[]{:S(2)}) copy-start(bf16[4,64,64]{2,1,0:T(8,128)(2,1)} %point_ref.1) | copy-start | bytes 98308
  10.6 11.3 %copy-start.5 = (f32[4,3,64]{2,0,1:T(4,128)S(1)}, f32[4,3,64]{2,0,1:T(4,128)}, u32[]{:S(2)}) copy-start(f32[4,3,64]{2,0,1:T(4,128)} %param.10) | copy-start | bytes 9220
  13.4 5.6 %collective-permute-start.2 = (bf16[2,256,128]{2,1,0:T(8,128)(2,1)S(1)}, bf16[2,256,128]{2,1,0:T(8,128)(2,1)S(1)}, u32[]{:S(2)}, u32[]{:S(2)}) collective-permute-start(bf16[2,256,128]{2,1,0:T(8,128)(2,1)S(1)} %get-tuple-element.33), channel_id=1, source_target_pairs={{0,16},{4,12},{8,24},{12,4},{16,0},{20,28},{24,8},{28,20},{1,17},{... | collective-permute-start | bytes 393224 | tf_op jit(solution)/shard_map/ppermute | solution.py:437
  14.6 7.3 %collective-permute-start.3 = (bf16[2,256,128]{2,1,0:T(8,128)(2,1)S(1)}, bf16[2,256,128]{2,1,0:T(8,128)(2,1)S(1)}, u32[]{:S(2)}, u32[]{:S(2)}) collective-permute-start(bf16[2,256,128]{2,1,0:T(8,128)(2,1)S(1)} %get-tuple-element.34), channel_id=1, source_target_pairs={{0,8},{4,20},{8,0},{12,28},{16,24},{20,4},{24,16},{28,12},{1,9},{5... | collective-permute-start | bytes 393224 | tf_op jit(solution)/shard_map/ppermute | solution.py:437
  15.9 6.9 %collective-permute-start.4 = (bf16[2,256,128]{2,1,0:T(8,128)(2,1)S(1)}, bf16[2,256,128]{2,1,0:T(8,128)(2,1)S(1)}, u32[]{:S(2)}, u32[]{:S(2)}) collective-permute-start(bf16[2,256,128]{2,1,0:T(8,128)(2,1)S(1)} %get-tuple-element.35), channel_id=1, source_target_pairs={{0,20},{4,8},{8,28},{12,0},{16,4},{20,24},{24,12},{28,16},{1,21},{... | collective-permute-start | bytes 393224 | tf_op jit(solution)/shard_map/ppermute | solution.py:437
  17.8 6.2 %collective-permute-start.5 = (bf16[2,256,128]{2,1,0:T(8,128)(2,1)S(1)}, bf16[2,256,128]{2,1,0:T(8,128)(2,1)S(1)}, u32[]{:S(2)}, u32[]{:S(2)}) collective-permute-start(bf16[2,256,128]{2,1,0:T(8,128)(2,1)S(1)} %get-tuple-element.36), channel_id=1, source_target_pairs={{0,12},{4,16},{8,4},{12,24},{16,28},{20,0},{24,20},{28,8},{1,13},{... | collective-permute-start | bytes 393224 | tf_op jit(solution)/shard_map/ppermute | solution.py:437
  17.8 8.0 %collective-permute-start.6 = (bf16[2,256,128]{2,1,0:T(8,128)(2,1)S(1)}, bf16[2,256,128]{2,1,0:T(8,128)(2,1)S(1)}, u32[]{:S(2)}, u32[]{:S(2)}) collective-permute-start(bf16[2,256,128]{2,1,0:T(8,128)(2,1)S(1)} %get-tuple-element.37), channel_id=1, source_target_pairs={{0,24},{4,28},{8,16},{12,20},{16,8},{20,12},{24,0},{28,4},{1,25},{... | collective-permute-start | bytes 393224 | tf_op jit(solution)/shard_map/ppermute | solution.py:437
  19.0 9.8 %collective-permute-start.7 = (bf16[2,256,128]{2,1,0:T(8,128)(2,1)S(1)}, bf16[2,256,128]{2,1,0:T(8,128)(2,1)S(1)}, u32[]{:S(2)}, u32[]{:S(2)}) collective-permute-start(bf16[2,256,128]{2,1,0:T(8,128)(2,1)S(1)} %get-tuple-element.38), channel_id=1, source_target_pairs={{0,28},{4,24},{8,20},{12,16},{16,12},{20,8},{24,4},{28,0},{1,29},{... | collective-permute-start | bytes 393224 | tf_op jit(solution)/shard_map/ppermute | solution.py:437
  22.0 6.9 %collective-permute-start.8 = (bf16[2,256,128]{2,1,0:T(8,128)(2,1)S(1)}, bf16[2,256,128]{2,1,0:T(8,128)(2,1)S(1)}, u32[]{:S(2)}, u32[]{:S(2)}) collective-permute-start(bf16[2,256,128]{2,1,0:T(8,128)(2,1)S(1)} %get-tuple-element.39), channel_id=1, source_target_pairs={{0,4},{4,0},{8,12},{12,8},{16,20},{20,16},{24,28},{28,24},{1,5},{5... | collective-permute-start | bytes 393224 | tf_op jit(solution)/shard_map/ppermute | solution.py:437
  32.6 4.6 %collective-permute-start.10 = (bf16[2,256,128]{2,1,0:T(8,128)(2,1)S(1)}, bf16[2,256,128]{2,1,0:T(8,128)(2,1)S(1)}, u32[]{:S(2)}, u32[]{:S(2)}) collective-permute-start(bf16[2,256,128]{2,1,0:T(8,128)(2,1)S(1)} %get-tuple-element.45), channel_id=1, source_target_pairs={{0,16},{4,12},{8,24},{12,4},{16,0},{20,28},{24,8},{28,20},{1,17},{... | collective-permute-start | bytes 393224 | tf_op jit(solution)/shard_map/ppermute | solution.py:437
  33.9 6.0 %collective-permute-start.11 = (bf16[2,256,128]{2,1,0:T(8,128)(2,1)S(1)}, bf16[2,256,128]{2,1,0:T(8,128)(2,1)S(1)}, u32[]{:S(2)}, u32[]{:S(2)}) collective-permute-start(bf16[2,256,128]{2,1,0:T(8,128)(2,1)S(1)} %get-tuple-element.46), channel_id=1, source_target_pairs={{0,8},{4,20},{8,0},{12,28},{16,24},{20,4},{24,16},{28,12},{1,9},{5... | collective-permute-start | bytes 393224 | tf_op jit(solution)/shard_map/ppermute | solution.py:437
  35.1 7.6 %collective-permute-start.12 = (bf16[2,256,128]{2,1,0:T(8,128)(2,1)S(1)}, bf16[2,256,128]{2,1,0:T(8,128)(2,1)S(1)}, u32[]{:S(2)}, u32[]{:S(2)}) collective-permute-start(bf16[2,256,128]{2,1,0:T(8,128)(2,1)S(1)} %get-tuple-element.47), channel_id=1, source_target_pairs={{0,20},{4,8},{8,28},{12,0},{16,4},{20,24},{24,12},{28,16},{1,21},{... | collective-permute-start | bytes 393224 | tf_op jit(solution)/shard_map/ppermute | solution.py:437
  36.1 7.2 %collective-permute-start.13 = (bf16[2,256,128]{2,1,0:T(8,128)(2,1)S(1)}, bf16[2,256,128]{2,1,0:T(8,128)(2,1)S(1)}, u32[]{:S(2)}, u32[]{:S(2)}) collective-permute-start(bf16[2,256,128]{2,1,0:T(8,128)(2,1)S(1)} %get-tuple-element.48), channel_id=1, source_target_pairs={{0,12},{4,16},{8,4},{12,24},{16,28},{20,0},{24,20},{28,8},{1,13},{... | collective-permute-start | bytes 393224 | tf_op jit(solution)/shard_map/ppermute | solution.py:437
  36.9 6.8 %collective-permute-start.14 = (bf16[2,256,128]{2,1,0:T(8,128)(2,1)S(1)}, bf16[2,256,128]{2,1,0:T(8,128)(2,1)S(1)}, u32[]{:S(2)}, u32[]{:S(2)}) collective-permute-start(bf16[2,256,128]{2,1,0:T(8,128)(2,1)S(1)} %get-tuple-element.49), channel_id=1, source_target_pairs={{0,24},{4,28},{8,16},{12,20},{16,8},{20,12},{24,0},{28,4},{1,25},{... | collective-permute-start | bytes 393224 | tf_op jit(solution)/shard_map/ppermute | solution.py:437
  37.2 10.1 %collective-permute-start.15 = (bf16[2,256,128]{2,1,0:T(8,128)(2,1)S(1)}, bf16[2,256,128]{2,1,0:T(8,128)(2,1)S(1)}, u32[]{:S(2)}, u32[]{:S(2)}) collective-permute-start(bf16[2,256,128]{2,1,0:T(8,128)(2,1)S(1)} %get-tuple-element.50), channel_id=1, source_target_pairs={{0,28},{4,24},{8,20},{12,16},{16,12},{20,8},{24,4},{28,0},{1,29},{... | collective-permute-start | bytes 393224 | tf_op jit(solution)/shard_map/ppermute | solution.py:437
  39.9 7.4 %collective-permute-start.9 = (bf16[2,256,128]{2,1,0:T(8,128)(2,1)S(1)}, bf16[2,256,128]{2,1,0:T(8,128)(2,1)S(1)}, u32[]{:S(2)}, u32[]{:S(2)}) collective-permute-start(bf16[2,256,128]{2,1,0:T(8,128)(2,1)S(1)} %get-tuple-element.44), channel_id=1, source_target_pairs={{0,4},{4,0},{8,12},{12,8},{16,20},{20,16},{24,28},{28,24},{1,5},{5... | collective-permute-start | bytes 393224 | tf_op jit(solution)/shard_map/ppermute | solution.py:437

commit v2 on v1

--- a/solution.py
+++ b/solution.py
@@ -10,6 +10,7 @@
 GROUP = 8
 LANES = 128
 MIB = 2**20
+ROLLED = jnp.bfloat16
 
 
 def params(mib):
@@ -28,7 +29,7 @@
     return lax.broadcasted_iota(jnp.int32, shape, dim)
 
 
-def edges_kernel(grid_ref, _, second_ref, first_ref):
+def edges_kernel(grid_ref, _, first_ref, second_ref):
     channels, frames, height, columns = grid_ref.shape
     groups, wide = channels // GROUP, GROUP * height
     count = groups * frames
@@ -89,7 +90,7 @@
                 )
         return carry
 
-    lax.fori_loop(0, groups, band, 0, unroll=True)
+    lax.fori_loop(0, groups, band, 0)
 
 
 def bands(conv_weight, height):
@@ -106,62 +107,17 @@
     )(taps)
 
 
-def inner_kernel(grid_ref, band_ref, summed_ref):
-    channels, frames, height, columns = grid_ref.shape
-    wide = GROUP * height
-    lanes = iota((wide, columns), 1)
-
-    def convolve(g, carry):
-        base = pl.multiple_of(g * GROUP, GROUP)
-        for f in range(frames):
-            cells = grid_ref[pl.ds(base, GROUP), f].reshape(wide, columns)
-            full = cells.astype(jnp.float32)
-            before = jnp.where(lanes == 0, 0.0, pltpu.roll(full, 1, 1)).astype(jnp.bfloat16)
-            after = jnp.where(lanes == columns - 1, 0.0, pltpu.roll(full, columns - 1, 1)).astype(jnp.bfloat16)
-            summed_ref[g, f] = dot(band_ref[g], jnp.concatenate([before, cells, after], axis=0))
-        return carry
-
-    lax.fori_loop(0, channels // GROUP, convolve, 0, unroll=True)
-
-
-def inner(grid, band):
-    channels, frames, height, columns = grid.shape
-    return pl.pallas_call(
-        inner_kernel,
-        out_shape=jax.ShapeDtypeStruct((channels // GROUP, frames, GROUP * height, columns), jnp.float32),
-        compiler_params=params(8),
-        cost_estimate=pl.CostEstimate(flops=2**31, bytes_accessed=2**23, transcendentals=0),
-        name="inner",
-    )(grid, band)
-
-
-def steps_of(count, core_first=False):
-    mixed = [(4, 2), (2, 4), (5, 3), (3, 5)] if count >= 8 else []
-    seen = {0, 1} | {a for a, _ in mixed}
-    across = mixed + [(d, d) for d in range(count) if d not in seen]
-    return [(0, 0), (1, 1)] + across if core_first else [(0, 0)] + across + [(1, 1)]
-
-
-def sent_to(me, step):
-    return me ^ jnp.where(me % 2 == 0, step[0], step[1])
-
-
-def got_from(me, step):
-    return sent_to(me, step) if step[0] % 2 == 0 else sent_to(me, step[::-1])
-
-
-def finish_kernel(occupied_ref, bias_ref, grid_ref, band_ref, summed_ref, second_ref, first_ref, hidden_ref, *rest):
-    message_refs, (pick_ref, side_ref) = rest[:-2], rest[-2:]
-    me = lax.axis_index("frame")
+def inner_kernel(occupied_ref, bias_ref, grid_ref, band_ref, summed_ref, cells_ref, pick_ref, side_ref):
     channels, frames, height, columns = grid_ref.shape
     halves = columns // LANES
     wide = GROUP * height
-    slots = occupied_ref.shape[1] // len(message_refs)
+    me, count = lax.axis_index("frame"), lax.axis_size("frame")
+    slots = occupied_ref.shape[1] // count
     part = GROUP * slots
     rows, lanes = iota((part, wide), 0), iota((part, wide), 1)
     at_slot, at_side = rows % slots, iota((part, LANES), 0) % slots
     same_channel, at_row = lanes // height == rows // slots, lanes % height
-    for d, step in enumerate(steps_of(len(message_refs))):
+    for d, step in enumerate(steps_of(count)):
         row, side = jnp.zeros((part, wide), jnp.int32), jnp.zeros((part, LANES), jnp.int32)
         for j in range(slots):
             block = occupied_ref[0, sent_to(me, step) * slots + j]
@@ -170,6 +126,72 @@
         pick_ref[d * part : (d + 1) * part, :] = (same_channel & (at_row == row)).astype(jnp.bfloat16)
         side_ref[d * part : (d + 1) * part, :] = side
 
+    tile_lanes = iota((wide, LANES), 1)
+    is_first, is_last = tile_lanes == 0, tile_lanes == LANES - 1
+    nothing = jnp.zeros((wide, LANES), ROLLED)
+
+    def shifted(g, f):
+        cells = grid_ref[g * GROUP : (g + 1) * GROUP, f].reshape(wide, columns)
+        tiles = [cells[:, side * LANES : (side + 1) * LANES].astype(ROLLED) for side in range(halves)]
+        right = [pltpu.roll(tile, 1, 1) for tile in tiles]
+        left = [pltpu.roll(tile, LANES - 1, 1) for tile in tiles]
+        before = [jnp.where(is_first, *pair) for pair in zip([nothing] + right[:-1], right)]
+        after = [jnp.where(is_last, *pair) for pair in zip(left[1:] + [nothing], left)]
+        join = lambda parts: jnp.concatenate(parts, axis=1).astype(jnp.bfloat16)
+        return jnp.concatenate([join(before), cells, join(after)], axis=0)
+
+    items = [(g, f) for g in range(channels // GROUP) for f in range(frames)]
+    ready = shifted(*items[0])
+    for (g, f), following in zip(items, items[1:] + [None]):
+        summed = dot(band_ref[g], ready)
+        if following is not None:
+            ready = shifted(*following)
+        for out in range(GROUP):
+            inside = slice(out * height, (out + 1) * height)
+            summed_ref[g, f, inside, :] = summed[inside] + 0.5 * bias_ref[g * GROUP + out]
+            cells_ref[g, f, inside, :] = grid_ref[g * GROUP + out, f].astype(jnp.float32)
+
+
+def inner(grid, band, conv_bias, occupied, parts):
+    channels, frames, height, columns = grid.shape
+    part = GROUP * (occupied.shape[1] // parts)
+    smem, vmem = pl.BlockSpec(memory_space=pltpu.SMEM), pl.BlockSpec(memory_space=pltpu.VMEM)
+    wide = jax.ShapeDtypeStruct((channels // GROUP, frames, GROUP * height, columns), jnp.float32)
+    return pl.pallas_call(
+        inner_kernel,
+        in_specs=[smem, smem, vmem, vmem],
+        out_shape=(
+            wide,
+            wide,
+            jax.ShapeDtypeStruct((parts * part, GROUP * height), jnp.bfloat16),
+            jax.ShapeDtypeStruct((parts * part, LANES), jnp.int32),
+        ),
+        compiler_params=params(8),
+        cost_estimate=pl.CostEstimate(flops=2**31, bytes_accessed=2**23, transcendentals=0),
+        name="inner",
+    )(occupied, conv_bias, grid, band)
+
+
+def steps_of(count, core_first=False):
+    mixed = [(4, 2), (2, 4), (5, 3), (3, 5)] if count >= 8 else []
+    seen = {0, 1} | {a for a, _ in mixed}
+    across = mixed + [(d, d) for d in range(count) if d not in seen]
+    return [(0, 0), (1, 1)] + across if core_first else [(0, 0)] + across + [(1, 1)]
+
+
+def sent_to(me, step):
+    return me ^ jnp.where(me % 2 == 0, step[0], step[1])
+
+
+def got_from(me, step):
+    return sent_to(me, step) if step[0] % 2 == 0 else sent_to(me, step[::-1])
+
+
+def finish_kernel(band_ref, summed_ref, cells_ref, pick_ref, side_ref, first_ref, second_ref, hidden_ref, *message_refs):
+    channels, frames, height, columns = hidden_ref.shape
+    halves = columns // LANES
+    wide = GROUP * height
+    part = pick_ref.shape[0] // len(message_refs)
     tile, tiles = lax.axis_index("tile"), lax.axis_size("tile")
     even = tile % 2 == 0
     first, second = first_ref[...].astype(jnp.float32), second_ref[...].astype(jnp.float32)
@@ -190,24 +212,28 @@
             dot(band_ref[g, :, 2 * wide :], jnp.concatenate(after, axis=0), ((1,), (1,))),
         )
 
-    def activate(g):
-        at_left, at_right = edge_terms(g)
+    def activate(g, at_left, at_right):
         for f in range(frames):
             across = slice(f * LANES, (f + 1) * LANES)
             for out in range(GROUP):
                 c = g * GROUP + out
                 part = slice(out * height, (out + 1) * height)
-                half = summed_ref[g, f, part, :] + 0.5 * bias_ref[c]
+                half = summed_ref[g, f, part, :]
                 tiles = [half[:, side * LANES : (side + 1) * LANES] for side in range(halves)]
                 tiles[0] += at_left[part, across]
                 tiles[-1] += at_right[part, across]
                 half = jnp.concatenate(tiles, axis=1)
-                hidden = grid_ref[c, f].astype(jnp.float32) + (half + half * jnp.tanh(half))
+                hidden = cells_ref[g, f, part, :] + (half + half * jnp.tanh(half))
                 hidden_ref[c, f] = hidden.astype(jnp.bfloat16)
 
     def pick(g):
-        for f in range(frames):
-            picked = dot(pick_ref[...], hidden_ref[g * GROUP : (g + 1) * GROUP, f].reshape(wide, columns))
+        return [
+            dot(pick_ref[...], hidden_ref[g * GROUP : (g + 1) * GROUP, f].reshape(wide, columns))
+            for f in range(frames)
+        ]
+
+    def send(g, picks):
+        for f, picked in enumerate(picks):
             chosen = picked[:, :LANES]
             for side in range(1, halves):
                 chosen = jnp.where(side_ref[...] == side, picked[:, side * LANES : (side + 1) * LANES], chosen)
@@ -216,30 +242,30 @@
                 message_ref[f, g * part : (g + 1) * part, :] = chosen[d * part : (d + 1) * part]
 
     groups = channels // GROUP
-    for g in range(groups + 1):
-        if g < groups:
-            activate(g)
-        if g > 0:
-            pick(g - 1)
-
-
-def finish(grid, band, summed, conv_bias, second, first, occupied, parts):
-    channels, frames, height, columns = grid.shape
-    slots = occupied.shape[1] // parts
-    smem, vmem = pl.BlockSpec(memory_space=pltpu.SMEM), pl.BlockSpec(memory_space=pltpu.VMEM)
+    terms = edge_terms(0)
+    for g in range(groups):
+        current = terms
+        picks = pick(g - 1) if g > 0 else None
+        terms = edge_terms(g + 1) if g + 1 < groups else None
+        activate(g, *current)
+        if picks is not None:
+            send(g - 1, picks)
+    send(groups - 1, pick(groups - 1))
+
+
+def finish(grid, band, summed, cells, pick, side, first, second, parts):
+    channels, frames, _, _ = grid.shape
+    slots = pick.shape[0] // (GROUP * parts)
+    vmem = pl.BlockSpec(memory_space=pltpu.VMEM)
     return pl.pallas_call(
         finish_kernel,
-        in_specs=[smem, smem, vmem, vmem, vmem, vmem, vmem],
+        in_specs=[vmem] * 7,
         out_shape=[jax.ShapeDtypeStruct(grid.shape, jnp.bfloat16)]
         + [jax.ShapeDtypeStruct((frames, channels * slots, LANES), jnp.bfloat16)] * parts,
-        scratch_shapes=[
-            pltpu.VMEM((parts * GROUP * slots, GROUP * height), jnp.bfloat16),
-            pltpu.VMEM((parts * GROUP * slots, LANES), jnp.int32),
-        ],
         compiler_params=params(8),
         cost_estimate=pl.CostEstimate(flops=2**30, bytes_accessed=2**23, transcendentals=2**20),
         name="finish",
-    )(occupied, conv_bias, grid, band, summed, second, first)
+    )(band, summed, cells, pick, side, first, second)
 
 
 def tables_kernel(depth_ref, point_ref, _, table_ref, mix_ref):
@@ -290,29 +316,43 @@
         for f in range(local):
             state[got_from(me, step) * local + f] = message_ref[f].astype(jnp.float32)
     height = 32
+
+    def blend(layer, q):
+        spacing = 2**layer
+        inside = range(q * quad, (q + 1) * quad)
+        for top in range(0, tall, height):
+            part = slice(top, top + height)
+            scale = [depth_ref[layer * taps + tap, part] for tap in range(taps)]
+            needed = {f - tap * spacing for f in inside for tap in range(taps)}
+            series = {f: state[f, part] for f in sorted(needed) if f >= 0}
+            for f in inside:
+                half = scale[0] * series[f]
+                for tap in range(1, taps):
+                    if f >= tap * spacing:
+                        half += scale[tap] * series[f - tap * spacing]
+                across = slice((f - q * quad) * lanes, (f - q * quad + 1) * lanes)
+                squashed[q, part, across] = (half + half * jnp.tanh(half)).astype(jnp.bfloat16)
+
+    def update(layer, q, mixed):
+        for f in range(q * quad, (q + 1) * quad):
+            after = state[f] + mixed[:, (f - q * quad) * lanes : (f - q * quad + 1) * lanes]
+            if layer + 1 < layers:
+                state[f] = after
+            else:
+                final[f] = after.astype(jnp.bfloat16)
+
+    waiting = None
     for layer in range(layers):
-        spacing = 2**layer
         for q in reversed(range(quads)):
-            inside = range(q * quad, (q + 1) * quad)
-            for top in range(0, tall, height):
-                part = slice(top, top + height)
-                scale = [depth_ref[layer * taps + tap, part] for tap in range(taps)]
-                needed = {f - tap * spacing for f in inside for tap in range(taps)}
-                series = {f: state[f, part] for f in needed if f >= 0}
-                for f in inside:
-                    half = scale[0] * series[f]
-                    for tap in range(1, taps):
-                        if f >= tap * spacing:
-                            half += scale[tap] * series[f - tap * spacing]
-                    across = slice((f - q * quad) * lanes, (f - q * quad + 1) * lanes)
-                    squashed[q, part, across] = (half + half * jnp.tanh(half)).astype(jnp.bfloat16)
-            mixed = dot(mix_ref[layer], squashed[q])
-            for f in inside:
-                after = state[f] + mixed[:, (f - q * quad) * lanes : (f - q * quad + 1) * lanes]
-                if layer + 1 < layers:
-                    state[f] = after
-                else:
-                    final[f] = after.astype(jnp.bfloat16)
+            reads = {(f - tap * 2**layer) // quad for f in range(q * quad, (q + 1) * quad) for tap in range(taps)}
+            late = waiting is not None and waiting[1] not in reads
+            if waiting is not None and not late:
+                update(*waiting)
+            blend(layer, q)
+            if late:
+                update(*waiting)
+            waiting = layer, q, dot(mix_ref[layer], squashed[q])
+    update(*waiting)
     for step, out_ref in zip(steps_of(sources, True), out_refs):
         for f in range(local):
             out_ref[f] = final[sent_to(me, step) * local + f]
@@ -383,31 +423,32 @@
     part = put_ref.shape[2] // sources
 
     def group_copy(g):
-        cells = pl.ds(pl.multiple_of(g * GROUP, GROUP), GROUP)
+        cells = pl.ds(g * GROUP, GROUP)
         return pltpu.make_async_copy(out_ref.at[cells], out_hbm.at[cells], sems.at[g])
 
-    def merge(g, carry):
-        base = pl.multiple_of(g * GROUP, GROUP)
-        rows_of = pl.ds(pl.multiple_of(g * part, part), part)
+    def spread(g):
+        rows = slice(g * part, (g + 1) * part)
         updated = jnp.concatenate(
-            [
-                jnp.concatenate([ref[f, rows_of, :] for f in range(frames)], axis=1)
-                for ref in message_refs
-            ],
-            axis=0,
+            [jnp.concatenate([ref[f, rows, :] for f in range(frames)], axis=1) for ref in message_refs], axis=0
         )
+        return [dot(put_ref[side], updated) for side in range(halves)]
+
+    def merge(g, spreads):
+        base = g * GROUP
         for side in range(halves):
-            spread = dot(put_ref[side], updated)
             across = slice(side * LANES, (side + 1) * LANES)
             for f in range(frames):
-                cells = hidden_ref[pl.ds(base, GROUP), f, :, across].reshape(wide, LANES).astype(jnp.float32)
-                merged = jnp.where(cover_ref[side] > 0.5, spread[:, f * LANES : (f + 1) * LANES], cells)
-                out_ref[pl.ds(base, GROUP), f, :, across] = merged.astype(jnp.bfloat16).reshape(GROUP, height, LANES)
+                cells = hidden_ref[base : base + GROUP, f, :, across].reshape(wide, LANES).astype(jnp.float32)
+                merged = jnp.where(cover_ref[side] > 0.5, spreads[side][:, f * LANES : (f + 1) * LANES], cells)
+                out_ref[base : base + GROUP, f, :, across] = merged.astype(jnp.bfloat16).reshape(GROUP, height, LANES)
         group_copy(g).start()
-        return carry
 
     groups = channels // GROUP
-    lax.fori_loop(0, groups, merge, 0, unroll=True)
+    following = spread(0)
+    for g in range(groups):
+        current = following
+        following = spread(g + 1) if g + 1 < groups else None
+        merge(g, current)
     for g in range(groups):
         group_copy(g).wait()
 
@@ -444,11 +485,11 @@
     tiles, parts = lax.axis_size("tile"), lax.axis_size("frame")
     slots = occupied.shape[1] // parts
     band = bands(conv_weight, height)
-    second, first = edge_columns(grid, band)
+    first, second = edge_columns(grid, band)
+    first = lax.ppermute(first, "tile", swaps(tiles, 0))
     second = lax.ppermute(second, "tile", swaps(tiles, 1))
-    first = lax.ppermute(first, "tile", swaps(tiles, 0))
-    summed = inner(grid, band)
-    hidden, *messages = finish(grid, band, summed, conv_bias, second, first, occupied, parts)
+    inside = inner(grid, band, conv_bias, occupied, parts)
+    hidden, *messages = finish(grid, band, *inside, first, second, parts)
     depth, mix = tables(depth_kernel, point_weight, slots, messages[0])
     updated = temporal(exchange(messages, False), depth, mix)
     put, cover = plan(occupied, counts, GROUP * height, columns // LANES, parts, updated[0])

time: 49.1 us -> 47.7 us (0.971)
  the two profiles are of different devices: /device:TPU:1 before, /device:TPU:9 now
where the time goes in v2:
time: 47.7 us; the launch traced here: 47.6 us
  starting transfers between devices  21.3 us (45%)
  Pallas kernels  13.7 us (29%)
  waiting for transfers between devices  10.9 us (23%)
  local copies, waits for them, and re-layouts  0.9 us (2%)
  between operations  0.82 us (2%)
    ppermute x14, starting transfers between devices, exchange(): lax.ppermute(array, 'frame', [(i, i ^ step[i % 2]) for i in range(count)])  16.7 us
    ppermute x14, waiting for transfers between devices, exchange(): lax.ppermute(array, 'frame', [(i, i ^ step[i % 2]) for i in range(count)])  10.9 us
    ppermute x1, starting transfers between devices, on_device(): second = lax.ppermute(second, 'tile', swaps(tiles, 1))  4.49 us
    pallas_call x1, Pallas kernels, temporal(): pl.pallas_call(functools.partial(temporal_kernel, sources), in_specs=[vme...  3.82 us
    pallas_call x1, Pallas kernels, inner(): pl.pallas_call(inner_kernel, in_specs=[smem, smem, vmem, vmem], out_shape...  2.6 us
    pallas_call x1, Pallas kernels, finish(): pl.pallas_call(finish_kernel, in_specs=[vmem] * 7, out_shape=[jax.ShapeDt...  1.84 us
    pallas_call x1, Pallas kernels, place(): pl.pallas_call(functools.partial(place_kernel, sources), in_specs=[vmem,...  1.62 us
    pallas_call x1, Pallas kernels, bands(): pl.pallas_call(functools.partial(bands_kernel, height), out_shape=jax.Sha...  1.33 us
  transfers between devices with their start and end apart: 16, of which 7 were waited for; matrix products, arithmetic and copies ran while one was open for 0% of the time, Pallas kernels for 9%

profile of v2, /device:TPU:9, one launch (start us, length us, event | category | flops | bytes accessed | tf_op | source)
XLA Modules:
  0.0 47.6 jit_solution(7432111195869001265)
XLA Ops:
  0.0 0.9 %copy-done.1 = bf16[9,64,8]{1,2,0:T(8,128)(2,1)S(1)} copy-done((bf16[9,64,8]{1,2,0:T(8,128)(2,1)S(1)}, bf16[9,64,8]{1,2,0:T(8,128)(2,1)}, u32[]{:S(2)}) %copy-start.1) | copy-done | bytes 9240
  0.9 1.3 %bands.1.band_ref._ = bf16[8,256,768]{2,1,0:T(8,128)(2,1)S(1)} custom-call(bf16[9,8,64]{2,1,0:T(8,128)(2,1)S(1)} %bitcast.2), custom_call_target="tpu_custom_call" | custom-call | flops 268435456 | bytes 8388608 | tf_op jit(solution)/shard_map/bands/pallas_call | solution.py:100
  2.2 0.7 %edge_columns.1 = (bf16[16,256]{1,0:T(8,128)(2,1)S(1)}, bf16[16,256]{1,0:T(8,128)(2,1)S(1)}) custom-call(bf16[64,2,32,256]{3,2,1,0:T(8,128)(2,1)S(1)} %copy-done, bf16[8,256,768]{2,1,0:T(8,128)(2,1)S(1)} %bands.1.band_ref._), custom_call_target="tpu_custom_call" | custom-call | flops 268435456 | bytes 2097152 | tf_op jit(solution)/shard_map/edge_columns/pallas_call | solution.py:61
  3.0 4.5 %collective-permute-start.1 = (bf16[16,256]{1,0:T(8,128)(2,1)S(1)}, bf16[16,256]{1,0:T(8,128)(2,1)S(1)}, u32[]{:S(2)}, u32[]{:S(2)}) collective-permute-start(bf16[16,256]{1,0:T(8,128)(2,1)S(1)} %get-tuple-element.37), channel_id=1, source_target_pairs={{0,0},{1,2},{2,1},{3,3},{4,4},{5,6},{6,5},{7,7},{8,8},{9,10},{10,9... | collective-permute-start | bytes 24584 | tf_op jit(solution)/shard_map/ppermute | solution.py:490
  7.5 2.6 %inner.1 = (f32[8,2,256,256]{3,2,1,0:T(8,128)S(1)}, f32[8,2,256,256]{3,2,1,0:T(8,128)S(1)}, bf16[256,256]{1,0:T(8,128)(2,1)S(1)}, s32[256,128]{1,0:T(8,128)S(1)}) custom-call(s32[1,32]{1,0:T(1,128)S(1)} %copy-done.5, f32[64]{0:T(128)S(1)} %copy-done.4, bf16[64,2,32,256]{3,2,1,0:T(8,128)(2,1)S(1)} %copy-done, bf16[8,256,768]{2,1,0:T(8,128)(2,1)S(1)} %bands.1.band_ref._), custom_call_target="tpu_custom_call" | custom-call | flops 2147483648 | bytes 8388608 | tf_op jit(solution)/shard_map/inner/pallas_call | solution.py:160
  10.1 1.8 %finish.1 = (bf16[64,2,32,256]{3,2,1,0:T(8,128)(2,1)S(1)}, bf16[2,256,128]{2,1,0:T(8,128)(2,1)S(1)}, bf16[2,256,128]{2,1,0:T(8,128)(2,1)S(1)}, bf16[2,256,128]{2...) custom-call(bf16[8,256,768]{2,1,0:T(8,128)(2,1)S(1)} %bands.1.band_r, ...), custom_call_target="tpu_custom_call" | custom-call | flops 1073741824 | bytes 8388608 | tf_op jit(solution)/shard_map/finish/pallas_call | solution.py:260
  12.0 1.3 %collective-permute-start.2 = (bf16[2,256,128]{2,1,0:T(8,128)(2,1)S(1)}, bf16[2,256,128]{2,1,0:T(8,128)(2,1)S(1)}, u32[]{:S(2)}, u32[]{:S(2)}) collective-permute-start(bf16[2,256,128]{2,1,0:T(8,128)(2,1)S(1)} %get-tuple-element.41), channel_id=1, source_target_pairs={{0,16},{4,12},{8,24},{12,4},{16,0},{20,28},{24,8},{28,20},{1,17},{... | collective-permute-start | bytes 393224 | tf_op jit(solution)/shard_map/ppermute | solution.py:478
  13.3 1.2 %collective-permute-start.3 = (bf16[2,256,128]{2,1,0:T(8,128)(2,1)S(1)}, bf16[2,256,128]{2,1,0:T(8,128)(2,1)S(1)}, u32[]{:S(2)}, u32[]{:S(2)}) collective-permute-start(bf16[2,256,128]{2,1,0:T(8,128)(2,1)S(1)} %get-tuple-element.42), channel_id=1, source_target_pairs={{0,8},{4,20},{8,0},{12,28},{16,24},{20,4},{24,16},{28,12},{1,9},{5... | collective-permute-start | bytes 393224 | tf_op jit(solution)/shard_map/ppermute | solution.py:478
  14.5 1.9 %collective-permute-start.4 = (bf16[2,256,128]{2,1,0:T(8,128)(2,1)S(1)}, bf16[2,256,128]{2,1,0:T(8,128)(2,1)S(1)}, u32[]{:S(2)}, u32[]{:S(2)}) collective-permute-start(bf16[2,256,128]{2,1,0:T(8,128)(2,1)S(1)} %get-tuple-element.43), channel_id=1, source_target_pairs={{0,20},{4,8},{8,28},{12,0},{16,4},{20,24},{24,12},{28,16},{1,21},{... | collective-permute-start | bytes 393224 | tf_op jit(solution)/shard_map/ppermute | solution.py:478
  16.4 1.2 %collective-permute-start.6 = (bf16[2,256,128]{2,1,0:T(8,128)(2,1)S(1)}, bf16[2,256,128]{2,1,0:T(8,128)(2,1)S(1)}, u32[]{:S(2)}, u32[]{:S(2)}) collective-permute-start(bf16[2,256,128]{2,1,0:T(8,128)(2,1)S(1)} %get-tuple-element.45), channel_id=1, source_target_pairs={{0,24},{4,28},{8,16},{12,20},{16,8},{20,12},{24,0},{28,4},{1,25},{... | collective-permute-start | bytes 393224 | tf_op jit(solution)/shard_map/ppermute | solution.py:478
  17.6 3.0 %collective-permute-start.7 = (bf16[2,256,128]{2,1,0:T(8,128)(2,1)S(1)}, bf16[2,256,128]{2,1,0:T(8,128)(2,1)S(1)}, u32[]{:S(2)}, u32[]{:S(2)}) collective-permute-start(bf16[2,256,128]{2,1,0:T(8,128)(2,1)S(1)} %get-tuple-element.46), channel_id=1, source_target_pairs={{0,28},{4,24},{8,20},{12,16},{16,12},{20,8},{24,4},{28,0},{1,29},{... | collective-permute-start | bytes 393224 | tf_op jit(solution)/shard_map/ppermute | solution.py:478
  21.4 1.3 %collective-permute-done.5.refs_4_ = bf16[2,256,128]{2,1,0:T(8,128)(2,1)S(1)} collective-permute-done((bf16[2,256,128]{2,1,0:T(8,128)(2,1)S(1)}, bf16[2,256,128]{2,1,0:T(8,128)(2,1)S(1)}, u32[]{:S(2)}, u32[]{:S(2)}) %collective-permute-start.5) | collective-permute-done | bytes 131104 | tf_op jit(solution)/shard_map/ppermute | solution.py:478
  22.7 1.8 %collective-permute-done.6.refs_5_ = bf16[2,256,128]{2,1,0:T(8,128)(2,1)S(1)} collective-permute-done((bf16[2,256,128]{2,1,0:T(8,128)(2,1)S(1)}, bf16[2,256,128]{2,1,0:T(8,128)(2,1)S(1)}, u32[]{:S(2)}, u32[]{:S(2)}) %collective-permute-start.6) | collective-permute-done | bytes 131104 | tf_op jit(solution)/shard_map/ppermute | solution.py:478
  24.4 3.0 %collective-permute-done.7.refs_6_ = bf16[2,256,128]{2,1,0:T(8,128)(2,1)S(1)} collective-permute-done((bf16[2,256,128]{2,1,0:T(8,128)(2,1)S(1)}, bf16[2,256,128]{2,1,0:T(8,128)(2,1)S(1)}, u32[]{:S(2)}, u32[]{:S(2)}) %collective-permute-start.7) | collective-permute-done | bytes 131104 | tf_op jit(solution)/shard_map/ppermute | solution.py:478
  27.4 3.8 %temporal.1 = (bf16[2,256,128]{2,1,0:T(8,128)(2,1)S(1)}, bf16[2,256,128]{2,1,0:T(8,128)(2,1)S(1)}, bf16[2,256,128]{2,1,0:T(8,128)(2,1)S(1)}, bf16[2,256,128]{2,1...) custom-call(f32[12,256,128]{2,1,0:T(8,128)S(1)} %get-tuple-element.3, ...), custom_call_target="tpu_custom_call" | custom-call | flops 1073741824 | bytes 2097152 | tf_op jit(solution)/shard_map/temporal/pallas_call | solution.py:365
  31.3 1.2 %collective-permute-start.10 = (bf16[2,256,128]{2,1,0:T(8,128)(2,1)S(1)}, bf16[2,256,128]{2,1,0:T(8,128)(2,1)S(1)}, u32[]{:S(2)}, u32[]{:S(2)}) collective-permute-start(bf16[2,256,128]{2,1,0:T(8,128)(2,1)S(1)} %get-tuple-element.53), channel_id=1, source_target_pairs={{0,16},{4,12},{8,24},{12,4},{16,0},{20,28},{24,8},{28,20},{1,17},{... | collective-permute-start | bytes 393224 | tf_op jit(solution)/shard_map/ppermute | solution.py:478
  32.5 1.2 %collective-permute-start.11 = (bf16[2,256,128]{2,1,0:T(8,128)(2,1)S(1)}, bf16[2,256,128]{2,1,0:T(8,128)(2,1)S(1)}, u32[]{:S(2)}, u32[]{:S(2)}) collective-permute-start(bf16[2,256,128]{2,1,0:T(8,128)(2,1)S(1)} %get-tuple-element.54), channel_id=1, source_target_pairs={{0,8},{4,20},{8,0},{12,28},{16,24},{20,4},{24,16},{28,12},{1,9},{5... | collective-permute-start | bytes 393224 | tf_op jit(solution)/shard_map/ppermute | solution.py:478
  33.8 0.9 %collective-permute-start.12 = (bf16[2,256,128]{2,1,0:T(8,128)(2,1)S(1)}, bf16[2,256,128]{2,1,0:T(8,128)(2,1)S(1)}, u32[]{:S(2)}, u32[]{:S(2)}) collective-permute-start(bf16[2,256,128]{2,1,0:T(8,128)(2,1)S(1)} %get-tuple-element.55), channel_id=1, source_target_pairs={{0,20},{4,8},{8,28},{12,0},{16,4},{20,24},{24,12},{28,16},{1,21},{... | collective-permute-start | bytes 393224 | tf_op jit(solution)/shard_map/ppermute | solution.py:478
  34.7 0.8 %collective-permute-start.13 = (bf16[2,256,128]{2,1,0:T(8,128)(2,1)S(1)}, bf16[2,256,128]{2,1,0:T(8,128)(2,1)S(1)}, u32[]{:S(2)}, u32[]{:S(2)}) collective-permute-start(bf16[2,256,128]{2,1,0:T(8,128)(2,1)S(1)} %get-tuple-element.56), channel_id=1, source_target_pairs={{0,12},{4,16},{8,4},{12,24},{16,28},{20,0},{24,20},{28,8},{1,13},{... | collective-permute-start | bytes 393224 | tf_op jit(solution)/shard_map/ppermute | solution.py:478
  35.9 2.7 %collective-permute-start.15 = (bf16[2,256,128]{2,1,0:T(8,128)(2,1)S(1)}, bf16[2,256,128]{2,1,0:T(8,128)(2,1)S(1)}, u32[]{:S(2)}, u32[]{:S(2)}) collective-permute-start(bf16[2,256,128]{2,1,0:T(8,128)(2,1)S(1)} %get-tuple-element.58), channel_id=1, source_target_pairs={{0,28},{4,24},{8,20},{12,16},{16,12},{20,8},{24,4},{28,0},{1,29},{... | collective-permute-start | bytes 393224 | tf_op jit(solution)/shard_map/ppermute | solution.py:478
  38.5 0.9 %collective-permute-start.9 = (bf16[2,256,128]{2,1,0:T(8,128)(2,1)S(1)}, bf16[2,256,128]{2,1,0:T(8,128)(2,1)S(1)}, u32[]{:S(2)}, u32[]{:S(2)}) collective-permute-start(bf16[2,256,128]{2,1,0:T(8,128)(2,1)S(1)} %get-tuple-element.52), channel_id=1, source_target_pairs={{0,4},{4,0},{8,12},{12,8},{16,20},{20,16},{24,28},{28,24},{1,5},{5... | collective-permute-start | bytes 393224 | tf_op jit(solution)/shard_map/ppermute | solution.py:478
  40.1 1.3 %plan.1 = (bf16[2,256,256]{2,1,0:T(8,128)(2,1)S(1)}, f32[2,256,128]{2,1,0:T(8,128)S(1)}) custom-call(s32[1,32]{1,0:T(1,128)S(1)} %copy-done.5, s32[1]{0:T(128)S(6)} %copy.8.counts_ref, bf16[2,256,128]{2,1,0:T(8,128)(2,1)S(1)} %get-tuple-element.48._.refs_0_), custom_call_target="tpu_custom_call" | custom-call | flops 134217728 | bytes 4194304 | tf_op jit(solution)/shard_map/plan/pallas_call | solution.py:405
  42.3 3.7 %collective-permute-done.15.refs_7_ = bf16[2,256,128]{2,1,0:T(8,128)(2,1)S(1)} collective-permute-done((bf16[2,256,128]{2,1,0:T(8,128)(2,1)S(1)}, bf16[2,256,128]{2,1,0:T(8,128)(2,1)S(1)}, u32[]{:S(2)}, u32[]{:S(2)}) %collective-permute-start.15) | collective-permute-done | bytes 131104 | tf_op jit(solution)/shard_map/ppermute | solution.py:478
  46.0 1.6 %place.1 = bf16[64,2,32,256]{3,2,1,0:T(8,128)(2,1)} custom-call(bf16[2,256,256]{2,1,0:T(8,128)(2,1)S(1)} %get-tuple-element.49.put_ref, f32[2,256,128]{2,1,0:T(8,128)S(1)} %get-tuple-element.50.cover_ref, bf16[64,2,32,256]{3,2,1,0:T(8,128)(2,1)S(1)} %get-tuple-element.51.hidden_ref, bf16[2,256,128]{2,1,0:T(8,128)(2,1)S(1)} %get-tuple-element.48._.refs_0_, ...), custom_call_target="tpu_custom_call" | custom-call | flops 268435456 | bytes 4194304 | tf_op jit(solution)/shard_map/place/pallas_call | solution.py:460
  (28 shorter events, 2.1 us)
Async XLA Ops:
  0.0 2.2 %copy-start = (bf16[64,2,32,256]{3,2,1,0:T(8,128)(2,1)S(1)}, bf16[64,2,32,256]{3,2,1,0:T(8,128)(2,1)}, u32[]{:S(2)}) copy-start(bf16[64,2,32,256]{3,2,1,0:T(8,128)(2,1)} %grid_ref.3) | copy-start | bytes 6291460
  0.0 0.9 %copy-start.1 = (bf16[9,64,8]{1,2,0:T(8,128)(2,1)S(1)}, bf16[9,64,8]{1,2,0:T(8,128)(2,1)}, u32[]{:S(2)}) copy-start(bf16[9,64,8]{1,2,0:T(8,128)(2,1)} %param.8) | copy-start | bytes 27652
  2.2 5.3 %copy-start.4 = (f32[64]{0:T(128)S(1)}, f32[64]{0:T(128)}, u32[]{:S(2)}) copy-start(f32[64]{0:T(128)} %bias_ref.1) | copy-start | bytes 772
  2.2 5.3 %copy-start.5 = (s32[1,32]{1,0:T(1,128)S(1)}, s32[1,32]{1,0:T(1,128)}, u32[]{:S(2)}) copy-start(s32[1,32]{1,0:T(1,128)} %occupied_ref.3) | copy-start | bytes 388
  2.9 7.2 %collective-permute-start = (bf16[16,256]{1,0:T(8,128)(2,1)S(1)}, bf16[16,256]{1,0:T(8,128)(2,1)S(1)}, u32[]{:S(2)}, u32[]{:S(2)}) collective-permute-start(bf16[16,256]{1,0:T(8,128)(2,1)S(1)} %get-tuple-element.36), channel_id=1, source_target_pairs={{0,1},{1,0},{2,3},{3,2},{4,5},{5,4},{6,7},{7,6},{8,9},{9,8},{10,11... | collective-permute-start | bytes 24584 | tf_op jit(solution)/shard_map/ppermute | solution.py:489
  3.0 7.1 %collective-permute-start.1 = (bf16[16,256]{1,0:T(8,128)(2,1)S(1)}, bf16[16,256]{1,0:T(8,128)(2,1)S(1)}, u32[]{:S(2)}, u32[]{:S(2)}) collective-permute-start(bf16[16,256]{1,0:T(8,128)(2,1)S(1)} %get-tuple-element.37), channel_id=1, source_target_pairs={{0,0},{1,2},{2,1},{3,3},{4,4},{5,6},{6,5},{7,7},{8,8},{9,10},{10,9... | collective-permute-start | bytes 24584 | tf_op jit(solution)/shard_map/ppermute | solution.py:490
  10.1 10.5 %copy-start.2 = (bf16[4,64,64]{2,1,0:T(8,128)(2,1)S(1)}, bf16[4,64,64]{2,1,0:T(8,128)(2,1)}, u32[]{:S(2)}) copy-start(bf16[4,64,64]{2,1,0:T(8,128)(2,1)} %point_ref.1) | copy-start | bytes 98308
  10.1 10.5 %copy-start.3 = (f32[4,3,64]{2,0,1:T(4,128)S(1)}, f32[4,3,64]{2,0,1:T(4,128)}, u32[]{:S(2)}) copy-start(f32[4,3,64]{2,0,1:T(4,128)} %param.10) | copy-start | bytes 9220
  12.0 5.6 %collective-permute-start.2 = (bf16[2,256,128]{2,1,0:T(8,128)(2,1)S(1)}, bf16[2,256,128]{2,1,0:T(8,128)(2,1)S(1)}, u32[]{:S(2)}, u32[]{:S(2)}) collective-permute-start(bf16[2,256,128]{2,1,0:T(8,128)(2,1)S(1)} %get-tuple-element.41), channel_id=1, source_target_pairs={{0,16},{4,12},{8,24},{12,4},{16,0},{20,28},{24,8},{28,20},{1,17},{... | collective-permute-start | bytes 393224 | tf_op jit(solution)/shard_map/ppermute | solution.py:478
  13.3 7.3 %collective-permute-start.3 = (bf16[2,256,128]{2,1,0:T(8,128)(2,1)S(1)}, bf16[2,256,128]{2,1,0:T(8,128)(2,1)S(1)}, u32[]{:S(2)}, u32[]{:S(2)}) collective-permute-start(bf16[2,256,128]{2,1,0:T(8,128)(2,1)S(1)} %get-tuple-element.42), channel_id=1, source_target_pairs={{0,8},{4,20},{8,0},{12,28},{16,24},{20,4},{24,16},{28,12},{1,9},{5... | collective-permute-start | bytes 393224 | tf_op jit(solution)/shard_map/ppermute | solution.py:478
  14.5 6.9 %collective-permute-start.4 = (bf16[2,256,128]{2,1,0:T(8,128)(2,1)S(1)}, bf16[2,256,128]{2,1,0:T(8,128)(2,1)S(1)}, u32[]{:S(2)}, u32[]{:S(2)}) collective-permute-start(bf16[2,256,128]{2,1,0:T(8,128)(2,1)S(1)} %get-tuple-element.43), channel_id=1, source_target_pairs={{0,20},{4,8},{8,28},{12,0},{16,4},{20,24},{24,12},{28,16},{1,21},{... | collective-permute-start | bytes 393224 | tf_op jit(solution)/shard_map/ppermute | solution.py:478
  16.4 6.2 %collective-permute-start.5 = (bf16[2,256,128]{2,1,0:T(8,128)(2,1)S(1)}, bf16[2,256,128]{2,1,0:T(8,128)(2,1)S(1)}, u32[]{:S(2)}, u32[]{:S(2)}) collective-permute-start(bf16[2,256,128]{2,1,0:T(8,128)(2,1)S(1)} %get-tuple-element.44), channel_id=1, source_target_pairs={{0,12},{4,16},{8,4},{12,24},{16,28},{20,0},{24,20},{28,8},{1,13},{... | collective-permute-start | bytes 393224 | tf_op jit(solution)/shard_map/ppermute | solution.py:478
  16.4 8.0 %collective-permute-start.6 = (bf16[2,256,128]{2,1,0:T(8,128)(2,1)S(1)}, bf16[2,256,128]{2,1,0:T(8,128)(2,1)S(1)}, u32[]{:S(2)}, u32[]{:S(2)}) collective-permute-start(bf16[2,256,128]{2,1,0:T(8,128)(2,1)S(1)} %get-tuple-element.45), channel_id=1, source_target_pairs={{0,24},{4,28},{8,16},{12,20},{16,8},{20,12},{24,0},{28,4},{1,25},{... | collective-permute-start | bytes 393224 | tf_op jit(solution)/shard_map/ppermute | solution.py:478
  17.6 9.8 %collective-permute-start.7 = (bf16[2,256,128]{2,1,0:T(8,128)(2,1)S(1)}, bf16[2,256,128]{2,1,0:T(8,128)(2,1)S(1)}, u32[]{:S(2)}, u32[]{:S(2)}) collective-permute-start(bf16[2,256,128]{2,1,0:T(8,128)(2,1)S(1)} %get-tuple-element.46), channel_id=1, source_target_pairs={{0,28},{4,24},{8,20},{12,16},{16,12},{20,8},{24,4},{28,0},{1,29},{... | collective-permute-start | bytes 393224 | tf_op jit(solution)/shard_map/ppermute | solution.py:478
  20.6 6.9 %collective-permute-start.8 = (bf16[2,256,128]{2,1,0:T(8,128)(2,1)S(1)}, bf16[2,256,128]{2,1,0:T(8,128)(2,1)S(1)}, u32[]{:S(2)}, u32[]{:S(2)}) collective-permute-start(bf16[2,256,128]{2,1,0:T(8,128)(2,1)S(1)} %get-tuple-element.47), channel_id=1, source_target_pairs={{0,4},{4,0},{8,12},{12,8},{16,20},{20,16},{24,28},{28,24},{1,5},{5... | collective-permute-start | bytes 393224 | tf_op jit(solution)/shard_map/ppermute | solution.py:478
  31.3 4.6 %collective-permute-start.10 = (bf16[2,256,128]{2,1,0:T(8,128)(2,1)S(1)}, bf16[2,256,128]{2,1,0:T(8,128)(2,1)S(1)}, u32[]{:S(2)}, u32[]{:S(2)}) collective-permute-start(bf16[2,256,128]{2,1,0:T(8,128)(2,1)S(1)} %get-tuple-element.53), channel_id=1, source_target_pairs={{0,16},{4,12},{8,24},{12,4},{16,0},{20,28},{24,8},{28,20},{1,17},{... | collective-permute-start | bytes 393224 | tf_op jit(solution)/shard_map/ppermute | solution.py:478
  32.5 6.0 %collective-permute-start.11 = (bf16[2,256,128]{2,1,0:T(8,128)(2,1)S(1)}, bf16[2,256,128]{2,1,0:T(8,128)(2,1)S(1)}, u32[]{:S(2)}, u32[]{:S(2)}) collective-permute-start(bf16[2,256,128]{2,1,0:T(8,128)(2,1)S(1)} %get-tuple-element.54), channel_id=1, source_target_pairs={{0,8},{4,20},{8,0},{12,28},{16,24},{20,4},{24,16},{28,12},{1,9},{5... | collective-permute-start | bytes 393224 | tf_op jit(solution)/shard_map/ppermute | solution.py:478
  33.8 7.6 %collective-permute-start.12 = (bf16[2,256,128]{2,1,0:T(8,128)(2,1)S(1)}, bf16[2,256,128]{2,1,0:T(8,128)(2,1)S(1)}, u32[]{:S(2)}, u32[]{:S(2)}) collective-permute-start(bf16[2,256,128]{2,1,0:T(8,128)(2,1)S(1)} %get-tuple-element.55), channel_id=1, source_target_pairs={{0,20},{4,8},{8,28},{12,0},{16,4},{20,24},{24,12},{28,16},{1,21},{... | collective-permute-start | bytes 393224 | tf_op jit(solution)/shard_map/ppermute | solution.py:478
  34.7 7.2 %collective-permute-start.13 = (bf16[2,256,128]{2,1,0:T(8,128)(2,1)S(1)}, bf16[2,256,128]{2,1,0:T(8,128)(2,1)S(1)}, u32[]{:S(2)}, u32[]{:S(2)}) collective-permute-start(bf16[2,256,128]{2,1,0:T(8,128)(2,1)S(1)} %get-tuple-element.56), channel_id=1, source_target_pairs={{0,12},{4,16},{8,4},{12,24},{16,28},{20,0},{24,20},{28,8},{1,13},{... | collective-permute-start | bytes 393224 | tf_op jit(solution)/shard_map/ppermute | solution.py:478
  35.5 6.8 %collective-permute-start.14 = (bf16[2,256,128]{2,1,0:T(8,128)(2,1)S(1)}, bf16[2,256,128]{2,1,0:T(8,128)(2,1)S(1)}, u32[]{:S(2)}, u32[]{:S(2)}) collective-permute-start(bf16[2,256,128]{2,1,0:T(8,128)(2,1)S(1)} %get-tuple-element.57), channel_id=1, source_target_pairs={{0,24},{4,28},{8,16},{12,20},{16,8},{20,12},{24,0},{28,4},{1,25},{... | collective-permute-start | bytes 393224 | tf_op jit(solution)/shard_map/ppermute | solution.py:478
  35.9 10.1 %collective-permute-start.15 = (bf16[2,256,128]{2,1,0:T(8,128)(2,1)S(1)}, bf16[2,256,128]{2,1,0:T(8,128)(2,1)S(1)}, u32[]{:S(2)}, u32[]{:S(2)}) collective-permute-start(bf16[2,256,128]{2,1,0:T(8,128)(2,1)S(1)} %get-tuple-element.58), channel_id=1, source_target_pairs={{0,28},{4,24},{8,20},{12,16},{16,12},{20,8},{24,4},{28,0},{1,29},{... | collective-permute-start | bytes 393224 | tf_op jit(solution)/shard_map/ppermute | solution.py:478
  38.5 7.4 %collective-permute-start.9 = (bf16[2,256,128]{2,1,0:T(8,128)(2,1)S(1)}, bf16[2,256,128]{2,1,0:T(8,128)(2,1)S(1)}, u32[]{:S(2)}, u32[]{:S(2)}) collective-permute-start(bf16[2,256,128]{2,1,0:T(8,128)(2,1)S(1)} %get-tuple-element.52), channel_id=1, source_target_pairs={{0,4},{4,0},{8,12},{12,8},{16,20},{20,16},{24,28},{28,24},{1,5},{5... | collective-permute-start | bytes 393224 | tf_op jit(solution)/shard_map/ppermute | solution.py:478

commit v3 on v2

--- a/solution.py
+++ b/solution.py
@@ -10,7 +10,6 @@
 GROUP = 8
 LANES = 128
 MIB = 2**20
-ROLLED = jnp.bfloat16
 
 
 def params(mib):
@@ -29,23 +28,23 @@
     return lax.broadcasted_iota(jnp.int32, shape, dim)
 
 
-def edges_kernel(grid_ref, _, first_ref, second_ref):
+def edges_kernel(grid_ref, _, first_ref, second_ref, found):
     channels, frames, height, columns = grid_ref.shape
     groups, wide = channels // GROUP, GROUP * height
     count = groups * frames
-    rows = iota((2 * count, columns), 0)
-    lanes = iota((2 * count, columns), 1)
     even = lax.axis_index("tile") % 2 == 0
     ahead, behind = jnp.where(even, columns - 1, 0), jnp.where(even, 0, columns - 1)
-    total = jnp.zeros((2 * count, wide), jnp.float32)
+    rows, lanes = iota((16, columns), 0), iota((16, columns), 1)
+    pick = (((rows == 0) & (lanes == ahead)) | ((rows == 1) & (lanes == behind))).astype(jnp.bfloat16)
     for g in range(groups):
         for f in range(frames):
             at = g * frames + f
-            pick = ((rows == at) & (lanes == ahead)) | ((rows == count + at) & (lanes == behind))
             cells = grid_ref[g * GROUP : (g + 1) * GROUP, f].reshape(wide, columns)
-            total += dot(pick.astype(jnp.bfloat16), cells, ((1,), (1,)))
-    first_ref[...] = total[:count].astype(jnp.bfloat16)
-    second_ref[...] = total[count:].astype(jnp.bfloat16)
+            both = dot(pick, cells, ((1,), (1,)))
+            found[at : at + 1, :] = both[0:1]
+            found[count + at : count + at + 1, :] = both[1:2]
+    first_ref[...] = found[:count].astype(jnp.bfloat16)
+    second_ref[...] = found[count:].astype(jnp.bfloat16)
 
 
 def swaps(count, start):
@@ -62,6 +61,7 @@
         edges_kernel,
         in_specs=[pl.BlockSpec(memory_space=pltpu.VMEM), pl.BlockSpec(memory_space=pl.ANY)],
         out_shape=(shape, shape),
+        scratch_shapes=[pltpu.VMEM((2 * shape.shape[0], shape.shape[1]), jnp.float32)],
         compiler_params=params(8),
         cost_estimate=pl.CostEstimate(flops=2**28, bytes_accessed=2**21, transcendentals=0),
         name="edge_columns",
@@ -70,7 +70,7 @@
 
 def bands_kernel(height, taps_ref, band_ref, spread):
     _, inner, channels = taps_ref.shape
-    groups, wide = channels // GROUP, GROUP * height
+    wide = GROUP * height
     repeat = (iota((inner, wide), 0) == iota((inner, wide), 1) // height).astype(jnp.bfloat16)
     offset = iota((height, wide), 1) % height - iota((height, wide), 0)
     masks = [offset == row - 1 for row in range(3)]
@@ -78,19 +78,13 @@
         half = (taps_ref[tap].astype(jnp.float32) * 0.5).astype(jnp.bfloat16)
         spread[tap] = dot(half, repeat, ((0,), (0,)))
 
-    def band(g, carry):
+    for c in range(channels):
+        out = c % GROUP * height
         for col in range(3):
-            rows = [spread[3 * row + col, pl.ds(pl.multiple_of(g * GROUP, GROUP), GROUP), :] for row in range(3)]
-            for out in range(GROUP):
-                value = jnp.zeros((height, wide), jnp.float32)
-                for row in range(3):
-                    value = jnp.where(masks[row], rows[row][out : out + 1], value)
-                band_ref[g, out * height : (out + 1) * height, col * wide : (col + 1) * wide] = value.astype(
-                    jnp.bfloat16
-                )
-        return carry
-
-    lax.fori_loop(0, groups, band, 0)
+            value = jnp.zeros((height, wide), jnp.float32)
+            for row in range(3):
+                value = jnp.where(masks[row], spread[3 * row + col, c : c + 1, :], value)
+            band_ref[c // GROUP, out : out + height, col * wide : (col + 1) * wide] = value.astype(jnp.bfloat16)
 
 
 def bands(conv_weight, height):
@@ -128,17 +122,19 @@
 
     tile_lanes = iota((wide, LANES), 1)
     is_first, is_last = tile_lanes == 0, tile_lanes == LANES - 1
-    nothing = jnp.zeros((wide, LANES), ROLLED)
+    nothing = jnp.zeros((wide, LANES), jnp.float32)
 
     def shifted(g, f):
         cells = grid_ref[g * GROUP : (g + 1) * GROUP, f].reshape(wide, columns)
-        tiles = [cells[:, side * LANES : (side + 1) * LANES].astype(ROLLED) for side in range(halves)]
+        full = cells.astype(jnp.float32)
+        cells_ref[g, f] = full
+        tiles = [full[:, side * LANES : (side + 1) * LANES] for side in range(halves)]
         right = [pltpu.roll(tile, 1, 1) for tile in tiles]
         left = [pltpu.roll(tile, LANES - 1, 1) for tile in tiles]
         before = [jnp.where(is_first, *pair) for pair in zip([nothing] + right[:-1], right)]
         after = [jnp.where(is_last, *pair) for pair in zip(left[1:] + [nothing], left)]
-        join = lambda parts: jnp.concatenate(parts, axis=1).astype(jnp.bfloat16)
-        return jnp.concatenate([join(before), cells, join(after)], axis=0)
+        before, after = (jnp.concatenate(parts, axis=1).astype(jnp.bfloat16) for parts in (before, after))
+        return jnp.concatenate([before, cells, after], axis=0)
 
     items = [(g, f) for g in range(channels // GROUP) for f in range(frames)]
     ready = shifted(*items[0])
@@ -149,7 +145,6 @@
         for out in range(GROUP):
             inside = slice(out * height, (out + 1) * height)
             summed_ref[g, f, inside, :] = summed[inside] + 0.5 * bias_ref[g * GROUP + out]
-            cells_ref[g, f, inside, :] = grid_ref[g * GROUP + out, f].astype(jnp.float32)
 
 
 def inner(grid, band, conv_bias, occupied, parts):

time: 47.7 us -> 47.9 us (level)
  transfers between devices with their start and end apart: 16 -> 16, of which waited for: 7 -> 7; matrix products, arithmetic and copies ran while one was open for 0% -> 0% of each run, Pallas kernels for 9% -> 10%
where the time goes in v3:
time: 47.9 us; the launch traced here: 47.8 us
  starting transfers between devices  21.3 us (44%)
  Pallas kernels  13.9 us (29%)
  waiting for transfers between devices  10.9 us (23%)
  local copies, waits for them, and re-layouts  0.9 us (2%)
  between operations  0.82 us (2%)
    ppermute x14, starting transfers between devices, exchange(): lax.ppermute(array, 'frame', [(i, i ^ step[i % 2]) for i in range(count)])  16.7 us
    ppermute x14, waiting for transfers between devices, exchange(): lax.ppermute(array, 'frame', [(i, i ^ step[i % 2]) for i in range(count)])  10.9 us
    ppermute x1, starting transfers between devices, on_device(): second = lax.ppermute(second, 'tile', swaps(tiles, 1))  4.48 us
    pallas_call x1, Pallas kernels, temporal(): pl.pallas_call(functools.partial(temporal_kernel, sources), in_specs=[vme...  3.82 us
    pallas_call x1, Pallas kernels, inner(): pl.pallas_call(inner_kernel, in_specs=[smem, smem, vmem, vmem], out_shape...  2.75 us
    pallas_call x1, Pallas kernels, finish(): pl.pallas_call(finish_kernel, in_specs=[vmem] * 7, out_shape=[jax.ShapeDt...  1.84 us
    pallas_call x1, Pallas kernels, place(): pl.pallas_call(functools.partial(place_kernel, sources), in_specs=[vmem,...  1.62 us
    pallas_call x1, Pallas kernels, bands(): pl.pallas_call(functools.partial(bands_kernel, height), out_shape=jax.Sha...  1.38 us
  transfers between devices with their start and end apart: 16, of which 7 were waited for; matrix products, arithmetic and copies ran while one was open for 0% of the time, Pallas kernels for 10%

profile of v3, /device:TPU:9, one launch (start us, length us, event | category | flops | bytes accessed | tf_op | source)
XLA Modules:
  0.0 47.8 jit_solution(18095422062802531412)
XLA Ops:
  0.0 0.9 %copy-done.1 = bf16[9,64,8]{1,2,0:T(8,128)(2,1)S(1)} copy-done((bf16[9,64,8]{1,2,0:T(8,128)(2,1)S(1)}, bf16[9,64,8]{1,2,0:T(8,128)(2,1)}, u32[]{:S(2)}) %copy-start.1) | copy-done | bytes 9240
  0.9 1.4 %bands.1.band_ref._ = bf16[8,256,768]{2,1,0:T(8,128)(2,1)S(1)} custom-call(bf16[9,8,64]{2,1,0:T(8,128)(2,1)S(1)} %bitcast.2), custom_call_target="tpu_custom_call" | custom-call | flops 268435456 | bytes 8388608 | tf_op jit(solution)/shard_map/bands/pallas_call | solution.py:94
  2.3 0.7 %edge_columns.1 = (bf16[16,256]{1,0:T(8,128)(2,1)S(1)}, bf16[16,256]{1,0:T(8,128)(2,1)S(1)}) custom-call(bf16[64,2,32,256]{3,2,1,0:T(8,128)(2,1)S(1)} %copy-done, bf16[8,256,768]{2,1,0:T(8,128)(2,1)S(1)} %bands.1.band_ref._), custom_call_target="tpu_custom_call" | custom-call | flops 268435456 | bytes 2097152 | tf_op jit(solution)/shard_map/edge_columns/pallas_call | solution.py:60
  3.0 4.5 %collective-permute-start.1 = (bf16[16,256]{1,0:T(8,128)(2,1)S(1)}, bf16[16,256]{1,0:T(8,128)(2,1)S(1)}, u32[]{:S(2)}, u32[]{:S(2)}) collective-permute-start(bf16[16,256]{1,0:T(8,128)(2,1)S(1)} %get-tuple-element.37), channel_id=1, source_target_pairs={{0,0},{1,2},{2,1},{3,3},{4,4},{5,6},{6,5},{7,7},{8,8},{9,10},{10,9... | collective-permute-start | bytes 24584 | tf_op jit(solution)/shard_map/ppermute | solution.py:485
  7.5 2.7 %inner.1 = (f32[8,2,256,256]{3,2,1,0:T(8,128)S(1)}, f32[8,2,256,256]{3,2,1,0:T(8,128)S(1)}, bf16[256,256]{1,0:T(8,128)(2,1)S(1)}, s32[256,128]{1,0:T(8,128)S(1)}) custom-call(s32[1,32]{1,0:T(1,128)S(1)} %copy-done.5, f32[64]{0:T(128)S(1)} %copy-done.4, bf16[64,2,32,256]{3,2,1,0:T(8,128)(2,1)S(1)} %copy-done, bf16[8,256,768]{2,1,0:T(8,128)(2,1)S(1)} %bands.1.band_ref._), custom_call_target="tpu_custom_call" | custom-call | flops 2147483648 | bytes 8388608 | tf_op jit(solution)/shard_map/inner/pallas_call | solution.py:155
  10.3 1.8 %finish.1 = (bf16[64,2,32,256]{3,2,1,0:T(8,128)(2,1)S(1)}, bf16[2,256,128]{2,1,0:T(8,128)(2,1)S(1)}, bf16[2,256,128]{2,1,0:T(8,128)(2,1)S(1)}, bf16[2,256,128]{2...) custom-call(bf16[8,256,768]{2,1,0:T(8,128)(2,1)S(1)} %bands.1.band_r, ...), custom_call_target="tpu_custom_call" | custom-call | flops 1073741824 | bytes 8388608 | tf_op jit(solution)/shard_map/finish/pallas_call | solution.py:255
  12.2 1.3 %collective-permute-start.2 = (bf16[2,256,128]{2,1,0:T(8,128)(2,1)S(1)}, bf16[2,256,128]{2,1,0:T(8,128)(2,1)S(1)}, u32[]{:S(2)}, u32[]{:S(2)}) collective-permute-start(bf16[2,256,128]{2,1,0:T(8,128)(2,1)S(1)} %get-tuple-element.41), channel_id=1, source_target_pairs={{0,16},{4,12},{8,24},{12,4},{16,0},{20,28},{24,8},{28,20},{1,17},{... | collective-permute-start | bytes 393224 | tf_op jit(solution)/shard_map/ppermute | solution.py:473
  13.5 1.2 %collective-permute-start.3 = (bf16[2,256,128]{2,1,0:T(8,128)(2,1)S(1)}, bf16[2,256,128]{2,1,0:T(8,128)(2,1)S(1)}, u32[]{:S(2)}, u32[]{:S(2)}) collective-permute-start(bf16[2,256,128]{2,1,0:T(8,128)(2,1)S(1)} %get-tuple-element.42), channel_id=1, source_target_pairs={{0,8},{4,20},{8,0},{12,28},{16,24},{20,4},{24,16},{28,12},{1,9},{5... | collective-permute-start | bytes 393224 | tf_op jit(solution)/shard_map/ppermute | solution.py:473
  14.7 1.9 %collective-permute-start.4 = (bf16[2,256,128]{2,1,0:T(8,128)(2,1)S(1)}, bf16[2,256,128]{2,1,0:T(8,128)(2,1)S(1)}, u32[]{:S(2)}, u32[]{:S(2)}) collective-permute-start(bf16[2,256,128]{2,1,0:T(8,128)(2,1)S(1)} %get-tuple-element.43), channel_id=1, source_target_pairs={{0,20},{4,8},{8,28},{12,0},{16,4},{20,24},{24,12},{28,16},{1,21},{... | collective-permute-start | bytes 393224 | tf_op jit(solution)/shard_map/ppermute | solution.py:473
  16.6 1.2 %collective-permute-start.6 = (bf16[2,256,128]{2,1,0:T(8,128)(2,1)S(1)}, bf16[2,256,128]{2,1,0:T(8,128)(2,1)S(1)}, u32[]{:S(2)}, u32[]{:S(2)}) collective-permute-start(bf16[2,256,128]{2,1,0:T(8,128)(2,1)S(1)} %get-tuple-element.45), channel_id=1, source_target_pairs={{0,24},{4,28},{8,16},{12,20},{16,8},{20,12},{24,0},{28,4},{1,25},{... | collective-permute-start | bytes 393224 | tf_op jit(solution)/shard_map/ppermute | solution.py:473
  17.8 3.0 %collective-permute-start.7 = (bf16[2,256,128]{2,1,0:T(8,128)(2,1)S(1)}, bf16[2,256,128]{2,1,0:T(8,128)(2,1)S(1)}, u32[]{:S(2)}, u32[]{:S(2)}) collective-permute-start(bf16[2,256,128]{2,1,0:T(8,128)(2,1)S(1)} %get-tuple-element.46), channel_id=1, source_target_pairs={{0,28},{4,24},{8,20},{12,16},{16,12},{20,8},{24,4},{28,0},{1,29},{... | collective-permute-start | bytes 393224 | tf_op jit(solution)/shard_map/ppermute | solution.py:473
  21.6 1.2 %collective-permute-done.5.refs_4_ = bf16[2,256,128]{2,1,0:T(8,128)(2,1)S(1)} collective-permute-done((bf16[2,256,128]{2,1,0:T(8,128)(2,1)S(1)}, bf16[2,256,128]{2,1,0:T(8,128)(2,1)S(1)}, u32[]{:S(2)}, u32[]{:S(2)}) %collective-permute-start.5) | collective-permute-done | bytes 131104 | tf_op jit(solution)/shard_map/ppermute | solution.py:473
  22.9 1.8 %collective-permute-done.6.refs_5_ = bf16[2,256,128]{2,1,0:T(8,128)(2,1)S(1)} collective-permute-done((bf16[2,256,128]{2,1,0:T(8,128)(2,1)S(1)}, bf16[2,256,128]{2,1,0:T(8,128)(2,1)S(1)}, u32[]{:S(2)}, u32[]{:S(2)}) %collective-permute-start.6) | collective-permute-done | bytes 131104 | tf_op jit(solution)/shard_map/ppermute | solution.py:473
  24.6 3.0 %collective-permute-done.7.refs_6_ = bf16[2,256,128]{2,1,0:T(8,128)(2,1)S(1)} collective-permute-done((bf16[2,256,128]{2,1,0:T(8,128)(2,1)S(1)}, bf16[2,256,128]{2,1,0:T(8,128)(2,1)S(1)}, u32[]{:S(2)}, u32[]{:S(2)}) %collective-permute-start.7) | collective-permute-done | bytes 131104 | tf_op jit(solution)/shard_map/ppermute | solution.py:473
  27.6 3.8 %temporal.1 = (bf16[2,256,128]{2,1,0:T(8,128)(2,1)S(1)}, bf16[2,256,128]{2,1,0:T(8,128)(2,1)S(1)}, bf16[2,256,128]{2,1,0:T(8,128)(2,1)S(1)}, bf16[2,256,128]{2,1...) custom-call(f32[12,256,128]{2,1,0:T(8,128)S(1)} %get-tuple-element.3, ...), custom_call_target="tpu_custom_call" | custom-call | flops 1073741824 | bytes 2097152 | tf_op jit(solution)/shard_map/temporal/pallas_call | solution.py:360
  31.5 1.2 %collective-permute-start.10 = (bf16[2,256,128]{2,1,0:T(8,128)(2,1)S(1)}, bf16[2,256,128]{2,1,0:T(8,128)(2,1)S(1)}, u32[]{:S(2)}, u32[]{:S(2)}) collective-permute-start(bf16[2,256,128]{2,1,0:T(8,128)(2,1)S(1)} %get-tuple-element.53), channel_id=1, source_target_pairs={{0,16},{4,12},{8,24},{12,4},{16,0},{20,28},{24,8},{28,20},{1,17},{... | collective-permute-start | bytes 393224 | tf_op jit(solution)/shard_map/ppermute | solution.py:473
  32.7 1.2 %collective-permute-start.11 = (bf16[2,256,128]{2,1,0:T(8,128)(2,1)S(1)}, bf16[2,256,128]{2,1,0:T(8,128)(2,1)S(1)}, u32[]{:S(2)}, u32[]{:S(2)}) collective-permute-start(bf16[2,256,128]{2,1,0:T(8,128)(2,1)S(1)} %get-tuple-element.54), channel_id=1, source_target_pairs={{0,8},{4,20},{8,0},{12,28},{16,24},{20,4},{24,16},{28,12},{1,9},{5... | collective-permute-start | bytes 393224 | tf_op jit(solution)/shard_map/ppermute | solution.py:473
  33.9 0.9 %collective-permute-start.12 = (bf16[2,256,128]{2,1,0:T(8,128)(2,1)S(1)}, bf16[2,256,128]{2,1,0:T(8,128)(2,1)S(1)}, u32[]{:S(2)}, u32[]{:S(2)}) collective-permute-start(bf16[2,256,128]{2,1,0:T(8,128)(2,1)S(1)} %get-tuple-element.55), channel_id=1, source_target_pairs={{0,20},{4,8},{8,28},{12,0},{16,4},{20,24},{24,12},{28,16},{1,21},{... | collective-permute-start | bytes 393224 | tf_op jit(solution)/shard_map/ppermute | solution.py:473
  34.9 0.8 %collective-permute-start.13 = (bf16[2,256,128]{2,1,0:T(8,128)(2,1)S(1)}, bf16[2,256,128]{2,1,0:T(8,128)(2,1)S(1)}, u32[]{:S(2)}, u32[]{:S(2)}) collective-permute-start(bf16[2,256,128]{2,1,0:T(8,128)(2,1)S(1)} %get-tuple-element.56), channel_id=1, source_target_pairs={{0,12},{4,16},{8,4},{12,24},{16,28},{20,0},{24,20},{28,8},{1,13},{... | collective-permute-start | bytes 393224 | tf_op jit(solution)/shard_map/ppermute | solution.py:473
  36.1 2.7 %collective-permute-start.15 = (bf16[2,256,128]{2,1,0:T(8,128)(2,1)S(1)}, bf16[2,256,128]{2,1,0:T(8,128)(2,1)S(1)}, u32[]{:S(2)}, u32[]{:S(2)}) collective-permute-start(bf16[2,256,128]{2,1,0:T(8,128)(2,1)S(1)} %get-tuple-element.58), channel_id=1, source_target_pairs={{0,28},{4,24},{8,20},{12,16},{16,12},{20,8},{24,4},{28,0},{1,29},{... | collective-permute-start | bytes 393224 | tf_op jit(solution)/shard_map/ppermute | solution.py:473
  38.7 0.9 %collective-permute-start.9 = (bf16[2,256,128]{2,1,0:T(8,128)(2,1)S(1)}, bf16[2,256,128]{2,1,0:T(8,128)(2,1)S(1)}, u32[]{:S(2)}, u32[]{:S(2)}) collective-permute-start(bf16[2,256,128]{2,1,0:T(8,128)(2,1)S(1)} %get-tuple-element.52), channel_id=1, source_target_pairs={{0,4},{4,0},{8,12},{12,8},{16,20},{20,16},{24,28},{28,24},{1,5},{5... | collective-permute-start | bytes 393224 | tf_op jit(solution)/shard_map/ppermute | solution.py:473
  40.3 1.3 %plan.1 = (bf16[2,256,256]{2,1,0:T(8,128)(2,1)S(1)}, f32[2,256,128]{2,1,0:T(8,128)S(1)}) custom-call(s32[1,32]{1,0:T(1,128)S(1)} %copy-done.5, s32[1]{0:T(128)S(6)} %copy.8.counts_ref, bf16[2,256,128]{2,1,0:T(8,128)(2,1)S(1)} %get-tuple-element.48._.refs_0_), custom_call_target="tpu_custom_call" | custom-call | flops 134217728 | bytes 4194304 | tf_op jit(solution)/shard_map/plan/pallas_call | solution.py:400
  42.5 3.7 %collective-permute-done.15.refs_7_ = bf16[2,256,128]{2,1,0:T(8,128)(2,1)S(1)} collective-permute-done((bf16[2,256,128]{2,1,0:T(8,128)(2,1)S(1)}, bf16[2,256,128]{2,1,0:T(8,128)(2,1)S(1)}, u32[]{:S(2)}, u32[]{:S(2)}) %collective-permute-start.15) | collective-permute-done | bytes 131104 | tf_op jit(solution)/shard_map/ppermute | solution.py:473
  46.1 1.6 %place.1 = bf16[64,2,32,256]{3,2,1,0:T(8,128)(2,1)} custom-call(bf16[2,256,256]{2,1,0:T(8,128)(2,1)S(1)} %get-tuple-element.49.put_ref, f32[2,256,128]{2,1,0:T(8,128)S(1)} %get-tuple-element.50.cover_ref, bf16[64,2,32,256]{3,2,1,0:T(8,128)(2,1)S(1)} %get-tuple-element.51.hidden_ref, bf16[2,256,128]{2,1,0:T(8,128)(2,1)S(1)} %get-tuple-element.48._.refs_0_, ...), custom_call_target="tpu_custom_call" | custom-call | flops 268435456 | bytes 4194304 | tf_op jit(solution)/shard_map/place/pallas_call | solution.py:455
  (28 shorter events, 2.2 us)
Async XLA Ops:
  0.0 2.3 %copy-start = (bf16[64,2,32,256]{3,2,1,0:T(8,128)(2,1)S(1)}, bf16[64,2,32,256]{3,2,1,0:T(8,128)(2,1)}, u32[]{:S(2)}) copy-start(bf16[64,2,32,256]{3,2,1,0:T(8,128)(2,1)} %grid_ref.3) | copy-start | bytes 6291460
  0.0 0.9 %copy-start.1 = (bf16[9,64,8]{1,2,0:T(8,128)(2,1)S(1)}, bf16[9,64,8]{1,2,0:T(8,128)(2,1)}, u32[]{:S(2)}) copy-start(bf16[9,64,8]{1,2,0:T(8,128)(2,1)} %param.8) | copy-start | bytes 27652
  2.3 5.2 %copy-start.4 = (f32[64]{0:T(128)S(1)}, f32[64]{0:T(128)}, u32[]{:S(2)}) copy-start(f32[64]{0:T(128)} %bias_ref.1) | copy-start | bytes 772
  2.3 5.2 %copy-start.5 = (s32[1,32]{1,0:T(1,128)S(1)}, s32[1,32]{1,0:T(1,128)}, u32[]{:S(2)}) copy-start(s32[1,32]{1,0:T(1,128)} %occupied_ref.3) | copy-start | bytes 388
  3.0 7.3 %collective-permute-start = (bf16[16,256]{1,0:T(8,128)(2,1)S(1)}, bf16[16,256]{1,0:T(8,128)(2,1)S(1)}, u32[]{:S(2)}, u32[]{:S(2)}) collective-permute-start(bf16[16,256]{1,0:T(8,128)(2,1)S(1)} %get-tuple-element.36), channel_id=1, source_target_pairs={{0,1},{1,0},{2,3},{3,2},{4,5},{5,4},{6,7},{7,6},{8,9},{9,8},{10,11... | collective-permute-start | bytes 24584 | tf_op jit(solution)/shard_map/ppermute | solution.py:484
  3.0 7.3 %collective-permute-start.1 = (bf16[16,256]{1,0:T(8,128)(2,1)S(1)}, bf16[16,256]{1,0:T(8,128)(2,1)S(1)}, u32[]{:S(2)}, u32[]{:S(2)}) collective-permute-start(bf16[16,256]{1,0:T(8,128)(2,1)S(1)} %get-tuple-element.37), channel_id=1, source_target_pairs={{0,0},{1,2},{2,1},{3,3},{4,4},{5,6},{6,5},{7,7},{8,8},{9,10},{10,9... | collective-permute-start | bytes 24584 | tf_op jit(solution)/shard_map/ppermute | solution.py:485
  10.3 10.5 %copy-start.2 = (bf16[4,64,64]{2,1,0:T(8,128)(2,1)S(1)}, bf16[4,64,64]{2,1,0:T(8,128)(2,1)}, u32[]{:S(2)}) copy-start(bf16[4,64,64]{2,1,0:T(8,128)(2,1)} %point_ref.1) | copy-start | bytes 98308
  10.3 10.5 %copy-start.3 = (f32[4,3,64]{2,0,1:T(4,128)S(1)}, f32[4,3,64]{2,0,1:T(4,128)}, u32[]{:S(2)}) copy-start(f32[4,3,64]{2,0,1:T(4,128)} %param.10) | copy-start | bytes 9220
  12.2 5.6 %collective-permute-start.2 = (bf16[2,256,128]{2,1,0:T(8,128)(2,1)S(1)}, bf16[2,256,128]{2,1,0:T(8,128)(2,1)S(1)}, u32[]{:S(2)}, u32[]{:S(2)}) collective-permute-start(bf16[2,256,128]{2,1,0:T(8,128)(2,1)S(1)} %get-tuple-element.41), channel_id=1, source_target_pairs={{0,16},{4,12},{8,24},{12,4},{16,0},{20,28},{24,8},{28,20},{1,17},{... | collective-permute-start | bytes 393224 | tf_op jit(solution)/shard_map/ppermute | solution.py:473
  13.5 7.3 %collective-permute-start.3 = (bf16[2,256,128]{2,1,0:T(8,128)(2,1)S(1)}, bf16[2,256,128]{2,1,0:T(8,128)(2,1)S(1)}, u32[]{:S(2)}, u32[]{:S(2)}) collective-permute-start(bf16[2,256,128]{2,1,0:T(8,128)(2,1)S(1)} %get-tuple-element.42), channel_id=1, source_target_pairs={{0,8},{4,20},{8,0},{12,28},{16,24},{20,4},{24,16},{28,12},{1,9},{5... | collective-permute-start | bytes 393224 | tf_op jit(solution)/shard_map/ppermute | solution.py:473
  14.7 6.9 %collective-permute-start.4 = (bf16[2,256,128]{2,1,0:T(8,128)(2,1)S(1)}, bf16[2,256,128]{2,1,0:T(8,128)(2,1)S(1)}, u32[]{:S(2)}, u32[]{:S(2)}) collective-permute-start(bf16[2,256,128]{2,1,0:T(8,128)(2,1)S(1)} %get-tuple-element.43), channel_id=1, source_target_pairs={{0,20},{4,8},{8,28},{12,0},{16,4},{20,24},{24,12},{28,16},{1,21},{... | collective-permute-start | bytes 393224 | tf_op jit(solution)/shard_map/ppermute | solution.py:473
  16.6 6.2 %collective-permute-start.5 = (bf16[2,256,128]{2,1,0:T(8,128)(2,1)S(1)}, bf16[2,256,128]{2,1,0:T(8,128)(2,1)S(1)}, u32[]{:S(2)}, u32[]{:S(2)}) collective-permute-start(bf16[2,256,128]{2,1,0:T(8,128)(2,1)S(1)} %get-tuple-element.44), channel_id=1, source_target_pairs={{0,12},{4,16},{8,4},{12,24},{16,28},{20,0},{24,20},{28,8},{1,13},{... | collective-permute-start | bytes 393224 | tf_op jit(solution)/shard_map/ppermute | solution.py:473
  16.6 8.0 %collective-permute-start.6 = (bf16[2,256,128]{2,1,0:T(8,128)(2,1)S(1)}, bf16[2,256,128]{2,1,0:T(8,128)(2,1)S(1)}, u32[]{:S(2)}, u32[]{:S(2)}) collective-permute-start(bf16[2,256,128]{2,1,0:T(8,128)(2,1)S(1)} %get-tuple-element.45), channel_id=1, source_target_pairs={{0,24},{4,28},{8,16},{12,20},{16,8},{20,12},{24,0},{28,4},{1,25},{... | collective-permute-start | bytes 393224 | tf_op jit(solution)/shard_map/ppermute | solution.py:473
  17.8 9.8 %collective-permute-start.7 = (bf16[2,256,128]{2,1,0:T(8,128)(2,1)S(1)}, bf16[2,256,128]{2,1,0:T(8,128)(2,1)S(1)}, u32[]{:S(2)}, u32[]{:S(2)}) collective-permute-start(bf16[2,256,128]{2,1,0:T(8,128)(2,1)S(1)} %get-tuple-element.46), channel_id=1, source_target_pairs={{0,28},{4,24},{8,20},{12,16},{16,12},{20,8},{24,4},{28,0},{1,29},{... | collective-permute-start | bytes 393224 | tf_op jit(solution)/shard_map/ppermute | solution.py:473
  20.8 6.9 %collective-permute-start.8 = (bf16[2,256,128]{2,1,0:T(8,128)(2,1)S(1)}, bf16[2,256,128]{2,1,0:T(8,128)(2,1)S(1)}, u32[]{:S(2)}, u32[]{:S(2)}) collective-permute-start(bf16[2,256,128]{2,1,0:T(8,128)(2,1)S(1)} %get-tuple-element.47), channel_id=1, source_target_pairs={{0,4},{4,0},{8,12},{12,8},{16,20},{20,16},{24,28},{28,24},{1,5},{5... | collective-permute-start | bytes 393224 | tf_op jit(solution)/shard_map/ppermute | solution.py:473
  31.5 4.6 %collective-permute-start.10 = (bf16[2,256,128]{2,1,0:T(8,128)(2,1)S(1)}, bf16[2,256,128]{2,1,0:T(8,128)(2,1)S(1)}, u32[]{:S(2)}, u32[]{:S(2)}) collective-permute-start(bf16[2,256,128]{2,1,0:T(8,128)(2,1)S(1)} %get-tuple-element.53), channel_id=1, source_target_pairs={{0,16},{4,12},{8,24},{12,4},{16,0},{20,28},{24,8},{28,20},{1,17},{... | collective-permute-start | bytes 393224 | tf_op jit(solution)/shard_map/ppermute | solution.py:473
  32.7 6.0 %collective-permute-start.11 = (bf16[2,256,128]{2,1,0:T(8,128)(2,1)S(1)}, bf16[2,256,128]{2,1,0:T(8,128)(2,1)S(1)}, u32[]{:S(2)}, u32[]{:S(2)}) collective-permute-start(bf16[2,256,128]{2,1,0:T(8,128)(2,1)S(1)} %get-tuple-element.54), channel_id=1, source_target_pairs={{0,8},{4,20},{8,0},{12,28},{16,24},{20,4},{24,16},{28,12},{1,9},{5... | collective-permute-start | bytes 393224 | tf_op jit(solution)/shard_map/ppermute | solution.py:473
  33.9 7.6 %collective-permute-start.12 = (bf16[2,256,128]{2,1,0:T(8,128)(2,1)S(1)}, bf16[2,256,128]{2,1,0:T(8,128)(2,1)S(1)}, u32[]{:S(2)}, u32[]{:S(2)}) collective-permute-start(bf16[2,256,128]{2,1,0:T(8,128)(2,1)S(1)} %get-tuple-element.55), channel_id=1, source_target_pairs={{0,20},{4,8},{8,28},{12,0},{16,4},{20,24},{24,12},{28,16},{1,21},{... | collective-permute-start | bytes 393224 | tf_op jit(solution)/shard_map/ppermute | solution.py:473
  34.9 7.2 %collective-permute-start.13 = (bf16[2,256,128]{2,1,0:T(8,128)(2,1)S(1)}, bf16[2,256,128]{2,1,0:T(8,128)(2,1)S(1)}, u32[]{:S(2)}, u32[]{:S(2)}) collective-permute-start(bf16[2,256,128]{2,1,0:T(8,128)(2,1)S(1)} %get-tuple-element.56), channel_id=1, source_target_pairs={{0,12},{4,16},{8,4},{12,24},{16,28},{20,0},{24,20},{28,8},{1,13},{... | collective-permute-start | bytes 393224 | tf_op jit(solution)/shard_map/ppermute | solution.py:473
  35.7 6.8 %collective-permute-start.14 = (bf16[2,256,128]{2,1,0:T(8,128)(2,1)S(1)}, bf16[2,256,128]{2,1,0:T(8,128)(2,1)S(1)}, u32[]{:S(2)}, u32[]{:S(2)}) collective-permute-start(bf16[2,256,128]{2,1,0:T(8,128)(2,1)S(1)} %get-tuple-element.57), channel_id=1, source_target_pairs={{0,24},{4,28},{8,16},{12,20},{16,8},{20,12},{24,0},{28,4},{1,25},{... | collective-permute-start | bytes 393224 | tf_op jit(solution)/shard_map/ppermute | solution.py:473
  36.1 10.1 %collective-permute-start.15 = (bf16[2,256,128]{2,1,0:T(8,128)(2,1)S(1)}, bf16[2,256,128]{2,1,0:T(8,128)(2,1)S(1)}, u32[]{:S(2)}, u32[]{:S(2)}) collective-permute-start(bf16[2,256,128]{2,1,0:T(8,128)(2,1)S(1)} %get-tuple-element.58), channel_id=1, source_target_pairs={{0,28},{4,24},{8,20},{12,16},{16,12},{20,8},{24,4},{28,0},{1,29},{... | collective-permute-start | bytes 393224 | tf_op jit(solution)/shard_map/ppermute | solution.py:473
  38.7 7.4 %collective-permute-start.9 = (bf16[2,256,128]{2,1,0:T(8,128)(2,1)S(1)}, bf16[2,256,128]{2,1,0:T(8,128)(2,1)S(1)}, u32[]{:S(2)}, u32[]{:S(2)}) collective-permute-start(bf16[2,256,128]{2,1,0:T(8,128)(2,1)S(1)} %get-tuple-element.52), channel_id=1, source_target_pairs={{0,4},{4,0},{8,12},{12,8},{16,20},{20,16},{24,28},{28,24},{1,5},{5... | collective-permute-start | bytes 393224 | tf_op jit(solution)/shard_map/ppermute | solution.py:473

commit v4 on v3

--- a/solution.py
+++ b/solution.py
@@ -22,6 +22,14 @@
 
 def dot(a, b, dims=((1,), (0,))):
     return lax.dot_general(a, b, (dims, ((), ())), preferred_element_type=jnp.float32)
+
+
+def quotient(value, size):
+    return value >> (size.bit_length() - 1) if size & (size - 1) == 0 else value // size
+
+
+def remainder(value, size):
+    return value & (size - 1) if size & (size - 1) == 0 else value % size
 
 
 def iota(shape, dim):
@@ -72,19 +80,27 @@
     _, inner, channels = taps_ref.shape
     wide = GROUP * height
     repeat = (iota((inner, wide), 0) == iota((inner, wide), 1) // height).astype(jnp.bfloat16)
-    offset = iota((height, wide), 1) % height - iota((height, wide), 0)
-    masks = [offset == row - 1 for row in range(3)]
     for tap in range(9):
         half = (taps_ref[tap].astype(jnp.float32) * 0.5).astype(jnp.bfloat16)
         spread[tap] = dot(half, repeat, ((0,), (0,)))
-
+    strip = 16
+    offset = remainder(iota((height, wide), 1), height) - iota((height, wide), 0)
+    offset = offset.astype(jnp.float32).astype(jnp.bfloat16)
+    masks = [
+        [offset[top : top + strip] == jnp.bfloat16(row - 1) for row in range(3)] for top in range(0, height, strip)
+    ]
     for c in range(channels):
-        out = c % GROUP * height
         for col in range(3):
-            value = jnp.zeros((height, wide), jnp.float32)
-            for row in range(3):
-                value = jnp.where(masks[row], spread[3 * row + col, c : c + 1, :], value)
-            band_ref[c // GROUP, out : out + height, col * wide : (col + 1) * wide] = value.astype(jnp.bfloat16)
+            rows = [
+                jnp.broadcast_to(spread[3 * row + col, c : c + 1, :], (strip, wide)).astype(jnp.bfloat16)
+                for row in range(3)
+            ]
+            for at, mask in enumerate(masks):
+                value = jnp.zeros((strip, wide), jnp.bfloat16)
+                for row in range(3):
+                    value = jnp.where(mask[row], rows[row], value)
+                top = c % GROUP * height + at * strip
+                band_ref[c // GROUP, top : top + strip, col * wide : (col + 1) * wide] = value
 
 
 def bands(conv_weight, height):
@@ -109,32 +125,30 @@
     slots = occupied_ref.shape[1] // count
     part = GROUP * slots
     rows, lanes = iota((part, wide), 0), iota((part, wide), 1)
-    at_slot, at_side = rows % slots, iota((part, LANES), 0) % slots
-    same_channel, at_row = lanes // height == rows // slots, lanes % height
+    at_slot, at_side = remainder(rows, slots), remainder(iota((part, LANES), 0), slots)
+    same_channel, at_row = quotient(lanes, height) == quotient(rows, slots), remainder(lanes, height)
     for d, step in enumerate(steps_of(count)):
         row, side = jnp.zeros((part, wide), jnp.int32), jnp.zeros((part, LANES), jnp.int32)
+        first = sent_to(me, step) * slots
         for j in range(slots):
-            block = occupied_ref[0, sent_to(me, step) * slots + j]
-            row = jnp.where(at_slot == j, block // halves, row)
-            side = jnp.where(at_side == j, block % halves, side)
+            block = occupied_ref[0, first + j]
+            row = jnp.where(at_slot == j, quotient(block, halves), row)
+            side = jnp.where(at_side == j, remainder(block, halves), side)
         pick_ref[d * part : (d + 1) * part, :] = (same_channel & (at_row == row)).astype(jnp.bfloat16)
         side_ref[d * part : (d + 1) * part, :] = side
 
     tile_lanes = iota((wide, LANES), 1)
     is_first, is_last = tile_lanes == 0, tile_lanes == LANES - 1
-    nothing = jnp.zeros((wide, LANES), jnp.float32)
+    nothing = jnp.zeros((wide, LANES), jnp.bfloat16)
 
     def shifted(g, f):
         cells = grid_ref[g * GROUP : (g + 1) * GROUP, f].reshape(wide, columns)
-        full = cells.astype(jnp.float32)
-        cells_ref[g, f] = full
-        tiles = [full[:, side * LANES : (side + 1) * LANES] for side in range(halves)]
+        tiles = [cells[:, side * LANES : (side + 1) * LANES] for side in range(halves)]
         right = [pltpu.roll(tile, 1, 1) for tile in tiles]
         left = [pltpu.roll(tile, LANES - 1, 1) for tile in tiles]
         before = [jnp.where(is_first, *pair) for pair in zip([nothing] + right[:-1], right)]
         after = [jnp.where(is_last, *pair) for pair in zip(left[1:] + [nothing], left)]
-        before, after = (jnp.concatenate(parts, axis=1).astype(jnp.bfloat16) for parts in (before, after))
-        return jnp.concatenate([before, cells, after], axis=0)
+        return jnp.concatenate([jnp.concatenate(before, axis=1), cells, jnp.concatenate(after, axis=1)], axis=0)
 
     items = [(g, f) for g in range(channels // GROUP) for f in range(frames)]
     ready = shifted(*items[0])
@@ -145,6 +159,7 @@
         for out in range(GROUP):
             inside = slice(out * height, (out + 1) * height)
             summed_ref[g, f, inside, :] = summed[inside] + 0.5 * bias_ref[g * GROUP + out]
+            cells_ref[g, f, inside, :] = grid_ref[g * GROUP + out, f].astype(jnp.float32)
 
 
 def inner(grid, band, conv_bias, occupied, parts):
@@ -175,7 +190,7 @@
 
 
 def sent_to(me, step):
-    return me ^ jnp.where(me % 2 == 0, step[0], step[1])
+    return me ^ jnp.where(remainder(me, 2) == 0, step[0], step[1])
 
 
 def got_from(me, step):

time: 47.9 us -> 47.4 us (0.990)
  Pallas kernels: 13.9 us -> 13.3 us
  transfers between devices with their start and end apart: 16 -> 16, of which waited for: 7 -> 7; matrix products, arithmetic and copies ran while one was open for 0% -> 0% of each run, Pallas kernels for 10% -> 9%
where the time goes in v4:
time: 47.4 us; the launch traced here: 47.2 us
  starting transfers between devices  21.3 us (45%)
  Pallas kernels  13.3 us (28%)
  waiting for transfers between devices  10.9 us (23%)
  local copies, waits for them, and re-layouts  0.9 us (2%)
  between operations  0.82 us (2%)
    ppermute x14, starting transfers between devices, exchange(): lax.ppermute(array, 'frame', [(i, i ^ step[i % 2]) for i in range(count)])  16.7 us
    ppermute x14, waiting for transfers between devices, exchange(): lax.ppermute(array, 'frame', [(i, i ^ step[i % 2]) for i in range(count)])  10.9 us
    ppermute x1, starting transfers between devices, on_device(): second = lax.ppermute(second, 'tile', swaps(tiles, 1))  4.48 us
    pallas_call x1, Pallas kernels, temporal(): pl.pallas_call(functools.partial(temporal_kernel, sources), in_specs=[vme...  3.82 us
    pallas_call x1, Pallas kernels, inner(): pl.pallas_call(inner_kernel, in_specs=[smem, smem, vmem, vmem], out_shape...  2.63 us
    pallas_call x1, Pallas kernels, finish(): pl.pallas_call(finish_kernel, in_specs=[vmem] * 7, out_shape=[jax.ShapeDt...  1.85 us
    pallas_call x1, Pallas kernels, place(): pl.pallas_call(functools.partial(place_kernel, sources), in_specs=[vmem,...  1.62 us
    pallas_call x1, Pallas kernels, plan(): pl.pallas_call(functools.partial(plan_kernel, sources), in_specs=[smem, s...  1.26 us
  transfers between devices with their start and end apart: 16, of which 7 were waited for; matrix products, arithmetic and copies ran while one was open for 0% of the time, Pallas kernels for 9%

profile of v4, /device:TPU:9, one launch (start us, length us, event | category | flops | bytes accessed | tf_op | source)
XLA Modules:
  0.0 47.2 jit_solution(11851143195252781562)
XLA Ops:
  0.0 0.9 %copy-done.1 = bf16[9,64,8]{1,2,0:T(8,128)(2,1)S(1)} copy-done((bf16[9,64,8]{1,2,0:T(8,128)(2,1)S(1)}, bf16[9,64,8]{1,2,0:T(8,128)(2,1)}, u32[]{:S(2)}) %copy-start.1) | copy-done | bytes 9240
  0.9 0.9 %bands.1.band_ref._ = bf16[8,256,768]{2,1,0:T(8,128)(2,1)S(1)} custom-call(bf16[9,8,64]{2,1,0:T(8,128)(2,1)S(1)} %bitcast.2), custom_call_target="tpu_custom_call" | custom-call | flops 268435456 | bytes 8388608 | tf_op jit(solution)/shard_map/bands/pallas_call | solution.py:110
  1.8 0.7 %edge_columns.1 = (bf16[16,256]{1,0:T(8,128)(2,1)S(1)}, bf16[16,256]{1,0:T(8,128)(2,1)S(1)}) custom-call(bf16[64,2,32,256]{3,2,1,0:T(8,128)(2,1)S(1)} %copy-done, bf16[8,256,768]{2,1,0:T(8,128)(2,1)S(1)} %bands.1.band_ref._), custom_call_target="tpu_custom_call" | custom-call | flops 268435456 | bytes 2097152 | tf_op jit(solution)/shard_map/edge_columns/pallas_call | solution.py:68
  2.6 4.5 %collective-permute-start.1 = (bf16[16,256]{1,0:T(8,128)(2,1)S(1)}, bf16[16,256]{1,0:T(8,128)(2,1)S(1)}, u32[]{:S(2)}, u32[]{:S(2)}) collective-permute-start(bf16[16,256]{1,0:T(8,128)(2,1)S(1)} %get-tuple-element.37), channel_id=1, source_target_pairs={{0,0},{1,2},{2,1},{3,3},{4,4},{5,6},{6,5},{7,7},{8,8},{9,10},{10,9... | collective-permute-start | bytes 24584 | tf_op jit(solution)/shard_map/ppermute | solution.py:500
  7.1 2.6 %inner.1 = (f32[8,2,256,256]{3,2,1,0:T(8,128)S(1)}, f32[8,2,256,256]{3,2,1,0:T(8,128)S(1)}, bf16[256,256]{1,0:T(8,128)(2,1)S(1)}, s32[256,128]{1,0:T(8,128)S(1)}) custom-call(s32[1,32]{1,0:T(1,128)S(1)} %copy-done.5, f32[64]{0:T(128)S(1)} %copy-done.4, bf16[64,2,32,256]{3,2,1,0:T(8,128)(2,1)S(1)} %copy-done, bf16[8,256,768]{2,1,0:T(8,128)(2,1)S(1)} %bands.1.band_ref._), custom_call_target="tpu_custom_call" | custom-call | flops 2147483648 | bytes 8388608 | tf_op jit(solution)/shard_map/inner/pallas_call | solution.py:170
  9.8 1.8 %finish.1 = (bf16[64,2,32,256]{3,2,1,0:T(8,128)(2,1)S(1)}, bf16[2,256,128]{2,1,0:T(8,128)(2,1)S(1)}, bf16[2,256,128]{2,1,0:T(8,128)(2,1)S(1)}, bf16[2,256,128]{2...) custom-call(bf16[8,256,768]{2,1,0:T(8,128)(2,1)S(1)} %bands.1.band_r, ...), custom_call_target="tpu_custom_call" | custom-call | flops 1073741824 | bytes 8388608 | tf_op jit(solution)/shard_map/finish/pallas_call | solution.py:270
  11.6 1.3 %collective-permute-start.2 = (bf16[2,256,128]{2,1,0:T(8,128)(2,1)S(1)}, bf16[2,256,128]{2,1,0:T(8,128)(2,1)S(1)}, u32[]{:S(2)}, u32[]{:S(2)}) collective-permute-start(bf16[2,256,128]{2,1,0:T(8,128)(2,1)S(1)} %get-tuple-element.41), channel_id=1, source_target_pairs={{0,16},{4,12},{8,24},{12,4},{16,0},{20,28},{24,8},{28,20},{1,17},{... | collective-permute-start | bytes 393224 | tf_op jit(solution)/shard_map/ppermute | solution.py:488
  12.9 1.2 %collective-permute-start.3 = (bf16[2,256,128]{2,1,0:T(8,128)(2,1)S(1)}, bf16[2,256,128]{2,1,0:T(8,128)(2,1)S(1)}, u32[]{:S(2)}, u32[]{:S(2)}) collective-permute-start(bf16[2,256,128]{2,1,0:T(8,128)(2,1)S(1)} %get-tuple-element.42), channel_id=1, source_target_pairs={{0,8},{4,20},{8,0},{12,28},{16,24},{20,4},{24,16},{28,12},{1,9},{5... | collective-permute-start | bytes 393224 | tf_op jit(solution)/shard_map/ppermute | solution.py:488
  14.1 1.9 %collective-permute-start.4 = (bf16[2,256,128]{2,1,0:T(8,128)(2,1)S(1)}, bf16[2,256,128]{2,1,0:T(8,128)(2,1)S(1)}, u32[]{:S(2)}, u32[]{:S(2)}) collective-permute-start(bf16[2,256,128]{2,1,0:T(8,128)(2,1)S(1)} %get-tuple-element.43), channel_id=1, source_target_pairs={{0,20},{4,8},{8,28},{12,0},{16,4},{20,24},{24,12},{28,16},{1,21},{... | collective-permute-start | bytes 393224 | tf_op jit(solution)/shard_map/ppermute | solution.py:488
  16.1 1.2 %collective-permute-start.6 = (bf16[2,256,128]{2,1,0:T(8,128)(2,1)S(1)}, bf16[2,256,128]{2,1,0:T(8,128)(2,1)S(1)}, u32[]{:S(2)}, u32[]{:S(2)}) collective-permute-start(bf16[2,256,128]{2,1,0:T(8,128)(2,1)S(1)} %get-tuple-element.45), channel_id=1, source_target_pairs={{0,24},{4,28},{8,16},{12,20},{16,8},{20,12},{24,0},{28,4},{1,25},{... | collective-permute-start | bytes 393224 | tf_op jit(solution)/shard_map/ppermute | solution.py:488
  17.2 3.0 %collective-permute-start.7 = (bf16[2,256,128]{2,1,0:T(8,128)(2,1)S(1)}, bf16[2,256,128]{2,1,0:T(8,128)(2,1)S(1)}, u32[]{:S(2)}, u32[]{:S(2)}) collective-permute-start(bf16[2,256,128]{2,1,0:T(8,128)(2,1)S(1)} %get-tuple-element.46), channel_id=1, source_target_pairs={{0,28},{4,24},{8,20},{12,16},{16,12},{20,8},{24,4},{28,0},{1,29},{... | collective-permute-start | bytes 393224 | tf_op jit(solution)/shard_map/ppermute | solution.py:488
  21.0 1.3 %collective-permute-done.5.refs_4_ = bf16[2,256,128]{2,1,0:T(8,128)(2,1)S(1)} collective-permute-done((bf16[2,256,128]{2,1,0:T(8,128)(2,1)S(1)}, bf16[2,256,128]{2,1,0:T(8,128)(2,1)S(1)}, u32[]{:S(2)}, u32[]{:S(2)}) %collective-permute-start.5) | collective-permute-done | bytes 131104 | tf_op jit(solution)/shard_map/ppermute | solution.py:488
  22.3 1.8 %collective-permute-done.6.refs_5_ = bf16[2,256,128]{2,1,0:T(8,128)(2,1)S(1)} collective-permute-done((bf16[2,256,128]{2,1,0:T(8,128)(2,1)S(1)}, bf16[2,256,128]{2,1,0:T(8,128)(2,1)S(1)}, u32[]{:S(2)}, u32[]{:S(2)}) %collective-permute-start.6) | collective-permute-done | bytes 131104 | tf_op jit(solution)/shard_map/ppermute | solution.py:488
  24.1 3.0 %collective-permute-done.7.refs_6_ = bf16[2,256,128]{2,1,0:T(8,128)(2,1)S(1)} collective-permute-done((bf16[2,256,128]{2,1,0:T(8,128)(2,1)S(1)}, bf16[2,256,128]{2,1,0:T(8,128)(2,1)S(1)}, u32[]{:S(2)}, u32[]{:S(2)}) %collective-permute-start.7) | collective-permute-done | bytes 131104 | tf_op jit(solution)/shard_map/ppermute | solution.py:488
  27.1 3.8 %temporal.1 = (bf16[2,256,128]{2,1,0:T(8,128)(2,1)S(1)}, bf16[2,256,128]{2,1,0:T(8,128)(2,1)S(1)}, bf16[2,256,128]{2,1,0:T(8,128)(2,1)S(1)}, bf16[2,256,128]{2,1...) custom-call(f32[12,256,128]{2,1,0:T(8,128)S(1)} %get-tuple-element.3, ...), custom_call_target="tpu_custom_call" | custom-call | flops 1073741824 | bytes 2097152 | tf_op jit(solution)/shard_map/temporal/pallas_call | solution.py:375
  30.9 1.2 %collective-permute-start.10 = (bf16[2,256,128]{2,1,0:T(8,128)(2,1)S(1)}, bf16[2,256,128]{2,1,0:T(8,128)(2,1)S(1)}, u32[]{:S(2)}, u32[]{:S(2)}) collective-permute-start(bf16[2,256,128]{2,1,0:T(8,128)(2,1)S(1)} %get-tuple-element.53), channel_id=1, source_target_pairs={{0,16},{4,12},{8,24},{12,4},{16,0},{20,28},{24,8},{28,20},{1,17},{... | collective-permute-start | bytes 393224 | tf_op jit(solution)/shard_map/ppermute | solution.py:488
  32.1 1.2 %collective-permute-start.11 = (bf16[2,256,128]{2,1,0:T(8,128)(2,1)S(1)}, bf16[2,256,128]{2,1,0:T(8,128)(2,1)S(1)}, u32[]{:S(2)}, u32[]{:S(2)}) collective-permute-start(bf16[2,256,128]{2,1,0:T(8,128)(2,1)S(1)} %get-tuple-element.54), channel_id=1, source_target_pairs={{0,8},{4,20},{8,0},{12,28},{16,24},{20,4},{24,16},{28,12},{1,9},{5... | collective-permute-start | bytes 393224 | tf_op jit(solution)/shard_map/ppermute | solution.py:488
  33.4 0.9 %collective-permute-start.12 = (bf16[2,256,128]{2,1,0:T(8,128)(2,1)S(1)}, bf16[2,256,128]{2,1,0:T(8,128)(2,1)S(1)}, u32[]{:S(2)}, u32[]{:S(2)}) collective-permute-start(bf16[2,256,128]{2,1,0:T(8,128)(2,1)S(1)} %get-tuple-element.55), channel_id=1, source_target_pairs={{0,20},{4,8},{8,28},{12,0},{16,4},{20,24},{24,12},{28,16},{1,21},{... | collective-permute-start | bytes 393224 | tf_op jit(solution)/shard_map/ppermute | solution.py:488
  34.3 0.8 %collective-permute-start.13 = (bf16[2,256,128]{2,1,0:T(8,128)(2,1)S(1)}, bf16[2,256,128]{2,1,0:T(8,128)(2,1)S(1)}, u32[]{:S(2)}, u32[]{:S(2)}) collective-permute-start(bf16[2,256,128]{2,1,0:T(8,128)(2,1)S(1)} %get-tuple-element.56), channel_id=1, source_target_pairs={{0,12},{4,16},{8,4},{12,24},{16,28},{20,0},{24,20},{28,8},{1,13},{... | collective-permute-start | bytes 393224 | tf_op jit(solution)/shard_map/ppermute | solution.py:488
  35.5 2.6 %collective-permute-start.15 = (bf16[2,256,128]{2,1,0:T(8,128)(2,1)S(1)}, bf16[2,256,128]{2,1,0:T(8,128)(2,1)S(1)}, u32[]{:S(2)}, u32[]{:S(2)}) collective-permute-start(bf16[2,256,128]{2,1,0:T(8,128)(2,1)S(1)} %get-tuple-element.58), channel_id=1, source_target_pairs={{0,28},{4,24},{8,20},{12,16},{16,12},{20,8},{24,4},{28,0},{1,29},{... | collective-permute-start | bytes 393224 | tf_op jit(solution)/shard_map/ppermute | solution.py:488
  38.1 0.9 %collective-permute-start.9 = (bf16[2,256,128]{2,1,0:T(8,128)(2,1)S(1)}, bf16[2,256,128]{2,1,0:T(8,128)(2,1)S(1)}, u32[]{:S(2)}, u32[]{:S(2)}) collective-permute-start(bf16[2,256,128]{2,1,0:T(8,128)(2,1)S(1)} %get-tuple-element.52), channel_id=1, source_target_pairs={{0,4},{4,0},{8,12},{12,8},{16,20},{20,16},{24,28},{28,24},{1,5},{5... | collective-permute-start | bytes 393224 | tf_op jit(solution)/shard_map/ppermute | solution.py:488
  39.7 1.3 %plan.1 = (bf16[2,256,256]{2,1,0:T(8,128)(2,1)S(1)}, f32[2,256,128]{2,1,0:T(8,128)S(1)}) custom-call(s32[1,32]{1,0:T(1,128)S(1)} %copy-done.5, s32[1]{0:T(128)S(6)} %copy.8.counts_ref, bf16[2,256,128]{2,1,0:T(8,128)(2,1)S(1)} %get-tuple-element.48._.refs_0_), custom_call_target="tpu_custom_call" | custom-call | flops 134217728 | bytes 4194304 | tf_op jit(solution)/shard_map/plan/pallas_call | solution.py:415
  41.9 3.7 %collective-permute-done.15.refs_7_ = bf16[2,256,128]{2,1,0:T(8,128)(2,1)S(1)} collective-permute-done((bf16[2,256,128]{2,1,0:T(8,128)(2,1)S(1)}, bf16[2,256,128]{2,1,0:T(8,128)(2,1)S(1)}, u32[]{:S(2)}, u32[]{:S(2)}) %collective-permute-start.15) | collective-permute-done | bytes 131104 | tf_op jit(solution)/shard_map/ppermute | solution.py:488
  45.6 1.6 %place.1 = bf16[64,2,32,256]{3,2,1,0:T(8,128)(2,1)} custom-call(bf16[2,256,256]{2,1,0:T(8,128)(2,1)S(1)} %get-tuple-element.49.put_ref, f32[2,256,128]{2,1,0:T(8,128)S(1)} %get-tuple-element.50.cover_ref, bf16[64,2,32,256]{3,2,1,0:T(8,128)(2,1)S(1)} %get-tuple-element.51.hidden_ref, bf16[2,256,128]{2,1,0:T(8,128)(2,1)S(1)} %get-tuple-element.48._.refs_0_, ...), custom_call_target="tpu_custom_call" | custom-call | flops 268435456 | bytes 4194304 | tf_op jit(solution)/shard_map/place/pallas_call | solution.py:470
  (28 shorter events, 2.2 us)
Async XLA Ops:
  0.0 1.8 %copy-start = (bf16[64,2,32,256]{3,2,1,0:T(8,128)(2,1)S(1)}, bf16[64,2,32,256]{3,2,1,0:T(8,128)(2,1)}, u32[]{:S(2)}) copy-start(bf16[64,2,32,256]{3,2,1,0:T(8,128)(2,1)} %grid_ref.3) | copy-start | bytes 6291460
  0.0 0.9 %copy-start.1 = (bf16[9,64,8]{1,2,0:T(8,128)(2,1)S(1)}, bf16[9,64,8]{1,2,0:T(8,128)(2,1)}, u32[]{:S(2)}) copy-start(bf16[9,64,8]{1,2,0:T(8,128)(2,1)} %param.8) | copy-start | bytes 27652
  1.8 5.2 %copy-start.4 = (f32[64]{0:T(128)S(1)}, f32[64]{0:T(128)}, u32[]{:S(2)}) copy-start(f32[64]{0:T(128)} %bias_ref.1) | copy-start | bytes 772
  1.8 5.2 %copy-start.5 = (s32[1,32]{1,0:T(1,128)S(1)}, s32[1,32]{1,0:T(1,128)}, u32[]{:S(2)}) copy-start(s32[1,32]{1,0:T(1,128)} %occupied_ref.3) | copy-start | bytes 388
  2.5 7.2 %collective-permute-start = (bf16[16,256]{1,0:T(8,128)(2,1)S(1)}, bf16[16,256]{1,0:T(8,128)(2,1)S(1)}, u32[]{:S(2)}, u32[]{:S(2)}) collective-permute-start(bf16[16,256]{1,0:T(8,128)(2,1)S(1)} %get-tuple-element.36), channel_id=1, source_target_pairs={{0,1},{1,0},{2,3},{3,2},{4,5},{5,4},{6,7},{7,6},{8,9},{9,8},{10,11... | collective-permute-start | bytes 24584 | tf_op jit(solution)/shard_map/ppermute | solution.py:499
  2.6 7.2 %collective-permute-start.1 = (bf16[16,256]{1,0:T(8,128)(2,1)S(1)}, bf16[16,256]{1,0:T(8,128)(2,1)S(1)}, u32[]{:S(2)}, u32[]{:S(2)}) collective-permute-start(bf16[16,256]{1,0:T(8,128)(2,1)S(1)} %get-tuple-element.37), channel_id=1, source_target_pairs={{0,0},{1,2},{2,1},{3,3},{4,4},{5,6},{6,5},{7,7},{8,8},{9,10},{10,9... | collective-permute-start | bytes 24584 | tf_op jit(solution)/shard_map/ppermute | solution.py:500
  9.7 10.5 %copy-start.2 = (bf16[4,64,64]{2,1,0:T(8,128)(2,1)S(1)}, bf16[4,64,64]{2,1,0:T(8,128)(2,1)}, u32[]{:S(2)}) copy-start(bf16[4,64,64]{2,1,0:T(8,128)(2,1)} %point_ref.1) | copy-start | bytes 98308
  9.7 10.5 %copy-start.3 = (f32[4,3,64]{2,0,1:T(4,128)S(1)}, f32[4,3,64]{2,0,1:T(4,128)}, u32[]{:S(2)}) copy-start(f32[4,3,64]{2,0,1:T(4,128)} %param.10) | copy-start | bytes 9220
  11.6 5.6 %collective-permute-start.2 = (bf16[2,256,128]{2,1,0:T(8,128)(2,1)S(1)}, bf16[2,256,128]{2,1,0:T(8,128)(2,1)S(1)}, u32[]{:S(2)}, u32[]{:S(2)}) collective-permute-start(bf16[2,256,128]{2,1,0:T(8,128)(2,1)S(1)} %get-tuple-element.41), channel_id=1, source_target_pairs={{0,16},{4,12},{8,24},{12,4},{16,0},{20,28},{24,8},{28,20},{1,17},{... | collective-permute-start | bytes 393224 | tf_op jit(solution)/shard_map/ppermute | solution.py:488
  12.9 7.3 %collective-permute-start.3 = (bf16[2,256,128]{2,1,0:T(8,128)(2,1)S(1)}, bf16[2,256,128]{2,1,0:T(8,128)(2,1)S(1)}, u32[]{:S(2)}, u32[]{:S(2)}) collective-permute-start(bf16[2,256,128]{2,1,0:T(8,128)(2,1)S(1)} %get-tuple-element.42), channel_id=1, source_target_pairs={{0,8},{4,20},{8,0},{12,28},{16,24},{20,4},{24,16},{28,12},{1,9},{5... | collective-permute-start | bytes 393224 | tf_op jit(solution)/shard_map/ppermute | solution.py:488
  14.1 6.9 %collective-permute-start.4 = (bf16[2,256,128]{2,1,0:T(8,128)(2,1)S(1)}, bf16[2,256,128]{2,1,0:T(8,128)(2,1)S(1)}, u32[]{:S(2)}, u32[]{:S(2)}) collective-permute-start(bf16[2,256,128]{2,1,0:T(8,128)(2,1)S(1)} %get-tuple-element.43), channel_id=1, source_target_pairs={{0,20},{4,8},{8,28},{12,0},{16,4},{20,24},{24,12},{28,16},{1,21},{... | collective-permute-start | bytes 393224 | tf_op jit(solution)/shard_map/ppermute | solution.py:488
  16.1 6.2 %collective-permute-start.5 = (bf16[2,256,128]{2,1,0:T(8,128)(2,1)S(1)}, bf16[2,256,128]{2,1,0:T(8,128)(2,1)S(1)}, u32[]{:S(2)}, u32[]{:S(2)}) collective-permute-start(bf16[2,256,128]{2,1,0:T(8,128)(2,1)S(1)} %get-tuple-element.44), channel_id=1, source_target_pairs={{0,12},{4,16},{8,4},{12,24},{16,28},{20,0},{24,20},{28,8},{1,13},{... | collective-permute-start | bytes 393224 | tf_op jit(solution)/shard_map/ppermute | solution.py:488
  16.1 8.0 %collective-permute-start.6 = (bf16[2,256,128]{2,1,0:T(8,128)(2,1)S(1)}, bf16[2,256,128]{2,1,0:T(8,128)(2,1)S(1)}, u32[]{:S(2)}, u32[]{:S(2)}) collective-permute-start(bf16[2,256,128]{2,1,0:T(8,128)(2,1)S(1)} %get-tuple-element.45), channel_id=1, source_target_pairs={{0,24},{4,28},{8,16},{12,20},{16,8},{20,12},{24,0},{28,4},{1,25},{... | collective-permute-start | bytes 393224 | tf_op jit(solution)/shard_map/ppermute | solution.py:488
  17.2 9.8 %collective-permute-start.7 = (bf16[2,256,128]{2,1,0:T(8,128)(2,1)S(1)}, bf16[2,256,128]{2,1,0:T(8,128)(2,1)S(1)}, u32[]{:S(2)}, u32[]{:S(2)}) collective-permute-start(bf16[2,256,128]{2,1,0:T(8,128)(2,1)S(1)} %get-tuple-element.46), channel_id=1, source_target_pairs={{0,28},{4,24},{8,20},{12,16},{16,12},{20,8},{24,4},{28,0},{1,29},{... | collective-permute-start | bytes 393224 | tf_op jit(solution)/shard_map/ppermute | solution.py:488
  20.2 6.9 %collective-permute-start.8 = (bf16[2,256,128]{2,1,0:T(8,128)(2,1)S(1)}, bf16[2,256,128]{2,1,0:T(8,128)(2,1)S(1)}, u32[]{:S(2)}, u32[]{:S(2)}) collective-permute-start(bf16[2,256,128]{2,1,0:T(8,128)(2,1)S(1)} %get-tuple-element.47), channel_id=1, source_target_pairs={{0,4},{4,0},{8,12},{12,8},{16,20},{20,16},{24,28},{28,24},{1,5},{5... | collective-permute-start | bytes 393224 | tf_op jit(solution)/shard_map/ppermute | solution.py:488
  30.9 4.6 %collective-permute-start.10 = (bf16[2,256,128]{2,1,0:T(8,128)(2,1)S(1)}, bf16[2,256,128]{2,1,0:T(8,128)(2,1)S(1)}, u32[]{:S(2)}, u32[]{:S(2)}) collective-permute-start(bf16[2,256,128]{2,1,0:T(8,128)(2,1)S(1)} %get-tuple-element.53), channel_id=1, source_target_pairs={{0,16},{4,12},{8,24},{12,4},{16,0},{20,28},{24,8},{28,20},{1,17},{... | collective-permute-start | bytes 393224 | tf_op jit(solution)/shard_map/ppermute | solution.py:488
  32.1 6.0 %collective-permute-start.11 = (bf16[2,256,128]{2,1,0:T(8,128)(2,1)S(1)}, bf16[2,256,128]{2,1,0:T(8,128)(2,1)S(1)}, u32[]{:S(2)}, u32[]{:S(2)}) collective-permute-start(bf16[2,256,128]{2,1,0:T(8,128)(2,1)S(1)} %get-tuple-element.54), channel_id=1, source_target_pairs={{0,8},{4,20},{8,0},{12,28},{16,24},{20,4},{24,16},{28,12},{1,9},{5... | collective-permute-start | bytes 393224 | tf_op jit(solution)/shard_map/ppermute | solution.py:488
  33.4 7.6 %collective-permute-start.12 = (bf16[2,256,128]{2,1,0:T(8,128)(2,1)S(1)}, bf16[2,256,128]{2,1,0:T(8,128)(2,1)S(1)}, u32[]{:S(2)}, u32[]{:S(2)}) collective-permute-start(bf16[2,256,128]{2,1,0:T(8,128)(2,1)S(1)} %get-tuple-element.55), channel_id=1, source_target_pairs={{0,20},{4,8},{8,28},{12,0},{16,4},{20,24},{24,12},{28,16},{1,21},{... | collective-permute-start | bytes 393224 | tf_op jit(solution)/shard_map/ppermute | solution.py:488
  34.3 7.2 %collective-permute-start.13 = (bf16[2,256,128]{2,1,0:T(8,128)(2,1)S(1)}, bf16[2,256,128]{2,1,0:T(8,128)(2,1)S(1)}, u32[]{:S(2)}, u32[]{:S(2)}) collective-permute-start(bf16[2,256,128]{2,1,0:T(8,128)(2,1)S(1)} %get-tuple-element.56), channel_id=1, source_target_pairs={{0,12},{4,16},{8,4},{12,24},{16,28},{20,0},{24,20},{28,8},{1,13},{... | collective-permute-start | bytes 393224 | tf_op jit(solution)/shard_map/ppermute | solution.py:488
  35.1 6.8 %collective-permute-start.14 = (bf16[2,256,128]{2,1,0:T(8,128)(2,1)S(1)}, bf16[2,256,128]{2,1,0:T(8,128)(2,1)S(1)}, u32[]{:S(2)}, u32[]{:S(2)}) collective-permute-start(bf16[2,256,128]{2,1,0:T(8,128)(2,1)S(1)} %get-tuple-element.57), channel_id=1, source_target_pairs={{0,24},{4,28},{8,16},{12,20},{16,8},{20,12},{24,0},{28,4},{1,25},{... | collective-permute-start | bytes 393224 | tf_op jit(solution)/shard_map/ppermute | solution.py:488
  35.5 10.1 %collective-permute-start.15 = (bf16[2,256,128]{2,1,0:T(8,128)(2,1)S(1)}, bf16[2,256,128]{2,1,0:T(8,128)(2,1)S(1)}, u32[]{:S(2)}, u32[]{:S(2)}) collective-permute-start(bf16[2,256,128]{2,1,0:T(8,128)(2,1)S(1)} %get-tuple-element.58), channel_id=1, source_target_pairs={{0,28},{4,24},{8,20},{12,16},{16,12},{20,8},{24,4},{28,0},{1,29},{... | collective-permute-start | bytes 393224 | tf_op jit(solution)/shard_map/ppermute | solution.py:488
  38.1 7.4 %collective-permute-start.9 = (bf16[2,256,128]{2,1,0:T(8,128)(2,1)S(1)}, bf16[2,256,128]{2,1,0:T(8,128)(2,1)S(1)}, u32[]{:S(2)}, u32[]{:S(2)}) collective-permute-start(bf16[2,256,128]{2,1,0:T(8,128)(2,1)S(1)} %get-tuple-element.52), channel_id=1, source_target_pairs={{0,4},{4,0},{8,12},{12,8},{16,20},{20,16},{24,28},{28,24},{1,5},{5... | collective-permute-start | bytes 393224 | tf_op jit(solution)/shard_map/ppermute | solution.py:488

commit v5 on v4

--- a/solution.py
+++ b/solution.py
@@ -325,7 +325,7 @@
     for step, message_ref in zip(steps_of(sources), message_refs):
         for f in range(local):
             state[got_from(me, step) * local + f] = message_ref[f].astype(jnp.float32)
-    height = 32
+    height = 16
 
     def blend(layer, q):
         spacing = 2**layer

time: 47.4 us -> 47.4 us (level)
  no operation moved by 1% of the time
where the time goes in v5:
time: 47.4 us; the launch traced here: 47.2 us
  starting transfers between devices  21.3 us (45%)
  Pallas kernels  13.3 us (28%)
  waiting for transfers between devices  10.9 us (23%)
  local copies, waits for them, and re-layouts  0.9 us (2%)
  between operations  0.82 us (2%)
    ppermute x14, starting transfers between devices, exchange(): lax.ppermute(array, 'frame', [(i, i ^ step[i % 2]) for i in range(count)])  16.7 us
    ppermute x14, waiting for transfers between devices, exchange(): lax.ppermute(array, 'frame', [(i, i ^ step[i % 2]) for i in range(count)])  10.9 us
    ppermute x1, starting transfers between devices, on_device(): second = lax.ppermute(second, 'tile', swaps(tiles, 1))  4.48 us
    pallas_call x1, Pallas kernels, temporal(): pl.pallas_call(functools.partial(temporal_kernel, sources), in_specs=[vme...  3.82 us
    pallas_call x1, Pallas kernels, inner(): pl.pallas_call(inner_kernel, in_specs=[smem, smem, vmem, vmem], out_shape...  2.63 us
    pallas_call x1, Pallas kernels, finish(): pl.pallas_call(finish_kernel, in_specs=[vmem] * 7, out_shape=[jax.ShapeDt...  1.85 us
    pallas_call x1, Pallas kernels, place(): pl.pallas_call(functools.partial(place_kernel, sources), in_specs=[vmem,...  1.62 us
    pallas_call x1, Pallas kernels, plan(): pl.pallas_call(functools.partial(plan_kernel, sources), in_specs=[smem, s...  1.26 us
  transfers between devices with their start and end apart: 16, of which 7 were waited for; matrix products, arithmetic and copies ran while one was open for 0% of the time, Pallas kernels for 9%

profile of v5, /device:TPU:9, one launch (start us, length us, event | category | flops | bytes accessed | tf_op | source)
XLA Modules:
  0.0 47.2 jit_solution(11851143195252781562)
XLA Ops:
  0.0 0.9 %copy-done.1 = bf16[9,64,8]{1,2,0:T(8,128)(2,1)S(1)} copy-done((bf16[9,64,8]{1,2,0:T(8,128)(2,1)S(1)}, bf16[9,64,8]{1,2,0:T(8,128)(2,1)}, u32[]{:S(2)}) %copy-start.1) | copy-done | bytes 9240
  0.9 0.9 %bands.1.band_ref._ = bf16[8,256,768]{2,1,0:T(8,128)(2,1)S(1)} custom-call(bf16[9,8,64]{2,1,0:T(8,128)(2,1)S(1)} %bitcast.2), custom_call_target="tpu_custom_call" | custom-call | flops 268435456 | bytes 8388608 | tf_op jit(solution)/shard_map/bands/pallas_call | solution.py:110
  1.8 0.7 %edge_columns.1 = (bf16[16,256]{1,0:T(8,128)(2,1)S(1)}, bf16[16,256]{1,0:T(8,128)(2,1)S(1)}) custom-call(bf16[64,2,32,256]{3,2,1,0:T(8,128)(2,1)S(1)} %copy-done, bf16[8,256,768]{2,1,0:T(8,128)(2,1)S(1)} %bands.1.band_ref._), custom_call_target="tpu_custom_call" | custom-call | flops 268435456 | bytes 2097152 | tf_op jit(solution)/shard_map/edge_columns/pallas_call | solution.py:68
  2.6 4.5 %collective-permute-start.1 = (bf16[16,256]{1,0:T(8,128)(2,1)S(1)}, bf16[16,256]{1,0:T(8,128)(2,1)S(1)}, u32[]{:S(2)}, u32[]{:S(2)}) collective-permute-start(bf16[16,256]{1,0:T(8,128)(2,1)S(1)} %get-tuple-element.37), channel_id=1, source_target_pairs={{0,0},{1,2},{2,1},{3,3},{4,4},{5,6},{6,5},{7,7},{8,8},{9,10},{10,9... | collective-permute-start | bytes 24584 | tf_op jit(solution)/shard_map/ppermute | solution.py:500
  7.1 2.6 %inner.1 = (f32[8,2,256,256]{3,2,1,0:T(8,128)S(1)}, f32[8,2,256,256]{3,2,1,0:T(8,128)S(1)}, bf16[256,256]{1,0:T(8,128)(2,1)S(1)}, s32[256,128]{1,0:T(8,128)S(1)}) custom-call(s32[1,32]{1,0:T(1,128)S(1)} %copy-done.5, f32[64]{0:T(128)S(1)} %copy-done.4, bf16[64,2,32,256]{3,2,1,0:T(8,128)(2,1)S(1)} %copy-done, bf16[8,256,768]{2,1,0:T(8,128)(2,1)S(1)} %bands.1.band_ref._), custom_call_target="tpu_custom_call" | custom-call | flops 2147483648 | bytes 8388608 | tf_op jit(solution)/shard_map/inner/pallas_call | solution.py:170
  9.8 1.8 %finish.1 = (bf16[64,2,32,256]{3,2,1,0:T(8,128)(2,1)S(1)}, bf16[2,256,128]{2,1,0:T(8,128)(2,1)S(1)}, bf16[2,256,128]{2,1,0:T(8,128)(2,1)S(1)}, bf16[2,256,128]{2...) custom-call(bf16[8,256,768]{2,1,0:T(8,128)(2,1)S(1)} %bands.1.band_r, ...), custom_call_target="tpu_custom_call" | custom-call | flops 1073741824 | bytes 8388608 | tf_op jit(solution)/shard_map/finish/pallas_call | solution.py:270
  11.6 1.3 %collective-permute-start.2 = (bf16[2,256,128]{2,1,0:T(8,128)(2,1)S(1)}, bf16[2,256,128]{2,1,0:T(8,128)(2,1)S(1)}, u32[]{:S(2)}, u32[]{:S(2)}) collective-permute-start(bf16[2,256,128]{2,1,0:T(8,128)(2,1)S(1)} %get-tuple-element.41), channel_id=1, source_target_pairs={{0,16},{4,12},{8,24},{12,4},{16,0},{20,28},{24,8},{28,20},{1,17},{... | collective-permute-start | bytes 393224 | tf_op jit(solution)/shard_map/ppermute | solution.py:488
  12.9 1.2 %collective-permute-start.3 = (bf16[2,256,128]{2,1,0:T(8,128)(2,1)S(1)}, bf16[2,256,128]{2,1,0:T(8,128)(2,1)S(1)}, u32[]{:S(2)}, u32[]{:S(2)}) collective-permute-start(bf16[2,256,128]{2,1,0:T(8,128)(2,1)S(1)} %get-tuple-element.42), channel_id=1, source_target_pairs={{0,8},{4,20},{8,0},{12,28},{16,24},{20,4},{24,16},{28,12},{1,9},{5... | collective-permute-start | bytes 393224 | tf_op jit(solution)/shard_map/ppermute | solution.py:488
  14.1 1.9 %collective-permute-start.4 = (bf16[2,256,128]{2,1,0:T(8,128)(2,1)S(1)}, bf16[2,256,128]{2,1,0:T(8,128)(2,1)S(1)}, u32[]{:S(2)}, u32[]{:S(2)}) collective-permute-start(bf16[2,256,128]{2,1,0:T(8,128)(2,1)S(1)} %get-tuple-element.43), channel_id=1, source_target_pairs={{0,20},{4,8},{8,28},{12,0},{16,4},{20,24},{24,12},{28,16},{1,21},{... | collective-permute-start | bytes 393224 | tf_op jit(solution)/shard_map/ppermute | solution.py:488
  16.1 1.2 %collective-permute-start.6 = (bf16[2,256,128]{2,1,0:T(8,128)(2,1)S(1)}, bf16[2,256,128]{2,1,0:T(8,128)(2,1)S(1)}, u32[]{:S(2)}, u32[]{:S(2)}) collective-permute-start(bf16[2,256,128]{2,1,0:T(8,128)(2,1)S(1)} %get-tuple-element.45), channel_id=1, source_target_pairs={{0,24},{4,28},{8,16},{12,20},{16,8},{20,12},{24,0},{28,4},{1,25},{... | collective-permute-start | bytes 393224 | tf_op jit(solution)/shard_map/ppermute | solution.py:488
  17.2 3.0 %collective-permute-start.7 = (bf16[2,256,128]{2,1,0:T(8,128)(2,1)S(1)}, bf16[2,256,128]{2,1,0:T(8,128)(2,1)S(1)}, u32[]{:S(2)}, u32[]{:S(2)}) collective-permute-start(bf16[2,256,128]{2,1,0:T(8,128)(2,1)S(1)} %get-tuple-element.46), channel_id=1, source_target_pairs={{0,28},{4,24},{8,20},{12,16},{16,12},{20,8},{24,4},{28,0},{1,29},{... | collective-permute-start | bytes 393224 | tf_op jit(solution)/shard_map/ppermute | solution.py:488
  21.0 1.3 %collective-permute-done.5.refs_4_ = bf16[2,256,128]{2,1,0:T(8,128)(2,1)S(1)} collective-permute-done((bf16[2,256,128]{2,1,0:T(8,128)(2,1)S(1)}, bf16[2,256,128]{2,1,0:T(8,128)(2,1)S(1)}, u32[]{:S(2)}, u32[]{:S(2)}) %collective-permute-start.5) | collective-permute-done | bytes 131104 | tf_op jit(solution)/shard_map/ppermute | solution.py:488
  22.3 1.8 %collective-permute-done.6.refs_5_ = bf16[2,256,128]{2,1,0:T(8,128)(2,1)S(1)} collective-permute-done((bf16[2,256,128]{2,1,0:T(8,128)(2,1)S(1)}, bf16[2,256,128]{2,1,0:T(8,128)(2,1)S(1)}, u32[]{:S(2)}, u32[]{:S(2)}) %collective-permute-start.6) | collective-permute-done | bytes 131104 | tf_op jit(solution)/shard_map/ppermute | solution.py:488
  24.1 3.0 %collective-permute-done.7.refs_6_ = bf16[2,256,128]{2,1,0:T(8,128)(2,1)S(1)} collective-permute-done((bf16[2,256,128]{2,1,0:T(8,128)(2,1)S(1)}, bf16[2,256,128]{2,1,0:T(8,128)(2,1)S(1)}, u32[]{:S(2)}, u32[]{:S(2)}) %collective-permute-start.7) | collective-permute-done | bytes 131104 | tf_op jit(solution)/shard_map/ppermute | solution.py:488
  27.1 3.8 %temporal.1 = (bf16[2,256,128]{2,1,0:T(8,128)(2,1)S(1)}, bf16[2,256,128]{2,1,0:T(8,128)(2,1)S(1)}, bf16[2,256,128]{2,1,0:T(8,128)(2,1)S(1)}, bf16[2,256,128]{2,1...) custom-call(f32[12,256,128]{2,1,0:T(8,128)S(1)} %get-tuple-element.3, ...), custom_call_target="tpu_custom_call" | custom-call | flops 1073741824 | bytes 2097152 | tf_op jit(solution)/shard_map/temporal/pallas_call | solution.py:375
  30.9 1.2 %collective-permute-start.10 = (bf16[2,256,128]{2,1,0:T(8,128)(2,1)S(1)}, bf16[2,256,128]{2,1,0:T(8,128)(2,1)S(1)}, u32[]{:S(2)}, u32[]{:S(2)}) collective-permute-start(bf16[2,256,128]{2,1,0:T(8,128)(2,1)S(1)} %get-tuple-element.53), channel_id=1, source_target_pairs={{0,16},{4,12},{8,24},{12,4},{16,0},{20,28},{24,8},{28,20},{1,17},{... | collective-permute-start | bytes 393224 | tf_op jit(solution)/shard_map/ppermute | solution.py:488
  32.1 1.2 %collective-permute-start.11 = (bf16[2,256,128]{2,1,0:T(8,128)(2,1)S(1)}, bf16[2,256,128]{2,1,0:T(8,128)(2,1)S(1)}, u32[]{:S(2)}, u32[]{:S(2)}) collective-permute-start(bf16[2,256,128]{2,1,0:T(8,128)(2,1)S(1)} %get-tuple-element.54), channel_id=1, source_target_pairs={{0,8},{4,20},{8,0},{12,28},{16,24},{20,4},{24,16},{28,12},{1,9},{5... | collective-permute-start | bytes 393224 | tf_op jit(solution)/shard_map/ppermute | solution.py:488
  33.4 0.9 %collective-permute-start.12 = (bf16[2,256,128]{2,1,0:T(8,128)(2,1)S(1)}, bf16[2,256,128]{2,1,0:T(8,128)(2,1)S(1)}, u32[]{:S(2)}, u32[]{:S(2)}) collective-permute-start(bf16[2,256,128]{2,1,0:T(8,128)(2,1)S(1)} %get-tuple-element.55), channel_id=1, source_target_pairs={{0,20},{4,8},{8,28},{12,0},{16,4},{20,24},{24,12},{28,16},{1,21},{... | collective-permute-start | bytes 393224 | tf_op jit(solution)/shard_map/ppermute | solution.py:488
  34.3 0.8 %collective-permute-start.13 = (bf16[2,256,128]{2,1,0:T(8,128)(2,1)S(1)}, bf16[2,256,128]{2,1,0:T(8,128)(2,1)S(1)}, u32[]{:S(2)}, u32[]{:S(2)}) collective-permute-start(bf16[2,256,128]{2,1,0:T(8,128)(2,1)S(1)} %get-tuple-element.56), channel_id=1, source_target_pairs={{0,12},{4,16},{8,4},{12,24},{16,28},{20,0},{24,20},{28,8},{1,13},{... | collective-permute-start | bytes 393224 | tf_op jit(solution)/shard_map/ppermute | solution.py:488
  35.5 2.6 %collective-permute-start.15 = (bf16[2,256,128]{2,1,0:T(8,128)(2,1)S(1)}, bf16[2,256,128]{2,1,0:T(8,128)(2,1)S(1)}, u32[]{:S(2)}, u32[]{:S(2)}) collective-permute-start(bf16[2,256,128]{2,1,0:T(8,128)(2,1)S(1)} %get-tuple-element.58), channel_id=1, source_target_pairs={{0,28},{4,24},{8,20},{12,16},{16,12},{20,8},{24,4},{28,0},{1,29},{... | collective-permute-start | bytes 393224 | tf_op jit(solution)/shard_map/ppermute | solution.py:488
  38.1 0.9 %collective-permute-start.9 = (bf16[2,256,128]{2,1,0:T(8,128)(2,1)S(1)}, bf16[2,256,128]{2,1,0:T(8,128)(2,1)S(1)}, u32[]{:S(2)}, u32[]{:S(2)}) collective-permute-start(bf16[2,256,128]{2,1,0:T(8,128)(2,1)S(1)} %get-tuple-element.52), channel_id=1, source_target_pairs={{0,4},{4,0},{8,12},{12,8},{16,20},{20,16},{24,28},{28,24},{1,5},{5... | collective-permute-start | bytes 393224 | tf_op jit(solution)/shard_map/ppermute | solution.py:488
  39.7 1.3 %plan.1 = (bf16[2,256,256]{2,1,0:T(8,128)(2,1)S(1)}, f32[2,256,128]{2,1,0:T(8,128)S(1)}) custom-call(s32[1,32]{1,0:T(1,128)S(1)} %copy-done.5, s32[1]{0:T(128)S(6)} %copy.8.counts_ref, bf16[2,256,128]{2,1,0:T(8,128)(2,1)S(1)} %get-tuple-element.48._.refs_0_), custom_call_target="tpu_custom_call" | custom-call | flops 134217728 | bytes 4194304 | tf_op jit(solution)/shard_map/plan/pallas_call | solution.py:415
  41.9 3.7 %collective-permute-done.15.refs_7_ = bf16[2,256,128]{2,1,0:T(8,128)(2,1)S(1)} collective-permute-done((bf16[2,256,128]{2,1,0:T(8,128)(2,1)S(1)}, bf16[2,256,128]{2,1,0:T(8,128)(2,1)S(1)}, u32[]{:S(2)}, u32[]{:S(2)}) %collective-permute-start.15) | collective-permute-done | bytes 131104 | tf_op jit(solution)/shard_map/ppermute | solution.py:488
  45.6 1.6 %place.1 = bf16[64,2,32,256]{3,2,1,0:T(8,128)(2,1)} custom-call(bf16[2,256,256]{2,1,0:T(8,128)(2,1)S(1)} %get-tuple-element.49.put_ref, f32[2,256,128]{2,1,0:T(8,128)S(1)} %get-tuple-element.50.cover_ref, bf16[64,2,32,256]{3,2,1,0:T(8,128)(2,1)S(1)} %get-tuple-element.51.hidden_ref, bf16[2,256,128]{2,1,0:T(8,128)(2,1)S(1)} %get-tuple-element.48._.refs_0_, ...), custom_call_target="tpu_custom_call" | custom-call | flops 268435456 | bytes 4194304 | tf_op jit(solution)/shard_map/place/pallas_call | solution.py:470
  (28 shorter events, 2.2 us)
Async XLA Ops:
  0.0 1.8 %copy-start = (bf16[64,2,32,256]{3,2,1,0:T(8,128)(2,1)S(1)}, bf16[64,2,32,256]{3,2,1,0:T(8,128)(2,1)}, u32[]{:S(2)}) copy-start(bf16[64,2,32,256]{3,2,1,0:T(8,128)(2,1)} %grid_ref.3) | copy-start | bytes 6291460
  0.0 0.9 %copy-start.1 = (bf16[9,64,8]{1,2,0:T(8,128)(2,1)S(1)}, bf16[9,64,8]{1,2,0:T(8,128)(2,1)}, u32[]{:S(2)}) copy-start(bf16[9,64,8]{1,2,0:T(8,128)(2,1)} %param.8) | copy-start | bytes 27652
  1.8 5.2 %copy-start.4 = (f32[64]{0:T(128)S(1)}, f32[64]{0:T(128)}, u32[]{:S(2)}) copy-start(f32[64]{0:T(128)} %bias_ref.1) | copy-start | bytes 772
  1.8 5.2 %copy-start.5 = (s32[1,32]{1,0:T(1,128)S(1)}, s32[1,32]{1,0:T(1,128)}, u32[]{:S(2)}) copy-start(s32[1,32]{1,0:T(1,128)} %occupied_ref.3) | copy-start | bytes 388
  2.5 7.2 %collective-permute-start = (bf16[16,256]{1,0:T(8,128)(2,1)S(1)}, bf16[16,256]{1,0:T(8,128)(2,1)S(1)}, u32[]{:S(2)}, u32[]{:S(2)}) collective-permute-start(bf16[16,256]{1,0:T(8,128)(2,1)S(1)} %get-tuple-element.36), channel_id=1, source_target_pairs={{0,1},{1,0},{2,3},{3,2},{4,5},{5,4},{6,7},{7,6},{8,9},{9,8},{10,11... | collective-permute-start | bytes 24584 | tf_op jit(solution)/shard_map/ppermute | solution.py:499
  2.6 7.2 %collective-permute-start.1 = (bf16[16,256]{1,0:T(8,128)(2,1)S(1)}, bf16[16,256]{1,0:T(8,128)(2,1)S(1)}, u32[]{:S(2)}, u32[]{:S(2)}) collective-permute-start(bf16[16,256]{1,0:T(8,128)(2,1)S(1)} %get-tuple-element.37), channel_id=1, source_target_pairs={{0,0},{1,2},{2,1},{3,3},{4,4},{5,6},{6,5},{7,7},{8,8},{9,10},{10,9... | collective-permute-start | bytes 24584 | tf_op jit(solution)/shard_map/ppermute | solution.py:500
  9.7 10.5 %copy-start.2 = (bf16[4,64,64]{2,1,0:T(8,128)(2,1)S(1)}, bf16[4,64,64]{2,1,0:T(8,128)(2,1)}, u32[]{:S(2)}) copy-start(bf16[4,64,64]{2,1,0:T(8,128)(2,1)} %point_ref.1) | copy-start | bytes 98308
  9.7 10.5 %copy-start.3 = (f32[4,3,64]{2,0,1:T(4,128)S(1)}, f32[4,3,64]{2,0,1:T(4,128)}, u32[]{:S(2)}) copy-start(f32[4,3,64]{2,0,1:T(4,128)} %param.10) | copy-start | bytes 9220
  11.6 5.6 %collective-permute-start.2 = (bf16[2,256,128]{2,1,0:T(8,128)(2,1)S(1)}, bf16[2,256,128]{2,1,0:T(8,128)(2,1)S(1)}, u32[]{:S(2)}, u32[]{:S(2)}) collective-permute-start(bf16[2,256,128]{2,1,0:T(8,128)(2,1)S(1)} %get-tuple-element.41), channel_id=1, source_target_pairs={{0,16},{4,12},{8,24},{12,4},{16,0},{20,28},{24,8},{28,20},{1,17},{... | collective-permute-start | bytes 393224 | tf_op jit(solution)/shard_map/ppermute | solution.py:488
  12.9 7.3 %collective-permute-start.3 = (bf16[2,256,128]{2,1,0:T(8,128)(2,1)S(1)}, bf16[2,256,128]{2,1,0:T(8,128)(2,1)S(1)}, u32[]{:S(2)}, u32[]{:S(2)}) collective-permute-start(bf16[2,256,128]{2,1,0:T(8,128)(2,1)S(1)} %get-tuple-element.42), channel_id=1, source_target_pairs={{0,8},{4,20},{8,0},{12,28},{16,24},{20,4},{24,16},{28,12},{1,9},{5... | collective-permute-start | bytes 393224 | tf_op jit(solution)/shard_map/ppermute | solution.py:488
  14.1 6.9 %collective-permute-start.4 = (bf16[2,256,128]{2,1,0:T(8,128)(2,1)S(1)}, bf16[2,256,128]{2,1,0:T(8,128)(2,1)S(1)}, u32[]{:S(2)}, u32[]{:S(2)}) collective-permute-start(bf16[2,256,128]{2,1,0:T(8,128)(2,1)S(1)} %get-tuple-element.43), channel_id=1, source_target_pairs={{0,20},{4,8},{8,28},{12,0},{16,4},{20,24},{24,12},{28,16},{1,21},{... | collective-permute-start | bytes 393224 | tf_op jit(solution)/shard_map/ppermute | solution.py:488
  16.1 6.2 %collective-permute-start.5 = (bf16[2,256,128]{2,1,0:T(8,128)(2,1)S(1)}, bf16[2,256,128]{2,1,0:T(8,128)(2,1)S(1)}, u32[]{:S(2)}, u32[]{:S(2)}) collective-permute-start(bf16[2,256,128]{2,1,0:T(8,128)(2,1)S(1)} %get-tuple-element.44), channel_id=1, source_target_pairs={{0,12},{4,16},{8,4},{12,24},{16,28},{20,0},{24,20},{28,8},{1,13},{... | collective-permute-start | bytes 393224 | tf_op jit(solution)/shard_map/ppermute | solution.py:488
  16.1 8.0 %collective-permute-start.6 = (bf16[2,256,128]{2,1,0:T(8,128)(2,1)S(1)}, bf16[2,256,128]{2,1,0:T(8,128)(2,1)S(1)}, u32[]{:S(2)}, u32[]{:S(2)}) collective-permute-start(bf16[2,256,128]{2,1,0:T(8,128)(2,1)S(1)} %get-tuple-element.45), channel_id=1, source_target_pairs={{0,24},{4,28},{8,16},{12,20},{16,8},{20,12},{24,0},{28,4},{1,25},{... | collective-permute-start | bytes 393224 | tf_op jit(solution)/shard_map/ppermute | solution.py:488
  17.2 9.8 %collective-permute-start.7 = (bf16[2,256,128]{2,1,0:T(8,128)(2,1)S(1)}, bf16[2,256,128]{2,1,0:T(8,128)(2,1)S(1)}, u32[]{:S(2)}, u32[]{:S(2)}) collective-permute-start(bf16[2,256,128]{2,1,0:T(8,128)(2,1)S(1)} %get-tuple-element.46), channel_id=1, source_target_pairs={{0,28},{4,24},{8,20},{12,16},{16,12},{20,8},{24,4},{28,0},{1,29},{... | collective-permute-start | bytes 393224 | tf_op jit(solution)/shard_map/ppermute | solution.py:488
  20.2 6.9 %collective-permute-start.8 = (bf16[2,256,128]{2,1,0:T(8,128)(2,1)S(1)}, bf16[2,256,128]{2,1,0:T(8,128)(2,1)S(1)}, u32[]{:S(2)}, u32[]{:S(2)}) collective-permute-start(bf16[2,256,128]{2,1,0:T(8,128)(2,1)S(1)} %get-tuple-element.47), channel_id=1, source_target_pairs={{0,4},{4,0},{8,12},{12,8},{16,20},{20,16},{24,28},{28,24},{1,5},{5... | collective-permute-start | bytes 393224 | tf_op jit(solution)/shard_map/ppermute | solution.py:488
  30.9 4.6 %collective-permute-start.10 = (bf16[2,256,128]{2,1,0:T(8,128)(2,1)S(1)}, bf16[2,256,128]{2,1,0:T(8,128)(2,1)S(1)}, u32[]{:S(2)}, u32[]{:S(2)}) collective-permute-start(bf16[2,256,128]{2,1,0:T(8,128)(2,1)S(1)} %get-tuple-element.53), channel_id=1, source_target_pairs={{0,16},{4,12},{8,24},{12,4},{16,0},{20,28},{24,8},{28,20},{1,17},{... | collective-permute-start | bytes 393224 | tf_op jit(solution)/shard_map/ppermute | solution.py:488
  32.1 6.0 %collective-permute-start.11 = (bf16[2,256,128]{2,1,0:T(8,128)(2,1)S(1)}, bf16[2,256,128]{2,1,0:T(8,128)(2,1)S(1)}, u32[]{:S(2)}, u32[]{:S(2)}) collective-permute-start(bf16[2,256,128]{2,1,0:T(8,128)(2,1)S(1)} %get-tuple-element.54), channel_id=1, source_target_pairs={{0,8},{4,20},{8,0},{12,28},{16,24},{20,4},{24,16},{28,12},{1,9},{5... | collective-permute-start | bytes 393224 | tf_op jit(solution)/shard_map/ppermute | solution.py:488
  33.4 7.6 %collective-permute-start.12 = (bf16[2,256,128]{2,1,0:T(8,128)(2,1)S(1)}, bf16[2,256,128]{2,1,0:T(8,128)(2,1)S(1)}, u32[]{:S(2)}, u32[]{:S(2)}) collective-permute-start(bf16[2,256,128]{2,1,0:T(8,128)(2,1)S(1)} %get-tuple-element.55), channel_id=1, source_target_pairs={{0,20},{4,8},{8,28},{12,0},{16,4},{20,24},{24,12},{28,16},{1,21},{... | collective-permute-start | bytes 393224 | tf_op jit(solution)/shard_map/ppermute | solution.py:488
  34.3 7.2 %collective-permute-start.13 = (bf16[2,256,128]{2,1,0:T(8,128)(2,1)S(1)}, bf16[2,256,128]{2,1,0:T(8,128)(2,1)S(1)}, u32[]{:S(2)}, u32[]{:S(2)}) collective-permute-start(bf16[2,256,128]{2,1,0:T(8,128)(2,1)S(1)} %get-tuple-element.56), channel_id=1, source_target_pairs={{0,12},{4,16},{8,4},{12,24},{16,28},{20,0},{24,20},{28,8},{1,13},{... | collective-permute-start | bytes 393224 | tf_op jit(solution)/shard_map/ppermute | solution.py:488
  35.1 6.8 %collective-permute-start.14 = (bf16[2,256,128]{2,1,0:T(8,128)(2,1)S(1)}, bf16[2,256,128]{2,1,0:T(8,128)(2,1)S(1)}, u32[]{:S(2)}, u32[]{:S(2)}) collective-permute-start(bf16[2,256,128]{2,1,0:T(8,128)(2,1)S(1)} %get-tuple-element.57), channel_id=1, source_target_pairs={{0,24},{4,28},{8,16},{12,20},{16,8},{20,12},{24,0},{28,4},{1,25},{... | collective-permute-start | bytes 393224 | tf_op jit(solution)/shard_map/ppermute | solution.py:488
  35.5 10.1 %collective-permute-start.15 = (bf16[2,256,128]{2,1,0:T(8,128)(2,1)S(1)}, bf16[2,256,128]{2,1,0:T(8,128)(2,1)S(1)}, u32[]{:S(2)}, u32[]{:S(2)}) collective-permute-start(bf16[2,256,128]{2,1,0:T(8,128)(2,1)S(1)} %get-tuple-element.58), channel_id=1, source_target_pairs={{0,28},{4,24},{8,20},{12,16},{16,12},{20,8},{24,4},{28,0},{1,29},{... | collective-permute-start | bytes 393224 | tf_op jit(solution)/shard_map/ppermute | solution.py:488
  38.1 7.4 %collective-permute-start.9 = (bf16[2,256,128]{2,1,0:T(8,128)(2,1)S(1)}, bf16[2,256,128]{2,1,0:T(8,128)(2,1)S(1)}, u32[]{:S(2)}, u32[]{:S(2)}) collective-permute-start(bf16[2,256,128]{2,1,0:T(8,128)(2,1)S(1)} %get-tuple-element.52), channel_id=1, source_target_pairs={{0,4},{4,0},{8,12},{12,8},{16,20},{20,16},{24,28},{28,24},{1,5},{5... | collective-permute-start | bytes 393224 | tf_op jit(solution)/shard_map/ppermute | solution.py:488
